TPU v7x, 256 devices: a whole 4x4x8 slice. The times are simulated.
256 devices in a mesh: slab: 2 (over z_hi), row: 8 (over x, core), col: 16 (over y, z_lo).
Axes of the slice: x: 4, y: 4, z: 8 (z_hi: 2, z_lo: 4; z = z_hi * 4 + z_lo), core: 2. Of those that a mesh axis runs over, the one named last changes fastest.
Arguments:
- pair_act: bfloat16 [512, 512, 128], P('row', 'col'), may hold values from -6 to 6
- out_grad: bfloat16 [512, 512, 128], P('row', 'col'), may hold values from -6 to 6
- pair_mask: int32 [512, 512], P('row', 'col'), may hold values 0 or 1
- chain_starts: int32 [6], replicated, may hold values from 0 to 511, as said below
- in_gain: float32 [128], replicated, may hold values from 0.25 to 1.75
- in_bias: float32 [128], replicated, may hold values from -3 to 3
- w_proj: bfloat16 [128, 512], replicated, may hold values from -0.5 to 0.5
- w_gate: bfloat16 [128, 128], replicated, may hold values from -0.5 to 0.5
- w_out: bfloat16 [128, 128], replicated, may hold values from -0.5 to 0.5
- mid_gain: float32 [128], replicated, may hold values from 0.25 to 1.75
- mid_bias: float32 [128], replicated, may hold values from -3 to 3
Outputs:
- pair_grad: bfloat16 [512, 16, 2, 16, 128], P('row', 'col', 'slab')
Inputs may be any that keep to these rules, and one draw needn't show every extreme that they name: `chain_starts`: rising, distinct, the first entry 0 and the last entry 511.
All inputs are finite; a program needn't handle non-finite values. No bound on the sum of `pair_mask` on one device may be relied on, other than what follows from the above.
Results may differ from a plain program's by a relative error of at most 0.022.
Values may be sent and summed in bfloat16 or wider, within the bound.
No kernel may reach another device: no remote copies, remote signals or barrier semaphores. Data moves between devices by JAX's collectives and lax.ppermute only.
A program may use at most 128 MiB of HBM per device.

v0:
```python
import jax
import jax.numpy as jnp
from jax import lax
from jax.sharding import PartitionSpec as P


def spread(x, axis, root):
    mine = lax.axis_index(axis) == root
    return lax.psum(jnp.where(mine, x, jnp.zeros_like(x)), axis)


def normalize(values):
    average = jnp.mean(values, axis=-1, keepdims=True)
    centred = values - average
    inv_std = lax.rsqrt(jnp.mean(centred * centred, axis=-1, keepdims=True) + 1e-05)
    return (centred * inv_std, inv_std)


def norm_backward(grad_normed, normed, inv_std):
    first = jnp.mean(grad_normed, axis=-1, keepdims=True)
    second = jnp.mean(grad_normed * normed, axis=-1, keepdims=True)
    return (grad_normed - first - normed * second) * inv_std


def chain_keep(pair_mask, chain_starts, row_ids, col_ids):
    row_chain = jnp.sum((row_ids[:, None] >= chain_starts[None, :]).astype(jnp.int32), axis=1)
    col_chain = jnp.sum((col_ids[:, None] >= chain_starts[None, :]).astype(jnp.int32), axis=1)
    same_chain = row_chain[:, None] == col_chain[None, :]
    return jnp.where(same_chain | (pair_mask > 0), 1.0, 0.0).astype(jnp.float32)


def gated_pair(projected, keep_mask):
    left_gate, left_val, right_gate, right_val = jnp.split(projected, 4, axis=-1)
    keep_wide = keep_mask[..., None]
    left = (keep_wide * jax.nn.sigmoid(left_gate) * left_val).astype(jnp.bfloat16)
    right = (keep_wide * jax.nn.sigmoid(right_gate) * right_val).astype(jnp.bfloat16)
    return (left, right)


def gating_backward(left_grad, right_grad, projected, keep_mask):
    left_gate, left_val, right_gate, right_val = jnp.split(projected, 4, axis=-1)
    sig_left = jax.nn.sigmoid(left_gate)
    sig_right = jax.nn.sigmoid(right_gate)
    keep_wide = keep_mask[..., None]
    parts = [
        left_grad * keep_wide * left_val * sig_left * (1.0 - sig_left),
        left_grad * keep_wide * sig_left,
        right_grad * keep_wide * right_val * sig_right * (1.0 - sig_right),
        right_grad * keep_wide * sig_right,
    ]
    return jnp.concatenate(parts, axis=-1).astype(jnp.bfloat16)


def mid_backward(triangle, grad_tile, x_tile, mid_gain, mid_bias, w_gate, w_out):
    tri_hat, tri_inv = normalize(triangle)
    mid_out = (tri_hat * mid_gain + mid_bias).astype(jnp.bfloat16)
    gate = jax.nn.sigmoid(
        jnp.einsum("ijp,pq->ijq", x_tile, w_gate, preferred_element_type=jnp.float32)
    )
    proj_out = jnp.einsum("ijh,hp->ijp", mid_out, w_out, preferred_element_type=jnp.float32)
    grad_in = grad_tile.astype(jnp.float32)
    gate_grad = (grad_in * proj_out * gate * (1.0 - gate)).astype(jnp.bfloat16)
    mid_in_grad = (grad_in * gate).astype(jnp.bfloat16)
    grad_hat = (
        jnp.einsum("ijp,hp->ijh", mid_in_grad, w_out, preferred_element_type=jnp.float32) * mid_gain
    )
    tri_grad = norm_backward(grad_hat, tri_hat, tri_inv).astype(jnp.bfloat16)
    return (tri_grad, gate_grad)


def on_device(
    pair_act,
    out_grad,
    pair_mask,
    chain_starts,
    in_gain,
    in_bias,
    w_proj,
    w_gate,
    w_out,
    mid_gain,
    mid_bias,
):
    slab_count = lax.axis_size("slab")
    row_count = lax.axis_size("row")
    col_count = lax.axis_size("col")
    slab_at = lax.axis_index("slab")
    row_at = lax.axis_index("row")
    col_at = lax.axis_index("col")
    tile_rows, tile_cols, pair_width = pair_act.shape
    hidden = w_out.shape[0]
    half_cols = tile_cols // slab_count
    col_ratio = col_count // row_count
    root_row = col_at // col_ratio
    row_slot = col_at % col_ratio
    own_start = slab_at * half_cols
    normed, inv_std = normalize(pair_act.astype(jnp.float32))
    x_full = (normed * in_gain + in_bias).astype(jnp.bfloat16)
    x_half = lax.dynamic_slice_in_dim(x_full, own_start, half_cols, 1)
    normed_half = lax.dynamic_slice_in_dim(normed, own_start, half_cols, 1)
    inv_half = lax.dynamic_slice_in_dim(inv_std, own_start, half_cols, 1)
    mask_half = lax.dynamic_slice_in_dim(pair_mask, own_start, half_cols, 1)
    row_ids = row_at * tile_rows + jnp.arange(tile_rows, dtype=jnp.int32)
    col_ids = col_at * tile_cols + own_start + jnp.arange(half_cols, dtype=jnp.int32)
    keep_mask = chain_keep(mask_half, chain_starts, row_ids, col_ids)
    projected = jnp.einsum("ikp,pq->ikq", x_half, w_proj, preferred_element_type=jnp.float32)
    left_half, right_half = gated_pair(projected, keep_mask)
    left_rows, right_rows = (
        lax.all_gather(left_half, "col", axis=1, tiled=True),
        lax.all_gather(right_half, "col", axis=1, tiled=True),
    )
    row_piece = lax.dynamic_slice_in_dim(right_rows, row_slot * tile_cols, tile_cols, 0)
    right_cols = spread(row_piece, "row", root_row)
    tri_part = jnp.einsum("ikc,jkc->ijc", left_rows, right_cols, preferred_element_type=jnp.float32)
    triangle = lax.psum(tri_part.astype(jnp.bfloat16), "slab").astype(jnp.float32)
    tri_grad, gate_full = mid_backward(
        triangle, out_grad, x_full, mid_gain, mid_bias, w_gate, w_out
    )
    gate_grad = lax.dynamic_slice_in_dim(gate_full, own_start, half_cols, 1)
    right_part = jnp.einsum("ijc,ikc->kjc", tri_grad, left_rows, preferred_element_type=jnp.float32)
    right_total = lax.psum(right_part.astype(jnp.bfloat16), "row").astype(jnp.float32)
    blank = jnp.zeros((right_total.shape[0], tile_rows, hidden), jnp.float32)
    placed = lax.dynamic_update_slice_in_dim(blank, right_total, row_slot * tile_cols, 1)
    embedded = jnp.where(row_at == root_row, placed, 0.0)
    right_grad = jnp.transpose(
        lax.psum_scatter(
            embedded.astype(jnp.bfloat16), "col", scatter_dimension=0, tiled=True
        ).astype(jnp.float32),
        (1, 0, 2),
    )
    left_grad = jnp.transpose(
        lax.psum_scatter(
            jnp.einsum(
                "ijc,jkc->kic", tri_grad, right_cols, preferred_element_type=jnp.float32
            ).astype(jnp.bfloat16),
            "col",
            scatter_dimension=0,
            tiled=True,
        ).astype(jnp.float32),
        (1, 0, 2),
    )
    proj_grad = gating_backward(left_grad, right_grad, projected, keep_mask)
    x_grad = jnp.einsum("ikq,pq->ikp", proj_grad, w_proj, preferred_element_type=jnp.float32)
    x_grad = x_grad + jnp.einsum(
        "ikq,pq->ikp", gate_grad, w_gate, preferred_element_type=jnp.float32
    )
    result = norm_backward(x_grad * in_gain, normed_half, inv_half).astype(jnp.bfloat16)
    return result.reshape(tile_rows, 1, 1, half_cols, pair_width)


def solution(mesh):
    in_specs = (
        P("row", "col", None),
        P("row", "col", None),
        P("row", "col"),
        P(),
        P(),
        P(),
        P(),
        P(),
        P(),
        P(),
        P(),
    )
    out_specs = P("row", "col", "slab", None, None)
    return jax.shard_map(
        on_device, mesh=mesh, in_specs=in_specs, out_specs=out_specs, check_vma=False
    )
```

profile of v0, /device:TPU:2, one launch (start us, length us, event | category | flops | bytes accessed | tf_op | source)
XLA Modules:
  0.0 700.1 jit_solution(15589311823496740882)
XLA Ops:
  8.9 1.4 convert_reduce_fusion.1
  10.3 1.7 fusion.18
  12.0 2.5 add_convert_fusion
  14.9 1.4 copy-done.1
  16.3 1.1 multiply_convert_fusion.3
  18.2 115.9 %all-gather.3.cloned.1.call-done = bf16[64,256,128]{2,1,0:T(8,128)(2,1)} async-done(((bf16[64,16,128]{2,1,0:T(8,128)(2,1)}), bf16[64,256,128]{2,1,0:T(8,128)(2,1)}) %all-gather.3.cloned.1.call-update) | async-done | bytes 4194320 | tf_op jit(solution)/shard_map/all_gather | solution.py:110
  134.2 3.1 dynamic-slice_select_fusion
  137.3 112.1 %all-gather.5.cloned.1.call-done = bf16[64,256,128]{2,1,0:T(8,128)(2,1)} async-done(((bf16[64,16,128]{2,1,0:T(8,128)(2,1)}), bf16[64,256,128]{2,1,0:T(8,128)(2,1)}) %all-gather.5.cloned.1.call-update) | async-done | bytes 4194320 | tf_op jit(solution)/shard_map/all_gather | solution.py:109
  249.4 15.6 %copy.25 = bf16[64,256,128]{0,1,2:T(8,128)(2,1)} copy(bf16[64,256,128]{2,1,0:T(8,128)(2,1)} %all-gather.5.cloned.1.call-done) | data formatting | bytes 8388608 | tf_op jit(solution)/shard_map/all_gather | solution.py:109
  265.0 55.0 %all-reduce.4.cloned.1.call-done = bf16[32,256,128]{2,1,0:T(8,128)(2,1)} async-done(((bf16[32,256,128]{2,1,0:T(8,128)(2,1)}), bf16[32,256,128]{2,1,0:T(8,128)(2,1)}) %all-reduce.4.cloned.1.call-update) | async-done | bytes 2097168 | tf_op jit(solution)/shard_map/psum | solution.py:9
  320.0 3.4 copy.27
  323.4 5.8 fusion.74
  329.2 3.6 copy.26
  333.1 1.4 fusion.2
  334.5 55.8 %all-reduce.6.cloned.1.call-done = bf16[64,32,128]{2,1,0:T(8,128)(2,1)} async-done(((bf16[64,32,128]{2,1,0:T(8,128)(2,1)}), bf16[64,32,128]{2,1,0:T(8,128)(2,1)}) %all-reduce.6.cloned.1.call-update) | async-done | bytes 524304 | tf_op jit(solution)/shard_map/psum | solution.py:115
  390.3 1.4 convert_reduce_fusion
  391.7 1.7 fusion.17
  393.5 2.6 fusion.72
  396.1 1.2 fusion.14
  397.3 2.6 copy.28
  399.9 8.0 %fusion.76 = bf16[128,256,32]{1,2,0:T(8,128)(2,1)} fusion(bf16[64,256,128]{0,1,2:T(8,128)(2,1)} %copy.25, bf16[64,32,128]{0,1,2:T(8,128)(2,1)} %copy.28), kind=kOutput, calls=%fused_computation.111 | convolution fusion | flops 134217728 | bytes 6815744 | tf_op jit(solution)/shard_map/ijc,ikc->kjc/dot_general | solution.py:120
  407.9 4.6 copy.32
  412.6 4.5 fusion.75
  417.1 6.9 copy.29
  424.1 53.2 %all-reduce.8.cloned.1.call-done = bf16[256,32,128]{2,0,1:T(8,128)(2,1)} async-done(((bf16[256,32,128]{2,0,1:T(8,128)(2,1)}), bf16[256,32,128]{2,0,1:T(8,128)(2,1)}) %all-reduce.8.cloned.1.call-update) | async-done | bytes 2097168 | tf_op jit(solution)/shard_map/psum | solution.py:121
  477.2 3.0 broadcast_in_dim.16
  480.2 1.9 select_dynamic-update-slice_fusion
  484.6 100.8 %reduce-scatter.3.cloned.1.call-done = bf16[16,64,128]{2,0,1:T(8,128)(2,1)} async-done(((bf16[256,64,128]{2,0,1:T(8,128)(2,1)}), bf16[16,64,128]{2,0,1:T(8,128)(2,1)}) %reduce-scatter.3.cloned.1.call-update) | async-done | bytes 262160 | tf_op jit(solution)/shard_map/reduce_scatter | solution.py:132
  585.5 103.4 %reduce-scatter.5.cloned.1.call-done = bf16[16,64,128]{2,0,1:T(8,128)(2,1)} async-done(((bf16[256,64,128]{2,0,1:T(8,128)(2,1)}), bf16[16,64,128]{2,0,1:T(8,128)(2,1)}) %reduce-scatter.5.cloned.1.call-update) | async-done | bytes 262160 | tf_op jit(solution)/shard_map/reduce_scatter | solution.py:126
  688.8 1.5 fusion.47
  690.4 1.7 fusion.73
  692.1 1.2 fusion.53
  (59 shorter events, 6.6 us)
Async XLA Ops:
  6.5 8.0 %copy-start = (bf16[128,512]{1,0:T(8,128)(2,1)S(1)}, bf16[128,512]{1,0:T(8,128)(2,1)}, u32[]{:S(2)}) copy-start(bf16[128,512]{1,0:T(8,128)(2,1)} %param.17) | copy-start | bytes 393220
  6.5 127.6 %all-gather.3.cloned.1.call-start = ((), (), s32[]{:S(2)}) async-start(), calls=%async_computation.2 | async-start | bytes 4456448 | tf_op jit(solution)/shard_map/all_gather | solution.py:110
  14.9 1.4 copy-start.1
  17.4 232.0 %all-gather.5.cloned.1.call-start = ((), (), s32[]{:S(2)}) async-start(), calls=%async_computation.4 | async-start | bytes 4456448 | tf_op jit(solution)/shard_map/all_gather | solution.py:109
  18.1 301.8 %all-reduce.4.cloned.1.call-start = ((), (), s32[]{:S(2)}) async-start(), calls=%async_computation.3 | async-start | bytes 4194304 | tf_op jit(solution)/shard_map/psum | solution.py:9
  137.2 253.0 %all-reduce.6.cloned.1.call-start = ((), (), s32[]{:S(2)}) async-start(), calls=%async_computation.5 | async-start | bytes 1048576 | tf_op jit(solution)/shard_map/psum | solution.py:115
  329.2 3.9 copy-start.10
  332.8 60.6 %copy-start.7 = (bf16[64,32,128]{2,1,0:T(8,128)(2,1)S(1)}, bf16[64,32,128]{2,1,0:T(8,128)(2,1)}, u32[]{:S(2)}) copy-start(bf16[64,32,128]{2,1,0:T(8,128)(2,1)} %param.12) | copy-start | bytes 1572868
  332.8 60.6 %copy-start.9 = (bf16[128,128]{1,0:T(8,128)(2,1)S(1)}, bf16[128,128]{1,0:T(8,128)(2,1)}, u32[]{:S(2)}) copy-start(bf16[128,128]{1,0:T(8,128)(2,1)} %param.19) | copy-start | bytes 98308
  332.8 60.6 %copy-start.11 = (f32[128]{0:T(128)S(1)}, f32[128]{0:T(128)}, u32[]{:S(2)}) copy-start(f32[128]{0:T(128)} %param.20) | copy-start | bytes 1540
  332.8 144.4 %all-reduce.8.cloned.1.call-start = ((), (), s32[]{:S(2)}) async-start(), calls=%async_computation.7 | async-start | bytes 4194304 | tf_op jit(solution)/shard_map/psum | solution.py:121
  391.7 4.4 copy-start.3
  412.5 172.9 %reduce-scatter.3.cloned.1.call-start = ((), (), s32[]{:S(2)}) async-start(), calls=%async_computation.6 | async-start | bytes 4456448 | tf_op jit(solution)/shard_map/reduce_scatter | solution.py:132
  424.0 264.8 %reduce-scatter.5.cloned.1.call-start = ((), (), s32[]{:S(2)}) async-start(), calls=%async_computation.8 | async-start | bytes 4456448 | tf_op jit(solution)/shard_map/reduce_scatter | solution.py:126
  477.2 3.0 copy-start.6
  482.1 1.0 copy-start.8
  482.1 1.3 copy-start.12
  483.1 1.2 copy-start.4
  483.3 205.6 %copy-start.2 = (f32[64,16,512]{2,1,0:T(8,128)S(1)}, f32[64,16,512]{2,1,0:T(8,128)}, u32[]{:S(2)}) copy-start(f32[64,16,512]{2,1,0:T(8,128)} %copy-done.1) | copy-start | bytes 6291460
  484.6 205.8 %copy-start.13 = (f32[128]{0:T(128)S(1)}, f32[128]{0:T(128)}, u32[]{:S(2)}) copy-start(f32[128]{0:T(128)} %param.15) | copy-start | bytes 1540
  690.4 1.7 copy-start.5
Sparse Core Ops, SparseCore 0:
  17.5 116.5 all-gather.2
  135.9 113.4 all-gather.4
  251.7 68.2 all-reduce.3
  332.9 57.3 all-reduce.5
  412.6 64.5 all-reduce.7
  479.8 105.6 reduce-scatter.2
  588.2 100.6 reduce-scatter.4
where the time goes:
time: 701 us; the launch traced here: 700 us
  waiting for transfers between devices  597 us (85%)
  local copies, waits for them, and re-layouts  42.5 us (6%)
  matrix products  25.3 us (4%)
  other arithmetic  21.1 us (3%)
  between operations  13.8 us (2%)
    all_gather x1, waiting for transfers between devices, on_device(): lax.all_gather(right_half, 'col', axis=1, tiled=True)  116 us
    all_gather x1, waiting for transfers between devices, on_device(): lax.all_gather(left_half, 'col', axis=1, tiled=True)  112 us
    reduce_scatter x1, waiting for transfers between devices, on_device(): lax.psum_scatter(embedded.astype(jnp.bfloat16), 'col', scatter_dimension=...  103 us
    reduce_scatter x1, waiting for transfers between devices, on_device(): lax.psum_scatter(jnp.einsum('ijc,jkc->kic', tri_grad, right_cols, preferr...  101 us
    psum x1, waiting for transfers between devices, on_device(): lax.psum(tri_part.astype(jnp.bfloat16), 'slab').astype(jnp.float32)  55.8 us
    psum x1, waiting for transfers between devices, spread(): return lax.psum(jnp.where(mine, x, jnp.zeros_like(x)), axis)  55 us
    psum x1, waiting for transfers between devices, on_device(): lax.psum(right_part.astype(jnp.bfloat16), 'row').astype(jnp.float32)  53.2 us
    all_gather x1, local copies, waits for them, and re-layouts, on_device(): lax.all_gather(left_half, 'col', axis=1, tiled=True)  15.6 us
  transfers between devices with their start and end apart: 7, of which 7 were waited for; matrix products, arithmetic and copies ran while one was open for 5% of the time, Pallas kernels for 0%

commit v1 on v0

v1 whole, which is shorter than its diff:
```python
import jax
import jax.numpy as jnp
from jax import lax
from jax.experimental import pallas as pl
from jax.experimental.pallas import tpu as pltpu
from jax.sharding import PartitionSpec as P

BF16 = jnp.bfloat16
F32 = jnp.float32
LANES = 128
ROWS = 64
HALF = 16
LOW = 8
CHANNELS = 128
POINTS = ROWS * HALF
PEERS = ("row", "col")
EVERYONE = ("row", "col", "slab")


def dot(a, b, ca, cb):
    return lax.dot_general(a, b, (((ca,), (cb,)), ((), ())), preferred_element_type=F32)


def place(k):
    return ((k % LOW) * (HALF // LOW) + k // LOW) * ROWS


def normalize(values):
    average = jnp.mean(values, axis=-1, keepdims=True)
    centred = values - average
    inv_std = lax.rsqrt(jnp.mean(centred * centred, axis=-1, keepdims=True) + 1e-05)
    return centred * inv_std, inv_std


def low_lanes(shape):
    return lax.broadcasted_iota(jnp.int32, shape, 1) < ROWS


def mix(a, b):
    low = low_lanes(a.shape)
    first = jnp.where(low, a, pltpu.roll(b, ROWS, 1))
    second = jnp.where(low, pltpu.roll(a, ROWS, 1), b)
    return first, second


def load_half(ref, slab_at, scratch):
    start = pl.multiple_of(slab_at * HALF, HALF)
    scratch[...] = ref[:, pl.ds(start, HALF), :].astype(F32).reshape(POINTS, LANES)


def column(scratch, k):
    return scratch[pl.ds(k, ROWS, stride=HALF), :]


def keep_rows(mask_ref, starts_ref, mask_t, slab_at, row_at, col_at):
    mask = mask_ref[...].astype(F32)
    twice = jnp.concatenate([mask, mask], axis=0)
    wide = jnp.concatenate([twice, jnp.zeros((LANES, LANES - mask.shape[1]), F32)], axis=1)
    mask_t[...] = wide.T
    start = pl.multiple_of(slab_at * HALF, HALF)
    own = mask_t[pl.ds(start, HALF), :]
    shape = (HALF, LANES)
    lane = lax.broadcasted_iota(jnp.int32, shape, 1)
    row_ids = row_at * ROWS + jnp.where(lane < ROWS, lane, lane - ROWS)
    col_ids = (col_at * 2 + slab_at) * HALF + lax.broadcasted_iota(jnp.int32, shape, 0)
    row_chain = jnp.zeros(shape, jnp.int32)
    col_chain = jnp.zeros(shape, jnp.int32)
    for at in range(starts_ref.shape[0]):
        start_at = starts_ref[at]
        row_chain = row_chain + (row_ids >= start_at).astype(jnp.int32)
        col_chain = col_chain + (col_ids >= start_at).astype(jnp.int32)
    return jnp.where((row_chain == col_chain) | (own > 0.0), 1.0, 0.0)


def edges_kernel(
    starts_ref, act_ref, mask_ref, gain_ref, bias_ref, w_ref, edges_ref, x_ref, keep_ref, tile, mask_t, projected, turned
):
    slab_at = lax.axis_index("slab")
    load_half(act_ref, slab_at, tile)
    keep_ref[...] = keep_rows(
        mask_ref, starts_ref, mask_t, slab_at, lax.axis_index("row"), lax.axis_index("col")
    )
    for k in range(HALF):
        normed, _ = normalize(column(tile, k))
        x_ref[pl.ds(place(k), ROWS), :] = (normed * gain_ref[...] + bias_ref[...]).astype(BF16)
    projected[...] = dot(x_ref[...], w_ref[...], 1, 0)
    for k in range(HALF):
        here = pl.ds(place(k), ROWS)
        left = jax.nn.sigmoid(projected[here, 0:128]) * projected[here, 128:256]
        right = jax.nn.sigmoid(projected[here, 256:384]) * projected[here, 384:512]
        both = jnp.concatenate([left, right], axis=0).T
        turned[pl.ds(k, CHANNELS, stride=HALF), :] = both * keep_ref[k : k + 1, :]
    edges_ref[...] = turned[...].astype(BF16)


def triangle_kernel(edges_ref, out_ref, left_ref, right_ref):
    depth = edges_ref.shape[0] // 8
    for m in range(4):
        a = edges_ref[pl.ds(2 * m * depth, depth), :].astype(F32)
        b = edges_ref[pl.ds((2 * m + 1) * depth, depth), :].astype(F32)
        left, right = mix(a, b)
        left_ref[:, m * LANES : (m + 1) * LANES] = left.astype(BF16)
        right_ref[:, m * LANES : (m + 1) * LANES] = right.astype(BF16)
    for m in range(4):
        tri = dot(right_ref[...], left_ref[:, m * LANES : (m + 1) * LANES], 0, 0)
        tri = tri.reshape(32, HALF, LANES)
        a = tri[:, 0:LOW, :].reshape(depth, LANES)
        b = tri[:, LOW:HALF, :].reshape(depth, LANES)
        first, second = mix(a, b)
        out_ref[pl.ds(2 * m * depth, depth), :] = first.astype(BF16)
        out_ref[pl.ds((2 * m + 1) * depth, depth), :] = second.astype(BF16)


def middle_kernel(
    tri_ref, grad_ref, x_ref, w_gate_ref, w_out_ref, gain_ref, bias_ref, out_ref, gate_grad_ref, tile, hats, turned
):
    slab_at = lax.axis_index("slab")
    load_half(grad_ref, slab_at, tile)
    parts = tri_ref[...].astype(F32).reshape(CHANNELS, HALF, LANES)
    tri = parts[:, 0:LOW, :] + parts[:, LOW:HALF, :]
    average = jnp.mean(tri, axis=0, keepdims=True)
    centred = tri - average
    inv = lax.rsqrt(jnp.mean(centred * centred, axis=0, keepdims=True) + 1e-05)
    hats[...] = (centred * inv).reshape(CHANNELS * LOW, LANES)
    gain = jnp.broadcast_to(gain_ref[...], (CHANNELS, LANES)).T
    bias = jnp.broadcast_to(bias_ref[...], (CHANNELS, LANES)).T
    for low in range(LOW):
        here = pl.ds(low * LANES, LANES)
        hat = hats[pl.ds(low, CHANNELS, stride=LOW), :]
        mid_out = (hat * gain + bias).astype(BF16)
        proj_out = dot(mid_out, w_out_ref[...], 0, 0)
        gate = jax.nn.sigmoid(dot(x_ref[here, :], w_gate_ref[...], 1, 0))
        grad_in = jnp.concatenate([column(tile, low), column(tile, low + LOW)], axis=0)
        gate_grad_ref[here, :] = (grad_in * proj_out * gate * (1.0 - gate)).astype(BF16)
        mid_in_grad = (grad_in * gate).astype(BF16)
        grad_hat = dot(w_out_ref[...], mid_in_grad, 1, 1) * gain
        first = jnp.mean(grad_hat, axis=0, keepdims=True)
        second = jnp.mean(grad_hat * hat, axis=0, keepdims=True)
        tri_grad = (grad_hat - first - hat * second) * inv[0, low : low + 1, :]
        turned[pl.ds(low, CHANNELS, stride=LOW), :] = tri_grad
    once = turned[...].reshape(CHANNELS, LOW, LANES)
    out_ref[...] = jnp.concatenate([once, once], axis=1).astype(BF16).reshape(CHANNELS * HALF, LANES)


def grads_kernel(tri_grad_ref, left_ref, right_ref, out_ref, grid_t):
    depth = tri_grad_ref.shape[0] // 8
    for m in range(4):
        a = tri_grad_ref[pl.ds(2 * m * depth, depth), :].astype(F32)
        b = tri_grad_ref[pl.ds((2 * m + 1) * depth, depth), :].astype(F32)
        first, second = mix(a, b)
        both = jnp.concatenate(
            [first.reshape(32, LOW, LANES), second.reshape(32, LOW, LANES)], axis=1
        )
        grid_t[:, m * LANES : (m + 1) * LANES] = both.reshape(32 * HALF, LANES).astype(BF16)
    for m in range(4):
        at = slice(m * LANES, (m + 1) * LANES)
        left_grad = dot(right_ref[...], grid_t[:, at], 1, 0)
        right_grad = dot(left_ref[...], grid_t[at, :], 1, 1)
        first, second = mix(left_grad, right_grad)
        out_ref[pl.ds(2 * m * depth, depth), :] = first.astype(BF16)
        out_ref[pl.ds((2 * m + 1) * depth, depth), :] = second.astype(BF16)


def final_kernel(
    grads_ref, act_ref, x_ref, keep_ref, gate_grad_ref, w_proj_ref, w_gate_ref, gain_ref, out_ref,
    tile, grads, projected, proj_grad, x_grad, result,
):
    slab_at = lax.axis_index("slab")
    load_half(act_ref, slab_at, tile)
    grads[...] = grads_ref[...].astype(F32)
    projected[...] = dot(x_ref[...], w_proj_ref[...], 1, 0)
    for k in range(HALF):
        here = pl.ds(place(k), ROWS)
        both = (grads[pl.ds(k, CHANNELS, stride=HALF), :] * keep_ref[k : k + 1, :]).T
        for side in range(2):
            grad = both[side * ROWS : (side + 1) * ROWS, :]
            at = side * 256
            sig = jax.nn.sigmoid(projected[here, at : at + 128])
            value = projected[here, at + 128 : at + 256]
            proj_grad[here, at : at + 128] = (grad * value * sig * (1.0 - sig)).astype(BF16)
            proj_grad[here, at + 128 : at + 256] = (grad * sig).astype(BF16)
    x_grad[...] = dot(proj_grad[...], w_proj_ref[...], 1, 1) + dot(gate_grad_ref[...], w_gate_ref[...], 1, 1)
    for k in range(HALF):
        normed, inv_std = normalize(column(tile, k))
        in_hat = x_grad[pl.ds(place(k), ROWS), :] * gain_ref[...]
        first = jnp.mean(in_hat, axis=-1, keepdims=True)
        second = jnp.mean(in_hat * normed, axis=-1, keepdims=True)
        result[pl.ds(k, ROWS, stride=HALF), :] = (in_hat - first - normed * second) * inv_std
    out_ref[...] = result[...].reshape(ROWS, HALF, LANES).astype(BF16)


SMEM = pl.BlockSpec(memory_space=pltpu.SMEM)
VMEM = pl.BlockSpec(memory_space=pltpu.VMEM)


def call(kernel, outs, scratch, args, name, smem=0):
    single = not isinstance(outs, list)
    return pl.pallas_call(
        kernel,
        out_shape=outs,
        in_specs=[SMEM] * smem + [VMEM] * (len(args) - smem),
        out_specs=VMEM if single else [VMEM] * len(outs),
        scratch_shapes=scratch,
        compiler_params=pltpu.CompilerParams(vmem_limit_bytes=24 * 1024 * 1024),
        name=name,
    )(*args)


def shape(dims, kind):
    return jax.ShapeDtypeStruct(dims, kind)


def exchange(flat, axes, pieces):
    cut = flat.reshape(pieces, flat.shape[0] // pieces, LANES)
    return lax.all_to_all(cut, axes, 0, 0, tiled=True).reshape(flat.shape)


def on_device(
    pair_act, out_grad, pair_mask, chain_starts, in_gain, in_bias, w_proj, w_gate, w_out, mid_gain, mid_bias
):
    in_gain, in_bias, mid_gain, mid_bias = (
        v.reshape(1, LANES) for v in (in_gain, in_bias, mid_gain, mid_bias)
    )
    peers = lax.axis_size("row") * lax.axis_size("col")
    rows = CHANNELS * HALF
    edges, x_in, keep = call(
        edges_kernel,
        [shape((rows, LANES), BF16), shape((POINTS, LANES), BF16), shape((HALF, LANES), F32)],
        [
            pltpu.VMEM((POINTS, LANES), F32),
            pltpu.VMEM((LANES, LANES), F32),
            pltpu.VMEM((POINTS, 512), F32),
            pltpu.VMEM((rows, LANES), F32),
        ],
        (chain_starts, pair_act, pair_mask, in_gain, in_bias, w_proj),
        "edges",
        smem=1,
    )
    edges = exchange(edges, PEERS, peers)
    tri, left, right = call(
        triangle_kernel,
        [shape((rows, LANES), BF16), shape((256, 512), BF16), shape((256, 512), BF16)],
        [],
        (edges,),
        "triangle",
    )
    tri = exchange(tri, EVERYONE, peers * 2)
    tri_grad, gate_grad = call(
        middle_kernel,
        [shape((rows, LANES), BF16), shape((POINTS, LANES), BF16)],
        [
            pltpu.VMEM((POINTS, LANES), F32),
            pltpu.VMEM((CHANNELS * LOW, LANES), F32),
            pltpu.VMEM((CHANNELS * LOW, LANES), F32),
        ],
        (tri, out_grad, x_in, w_gate, w_out, mid_gain, mid_bias),
        "middle",
    )
    tri_grad = exchange(tri_grad, EVERYONE, peers * 2)
    grads = call(
        grads_kernel,
        shape((rows, LANES), BF16),
        [pltpu.VMEM((512, 512), BF16)],
        (tri_grad, left, right),
        "grads",
    )
    grads = exchange(grads, PEERS, peers)
    result = call(
        final_kernel,
        shape((ROWS, HALF, LANES), BF16),
        [
            pltpu.VMEM((POINTS, LANES), F32),
            pltpu.VMEM((rows, LANES), F32),
            pltpu.VMEM((POINTS, 512), F32),
            pltpu.VMEM((POINTS, 512), BF16),
            pltpu.VMEM((POINTS, LANES), F32),
            pltpu.VMEM((POINTS, LANES), F32),
        ],
        (grads, pair_act, x_in, keep, gate_grad, w_proj, w_gate, in_gain),
        "final",
    )
    return result.reshape(ROWS, 1, 1, HALF, LANES)


def solution(mesh):
    in_specs = (
        P("row", "col", None),
        P("row", "col", None),
        P("row", "col"),
        P(),
        P(),
        P(),
        P(),
        P(),
        P(),
        P(),
        P(),
    )
    out_specs = P("row", "col", "slab", None, None)
    return jax.shard_map(
        on_device, mesh=mesh, in_specs=in_specs, out_specs=out_specs, check_vma=False
    )
```

time: 701 us -> 125 us (0.18)
  waiting for transfers between devices: 597 us -> 0 us
  blocking collectives: 0 us -> 111 us
  local copies, waits for them, and re-layouts: 42.5 us -> 4.09 us
  matrix products: 25.3 us -> 0 us
  other arithmetic: 21.1 us -> 0 us
  between operations: 13.8 us -> 0.11 us
  Pallas kernels: 0 us -> 8.12 us
    all_gather x2 -> x0, waiting for transfers between devices: 228 us -> none  [the longest x1 116 us: on_device(): lax.all_gather(right_half, 'col', axis=1, tiled=True)]
    reduce_scatter x2 -> x0, waiting for transfers between devices: 204 us -> none  [the longest x1 103 us: on_device(): lax.psum_scatter(embedded.astype(jnp.bfloat16), 'col', scatter_dimension=...]
    psum x3 -> x0, waiting for transfers between devices: 164 us -> none  [the longest x1 55.8 us: on_device(): lax.psum(tri_part.astype(jnp.bfloat16), 'slab').astype(jnp.float32)]
    all_to_all x0 -> x4, blocking collectives: none -> 111 us  [exchange(): return lax.all_to_all(cut, axes, 0, 0, tiled=True).reshape(flat.shape)]
    dot_general x9 -> x0, matrix products: 25.3 us -> none  [the longest x1 8.01 us: on_device(): jnp.einsum('ijc,ikc->kjc', tri_grad, left_rows, preferred_element_type=jn...]
    all_gather x1 -> x0, local copies, waits for them, and re-layouts: 15.6 us -> none  [on_device(): lax.all_gather(left_half, 'col', axis=1, tiled=True)]
    dot_general x3 -> x0, local copies, waits for them, and re-layouts: 15.1 us -> none  [the longest x1 6.91 us: on_device(): jnp.einsum('ijc,jkc->kic', tri_grad, right_cols, preferred_element_type=j...]
    pallas_call x0 -> x5, Pallas kernels: none -> 8.12 us  [call(): pl.pallas_call(kernel, out_shape=outs, in_specs=[SMEM] * smem + [VMEM] *...]
  transfers between devices with their start and end apart: 7 -> 0, of which waited for: 7 -> 0; matrix products, arithmetic and copies ran while one was open for 5% -> 0% of each run, Pallas kernels for 0% -> 0%
where the time goes in v1:
time: 125 us; the launch traced here: 123 us
  blocking collectives  111 us (89%)
  Pallas kernels  8.12 us (6%)
  local copies, waits for them, and re-layouts  4.09 us (3%)
    all_to_all x4, blocking collectives, exchange(): return lax.all_to_all(cut, axes, 0, 0, tiled=True).reshape(flat.shape)  111 us
    pallas_call x5, Pallas kernels, call(): pl.pallas_call(kernel, out_shape=outs, in_specs=[SMEM] * smem + [VMEM] *...  8.12 us
    unnamed x25, local copies, waits for them, and re-layouts  4.09 us

profile of v1, /device:TPU:2, one launch (start us, length us, event | category | flops | bytes accessed | tf_op | source)
XLA Modules:
  0.0 123.4 jit_solution(7777210004222617643)
XLA Ops:
  0.0 0.8 copy.12.mask_ref
  0.8 0.0 copy-start.7
  0.8 0.0 copy-start.8
  0.8 0.0 copy-start.9
  0.8 0.6 copy-done.7
  1.5 0.0 copy-done.8
  1.5 0.0 copy-done.9
  1.5 0.0 copy-start
  1.5 1.0 copy-done
  2.5 0.0 copy-start.3
  2.5 0.9 copy-done.3
  3.4 2.0 %edges.1 = (bf16[2048,128]{1,0:T(8,128)(2,1)S(1)}, bf16[1024,128]{1,0:T(8,128)(2,1)S(1)}, f32[16,128]{1,0:T(8,128)S(1)}) custom-call(s32[6]{0:T(128)S(1)} %copy-done.8, bf16[64,32,128]{2,1,0:T(8,128)(2,1)S(1)} %copy-done, s32[64,32]{1,0:T(8,128)S(1)} %copy.12.mask_ref, f32[1,128]{1,0:T(1,128)S(1)} %bitcast.23, f32[1,128]{1,0:T(1,128)S(1)} %bitcast.25, ...), custom_call_target="tpu_custom_call" | custom-call | tf_op jit(solution)/shard_map/edges/pallas_call | solution.py:198
  5.5 31.1 %all_to_all.20 = bf16[128,16,128]{2,1,0:T(8,128)(2,1)S(1)} all-to-all(bf16[128,16,128]{2,1,0:T(8,128)(2,1)S(1)} %bitcast.20), channel_id=1, replica_groups=mesh['slab'=2,'row'=8,'col'=16] {'row','col'}, dimensions={0} | all-to-all | bytes 1048576 | tf_op jit(solution)/shard_map/all_to_all | solution.py:215
  36.5 0.8 triangle.1
  37.4 0.0 copy-start.2
  37.4 0.0 copy-start.5
  37.4 0.0 copy-start.6
  37.4 27.8 %all_to_all.21 = bf16[256,8,128]{2,1,0:T(8,128)(2,1)S(1)} all-to-all(bf16[256,8,128]{2,1,0:T(8,128)(2,1)S(1)} %bitcast.21), channel_id=1, replica_groups=mesh['slab'=2,'row'=8,'col'=16] {'row','col','slab'}, dimensions={0} | all-to-all | bytes 1048576 | tf_op jit(solution)/shard_map/all_to_all | solution.py:215
  65.3 0.0 copy-done.2
  65.3 0.0 copy-done.5
  65.3 0.0 copy-done.6
  65.3 0.6 copy-done.10
  65.9 0.0 copy-done.11
  65.9 1.2 middle.1
  67.2 26.3 %all_to_all.22 = bf16[256,8,128]{2,1,0:T(8,128)(2,1)S(1)} all-to-all(bf16[256,8,128]{2,1,0:T(8,128)(2,1)S(1)} %bitcast.22), channel_id=1, replica_groups=mesh['slab'=2,'row'=8,'col'=16] {'row','col','slab'}, dimensions={0} | all-to-all | bytes 1048576 | tf_op jit(solution)/shard_map/all_to_all | solution.py:215
  93.5 0.9 grads.1
  94.4 0.0 copy-start.1
  94.4 0.0 copy-start.4
  94.4 25.8 %all_to_all.23 = bf16[128,16,128]{2,1,0:T(8,128)(2,1)S(1)} all-to-all(bf16[128,16,128]{2,1,0:T(8,128)(2,1)S(1)} %bitcast.17), channel_id=1, replica_groups=mesh['slab'=2,'row'=8,'col'=16] {'row','col'}, dimensions={0} | all-to-all | bytes 1048576 | tf_op jit(solution)/shard_map/all_to_all | solution.py:215
  120.3 0.0 copy-done.1
  120.3 0.0 copy-done.4
  120.3 3.1 %final.1 = bf16[64,16,128]{2,1,0:T(8,128)(2,1)} custom-call(bf16[2048,128]{1,0:T(8,128)(2,1)S(1)} %bitcast.15, bf16[64,32,128]{2,1,0:T(8,128)(2,1)S(1)} %copy-done.1, bf16[1024,128]{1,0:T(8,128)(2,1)S(1)} %get-tuple-element.15.x_ref, f32[16,128]{1,0:T(8,128)S(1)} %get-tuple-element.19.keep_ref, bf16[1024,128]{1,0:T(8,128)(2,1)S(1)} %get-tuple-element.20.gate_grad_ref, ...), custom_call_target="tpu_custom_call" | custom-call | tf_op jit(solution)/shard_map/final/pallas_call | solution.py:198
  (2 shorter events, 0.0 us)
Async XLA Ops:
  0.8 0.7 copy-start.7
  0.8 0.7 copy-start.8
  0.8 0.7 copy-start.9
  1.5 1.0 copy-start
  2.5 0.9 copy-start.3
  37.4 27.9 %copy-start.2 = (bf16[64,32,128]{2,1,0:T(8,128)(2,1)S(1)}, bf16[64,32,128]{2,1,0:T(8,128)(2,1)}, u32[]{:S(2)}) copy-start(bf16[64,32,128]{2,1,0:T(8,128)(2,1)} %grad_ref.1) | copy-start | bytes 1572868
  37.4 27.9 %copy-start.5 = (bf16[128,128]{1,0:T(8,128)(2,1)S(1)}, bf16[128,128]{1,0:T(8,128)(2,1)}, u32[]{:S(2)}) copy-start(bf16[128,128]{1,0:T(8,128)(2,1)} %w_gate_ref.3) | copy-start | bytes 98308
  37.4 27.9 %copy-start.6 = (bf16[128,128]{1,0:T(8,128)(2,1)S(1)}, bf16[128,128]{1,0:T(8,128)(2,1)}, u32[]{:S(2)}) copy-start(bf16[128,128]{1,0:T(8,128)(2,1)} %w_out_ref.1) | copy-start | bytes 98308
  65.3 0.7 copy-start.10
  65.3 0.7 copy-start.11
  94.4 25.9 %copy-start.1 = (bf16[64,32,128]{2,1,0:T(8,128)(2,1)S(1)}, bf16[64,32,128]{2,1,0:T(8,128)(2,1)}, u32[]{:S(2)}) copy-start(bf16[64,32,128]{2,1,0:T(8,128)(2,1)} %act_ref.3) | copy-start | bytes 1572868
  94.4 25.9 %copy-start.4 = (bf16[128,512]{1,0:T(8,128)(2,1)S(1)}, bf16[128,512]{1,0:T(8,128)(2,1)}, u32[]{:S(2)}) copy-start(bf16[128,512]{1,0:T(8,128)(2,1)} %w_proj_ref.1) | copy-start | bytes 393220

commit v2 on v1

v2 whole, which is shorter than its diff:
```python
import jax
import jax.numpy as jnp
from jax import lax
from jax.experimental import pallas as pl
from jax.experimental.pallas import tpu as pltpu
from jax.sharding import Mesh
from jax.sharding import PartitionSpec as P

BF16 = jnp.bfloat16
F32 = jnp.float32
LANES = 128
ROWS = 64
HALF = 16
COLS = 2 * HALF
LOW = 8
CHANNELS = 128
OWN = CHANNELS // 2
POINTS = ROWS * HALF
LINES = 4
NEAR = ("x", "y", "z")
FAR = ("x", "y", "z", "slab")


def dot(a, b, ca, cb):
    return lax.dot_general(a, b, (((ca,), (cb,)), ((), ())), preferred_element_type=F32)


def place(k):
    return (k // HALF) * POINTS + ((k % LOW) * (HALF // LOW) + k % HALF // LOW) * ROWS


def normalize(values):
    average = jnp.mean(values, axis=-1, keepdims=True)
    centred = values - average
    inv_std = lax.rsqrt(jnp.mean(centred * centred, axis=-1, keepdims=True) + 1e-05)
    return centred * inv_std, inv_std


def mix(a, b):
    low = lax.broadcasted_iota(jnp.int32, a.shape, 1) < ROWS
    first = jnp.where(low, a, pltpu.roll(b, ROWS, 1))
    second = jnp.where(low, pltpu.roll(a, ROWS, 1), b)
    return first, second


def block(m):
    return slice(m * LANES, (m + 1) * LANES)


def load_half(ref, slab_at, scratch):
    start = pl.multiple_of(slab_at * HALF, HALF)
    scratch[...] = ref[:, pl.ds(start, HALF), :].astype(F32).reshape(POINTS, LANES)


def column(scratch, k, width=HALF):
    return scratch[pl.ds(k, ROWS, stride=width), :]


def keep_rows(mask_ref, starts_ref, slab_at, row_at, col_at):
    mask = mask_ref[...].astype(F32)
    twice = jnp.concatenate([mask, mask], axis=0)
    wide = jnp.concatenate([twice, jnp.zeros((LANES, LANES - COLS), F32)], axis=1)
    shape = (COLS, LANES)
    lane = lax.broadcasted_iota(jnp.int32, shape, 1)
    row_ids = row_at * ROWS + jnp.where(lane < ROWS, lane, lane - ROWS)
    col_ids = col_at * COLS + lax.broadcasted_iota(jnp.int32, shape, 0)
    row_chain = jnp.zeros(shape, jnp.int32)
    col_chain = jnp.zeros(shape, jnp.int32)
    for at in range(starts_ref.shape[0]):
        start_at = starts_ref[at]
        row_chain = row_chain + (row_ids >= start_at).astype(jnp.int32)
        col_chain = col_chain + (col_ids >= start_at).astype(jnp.int32)
    return jnp.where((row_chain == col_chain) | (wide.T[0:COLS, :] > 0.0), 1.0, 0.0)


def edges_kernel(
    starts_ref, act_ref, mask_ref, gain_ref, bias_ref, w_ref, edges_ref, x_ref, keep_ref, tile, kept, x_all, projected, turned
):
    slab_at = lax.axis_index("slab")
    row_at = lax.axis_index("x") * 2 + lax.axis_index("core")
    col_at = lax.axis_index("y") * 4 + lax.axis_index("z")
    tile[...] = act_ref[...].astype(F32).reshape(ROWS * COLS, LANES)
    kept[...] = keep_rows(mask_ref, starts_ref, slab_at, row_at, col_at)
    keep_ref[...] = kept[pl.ds(pl.multiple_of(slab_at * HALF, HALF), HALF), :]
    for k in range(COLS):
        normed, _ = normalize(column(tile, k, COLS))
        x_all[pl.ds(place(k), ROWS), :] = (normed * gain_ref[...] + bias_ref[...]).astype(BF16)
    x_ref[...] = x_all[pl.ds(pl.multiple_of(slab_at * POINTS, POINTS), POINTS), :]
    own = []
    for at in range(2):
        first, second = mix(w_ref[:, block(at)].astype(F32), w_ref[:, block(at + 2)].astype(F32))
        own.append(jnp.where(slab_at == 0, first, second).astype(BF16))
    projected[...] = dot(x_all[...], jnp.concatenate(own, axis=1), 1, 0)
    for k in range(HALF):
        parts = []
        for at in (k, k + HALF):
            here = pl.ds(place(at), ROWS)
            parts.append(jax.nn.sigmoid(projected[here, 0:128]) * projected[here, 128:256])
        both = jnp.concatenate(parts, axis=0).T
        low = lax.broadcasted_iota(jnp.int32, (1, LANES), 1) < ROWS
        both = both * jnp.where(low, kept[k : k + 1, :], kept[k + HALF : k + HALF + 1, :])
        turned[pl.ds(k, OWN, stride=COLS), :] = both[0:OWN, :]
        turned[pl.ds(k + HALF, OWN, stride=COLS), :] = both[OWN:CHANNELS, :]
    edges_ref[...] = turned[...].astype(BF16)


def sort_kernel(edges_ref, left_ref, right_ref):
    for m in range(LINES // 2):
        pair = edges_ref[pl.ds(m * 1024, 1024), :].astype(F32).reshape(2, 16, COLS, LANES)
        for side, ref in enumerate((left_ref, right_ref)):
            a, b = (
                pair[at, :, side * HALF : (side + 1) * HALF, :].reshape(16 * HALF, LANES)
                for at in range(2)
            )
            first, second = mix(a, b)
            both = jnp.concatenate(
                [first.reshape(16, HALF, LANES), second.reshape(16, HALF, LANES)], axis=1
            )
            ref[:, block(m)] = both.reshape(512, LANES).astype(BF16)


def triangle_kernel(left_ref, own_ref, other_ref, out_ref, right_ref):
    core_at = lax.axis_index("core")
    for m in range(LINES // 2):
        own, other = own_ref[:, block(m)].astype(F32), other_ref[:, block(m)].astype(F32)
        a = jnp.where(core_at == 0, own, other)
        b = jnp.where(core_at == 0, other, own)
        first, second = mix(a, b)
        right_ref[:, block(2 * m)] = first.astype(BF16)
        right_ref[:, block(2 * m + 1)] = second.astype(BF16)
    for m in range(LINES // 2):
        tri = dot(right_ref[...], left_ref[:, block(m)], 0, 0)
        tri = tri.reshape(32, HALF, LANES)
        a = tri[:, 0:LOW, :].reshape(256, LANES)
        b = tri[:, LOW:HALF, :].reshape(256, LANES)
        first, second = mix(a, b)
        out_ref[pl.ds(2 * m * 256, 256), :] = first.astype(BF16)
        out_ref[pl.ds((2 * m + 1) * 256, 256), :] = second.astype(BF16)


def middle_kernel(
    tri_ref, grad_ref, x_ref, w_gate_ref, w_out_ref, gain_ref, bias_ref, out_ref, gate_grad_ref, tile, hats, turned
):
    slab_at = lax.axis_index("slab")
    load_half(grad_ref, slab_at, tile)
    parts = tri_ref[...].astype(F32).reshape(OWN, 2 * LOW, LANES)
    tri = jnp.concatenate([parts[:, 0:LOW, :], parts[:, LOW : 2 * LOW, :]], axis=0)
    average = jnp.mean(tri, axis=0, keepdims=True)
    centred = tri - average
    inv = lax.rsqrt(jnp.mean(centred * centred, axis=0, keepdims=True) + 1e-05)
    hats[...] = (centred * inv).reshape(CHANNELS * LOW, LANES)
    gain = jnp.broadcast_to(gain_ref[...], (CHANNELS, LANES)).T
    bias = jnp.broadcast_to(bias_ref[...], (CHANNELS, LANES)).T
    for low in range(LOW):
        here = pl.ds(low * LANES, LANES)
        hat = hats[pl.ds(low, CHANNELS, stride=LOW), :]
        mid_out = (hat * gain + bias).astype(BF16)
        proj_out = dot(mid_out, w_out_ref[...], 0, 0)
        gate = jax.nn.sigmoid(dot(x_ref[here, :], w_gate_ref[...], 1, 0))
        grad_in = jnp.concatenate([column(tile, low), column(tile, low + LOW)], axis=0)
        gate_grad_ref[here, :] = (grad_in * proj_out * gate * (1.0 - gate)).astype(BF16)
        mid_in_grad = (grad_in * gate).astype(BF16)
        grad_hat = dot(w_out_ref[...], mid_in_grad, 1, 1) * gain
        first = jnp.mean(grad_hat, axis=0, keepdims=True)
        second = jnp.mean(grad_hat * hat, axis=0, keepdims=True)
        tri_grad = (grad_hat - first - hat * second) * inv[0, low : low + 1, :]
        turned[pl.ds(low, CHANNELS, stride=LOW), :] = tri_grad
    done = turned[...].reshape(CHANNELS, LOW, LANES)
    both = jnp.concatenate([done[0:OWN], done[OWN:CHANNELS]], axis=1)
    out_ref[...] = both.astype(BF16).reshape(CHANNELS * LOW, LANES)


def grads_kernel(tri_grad_ref, left_ref, right_ref, left_grad_ref, own_ref, other_ref, grid_t):
    core_at = lax.axis_index("core")
    for m in range(LINES // 2):
        a = tri_grad_ref[pl.ds(2 * m * 256, 256), :].astype(F32)
        b = tri_grad_ref[pl.ds((2 * m + 1) * 256, 256), :].astype(F32)
        first, second = mix(a, b)
        both = jnp.concatenate(
            [first.reshape(32, LOW, LANES), second.reshape(32, LOW, LANES)], axis=1
        )
        grid_t[:, block(m)] = both.reshape(32 * HALF, LANES).astype(BF16)
    for m in range(LINES // 2):
        a = dot(left_ref[...], grid_t[pl.ds(2 * m * LANES, LANES), :], 1, 1)
        b = dot(left_ref[...], grid_t[pl.ds((2 * m + 1) * LANES, LANES), :], 1, 1)
        first, second = mix(a, b)
        own_ref[:, block(m)] = jnp.where(core_at == 0, first, second)
        other_ref[:, block(m)] = jnp.where(core_at == 0, second, first).astype(BF16)
    for m in range(LINES // 2):
        left_grad_ref[:, block(m)] = dot(right_ref[...], grid_t[:, block(m)], 1, 0)


def join_kernel(left_grad_ref, own_ref, other_ref, out_ref):
    for m in range(LINES // 2):
        right_grad = own_ref[:, block(m)] + other_ref[:, block(m)].astype(F32)
        first, second = mix(left_grad_ref[:, block(m)], right_grad)
        out_ref[pl.ds(2 * m * 512, 512), :] = first.astype(BF16)
        out_ref[pl.ds((2 * m + 1) * 512, 512), :] = second.astype(BF16)


def final_kernel(
    grads_ref, act_ref, x_ref, keep_ref, gate_grad_ref, w_proj_ref, w_gate_ref, gain_ref, out_ref,
    tile, grads, projected, proj_grad, x_grad, result,
):
    slab_at = lax.axis_index("slab")
    load_half(act_ref, slab_at, tile)
    grads[...] = grads_ref[...].astype(F32)
    projected[...] = dot(x_ref[...], w_proj_ref[...], 1, 0)
    for k in range(HALF):
        here = pl.ds(place(k), ROWS)
        both = jnp.concatenate(
            [grads[pl.ds(k + at, OWN, stride=2 * HALF), :] for at in (0, HALF)], axis=0
        )
        both = (both * keep_ref[k : k + 1, :]).T
        for side in range(2):
            grad = both[side * ROWS : (side + 1) * ROWS, :]
            at = side * 256
            sig = jax.nn.sigmoid(projected[here, at : at + 128])
            value = projected[here, at + 128 : at + 256]
            proj_grad[here, at : at + 128] = (grad * value * sig * (1.0 - sig)).astype(BF16)
            proj_grad[here, at + 128 : at + 256] = (grad * sig).astype(BF16)
    x_grad[...] = dot(proj_grad[...], w_proj_ref[...], 1, 1) + dot(gate_grad_ref[...], w_gate_ref[...], 1, 1)
    for k in range(HALF):
        normed, inv_std = normalize(column(tile, k))
        in_hat = x_grad[pl.ds(place(k), ROWS), :] * gain_ref[...]
        first = jnp.mean(in_hat, axis=-1, keepdims=True)
        second = jnp.mean(in_hat * normed, axis=-1, keepdims=True)
        result[pl.ds(k, ROWS, stride=HALF), :] = (in_hat - first - normed * second) * inv_std
    out_ref[...] = result[...].reshape(ROWS, HALF, LANES).astype(BF16)


SMEM = pl.BlockSpec(memory_space=pltpu.SMEM)
VMEM = pl.BlockSpec(memory_space=pltpu.VMEM)


def call(kernel, outs, scratch, args, name, smem=0):
    single = not isinstance(outs, list)
    return pl.pallas_call(
        kernel,
        out_shape=outs,
        in_specs=[SMEM] * smem + [VMEM] * (len(args) - smem),
        out_specs=VMEM if single else [VMEM] * len(outs),
        scratch_shapes=scratch,
        compiler_params=pltpu.CompilerParams(vmem_limit_bytes=24 * 1024 * 1024),
        name=name,
    )(*args)


def shape(dims, kind):
    return jax.ShapeDtypeStruct(dims, kind)


def exchange(flat, axes):
    pieces = lax.axis_size(axes)
    cut = flat.reshape(pieces, flat.shape[0] // pieces, LANES)
    return lax.all_to_all(cut, axes, 0, 0, tiled=True).reshape(flat.shape)


def swap(x):
    return lax.ppermute(x, "core", [(0, 1), (1, 0)])


def on_device(
    pair_act, out_grad, pair_mask, chain_starts, in_gain, in_bias, w_proj, w_gate, w_out, mid_gain, mid_bias
):
    in_gain, in_bias, mid_gain, mid_bias = (
        v.reshape(1, LANES) for v in (in_gain, in_bias, mid_gain, mid_bias)
    )
    edge_rows = OWN * COLS
    tri_rows = CHANNELS * LOW
    edges, x_in, keep = call(
        edges_kernel,
        [shape((edge_rows, LANES), BF16), shape((POINTS, LANES), BF16), shape((HALF, LANES), F32)],
        [
            pltpu.VMEM((2 * POINTS, LANES), F32),
            pltpu.VMEM((COLS, LANES), F32),
            pltpu.VMEM((2 * POINTS, LANES), BF16),
            pltpu.VMEM((2 * POINTS, 256), F32),
            pltpu.VMEM((edge_rows, LANES), F32),
        ],
        (chain_starts, pair_act, pair_mask, in_gain, in_bias, w_proj),
        "edges",
        smem=1,
    )
    edges = exchange(edges, NEAR)
    left, own = call(
        sort_kernel, [shape((512, 256), BF16), shape((512, 256), BF16)], [], (edges,), "sort"
    )
    tri, right = call(
        triangle_kernel,
        [shape((tri_rows, LANES), BF16), shape((512, 512), BF16)],
        [],
        (left, own, swap(own)),
        "triangle",
    )
    tri = exchange(tri, FAR)
    tri_grad, gate_grad = call(
        middle_kernel,
        [shape((tri_rows, LANES), BF16), shape((POINTS, LANES), BF16)],
        [
            pltpu.VMEM((POINTS, LANES), F32),
            pltpu.VMEM((tri_rows, LANES), F32),
            pltpu.VMEM((tri_rows, LANES), F32),
        ],
        (tri, out_grad, x_in, w_gate, w_out, mid_gain, mid_bias),
        "middle",
    )
    tri_grad = exchange(tri_grad, FAR)
    left_grad, own, other = call(
        grads_kernel,
        [shape((512, 256), F32), shape((512, 256), F32), shape((512, 256), BF16)],
        [pltpu.VMEM((512, 256), BF16)],
        (tri_grad, left, right),
        "grads",
    )
    grads = call(
        join_kernel, shape((CHANNELS * HALF, LANES), BF16), [], (left_grad, own, swap(other)), "join"
    )
    grads = exchange(grads, FAR)
    result = call(
        final_kernel,
        shape((ROWS, HALF, LANES), BF16),
        [
            pltpu.VMEM((POINTS, LANES), F32),
            pltpu.VMEM((CHANNELS * HALF, LANES), F32),
            pltpu.VMEM((POINTS, 512), F32),
            pltpu.VMEM((POINTS, 512), BF16),
            pltpu.VMEM((POINTS, LANES), F32),
            pltpu.VMEM((POINTS, LANES), F32),
        ],
        (grads, pair_act, x_in, keep, gate_grad, w_proj, w_gate, in_gain),
        "final",
    )
    return result.reshape(ROWS, 1, 1, HALF, LANES)


def solution(mesh):
    fine = Mesh(mesh.devices.reshape(2, LINES, 2, 4, 4), ("slab", "x", "core", "y", "z"))
    row, col = ("x", "core"), ("y", "z")
    in_specs = (P(row, col, None), P(row, col, None), P(row, col)) + (P(),) * 8
    out_specs = P(row, col, "slab", None, None)
    return jax.shard_map(
        on_device, mesh=fine, in_specs=in_specs, out_specs=out_specs, check_vma=False
    )
```

time: 125 us -> 118 us (0.944)
  blocking collectives: 111 us -> 99.4 us
  waiting for transfers between devices: 0 us -> 3.04 us
  Pallas kernels: 8.12 us -> 10.5 us
    all_to_all x4, blocking collectives: 111 us -> 99.4 us  [exchange(): return lax.all_to_all(cut, axes, 0, 0, tiled=True).reshape(flat.shape)]
    ppermute x0 -> x2, waiting for transfers between devices: none -> 3.04 us  [swap(): return lax.ppermute(x, 'core', [(0, 1), (1, 0)])]
    pallas_call x5 -> x7, Pallas kernels: 8.12 us -> 10.5 us  [call(): pl.pallas_call(kernel, out_shape=outs, in_specs=[SMEM] * smem + [VMEM] *...]
  transfers between devices with their start and end apart: 0 -> 2, of which waited for: 0 -> 2; matrix products, arithmetic and copies ran while one was open for 0% -> 0% of each run, Pallas kernels for 0% -> 0%
where the time goes in v2:
time: 118 us; the launch traced here: 117 us
  blocking collectives  99.4 us (84%)
  Pallas kernels  10.5 us (9%)
  local copies, waits for them, and re-layouts  4.09 us (3%)
  waiting for transfers between devices  3.04 us (3%)
    all_to_all x4, blocking collectives, exchange(): return lax.all_to_all(cut, axes, 0, 0, tiled=True).reshape(flat.shape)  99.4 us
    pallas_call x7, Pallas kernels, call(): pl.pallas_call(kernel, out_shape=outs, in_specs=[SMEM] * smem + [VMEM] *...  10.5 us
    unnamed x25, local copies, waits for them, and re-layouts  4.09 us
    ppermute x2, waiting for transfers between devices, swap(): return lax.ppermute(x, 'core', [(0, 1), (1, 0)])  3.04 us
  transfers between devices with their start and end apart: 2, of which 2 were waited for; matrix products, arithmetic and copies ran while one was open for 0% of the time, Pallas kernels for 0%

profile of v2, /device:TPU:2, one launch (start us, length us, event | category | flops | bytes accessed | tf_op | source)
XLA Modules:
  0.0 117.4 jit_solution(17166837376733244203)
XLA Ops:
  0.0 0.8 copy.12.mask_ref
  0.8 0.0 copy-start.10
  0.8 0.0 copy-start.11
  0.8 0.6 copy-done.7
  1.5 0.0 copy-done.10
  1.5 0.0 copy-done.11
  1.5 1.0 copy-done
  2.5 0.9 copy-done.3
  3.4 3.9 %edges.1 = (bf16[2048,128]{1,0:T(8,128)(2,1)S(1)}, bf16[1024,128]{1,0:T(8,128)(2,1)S(1)}, f32[16,128]{1,0:T(8,128)S(1)}) custom-call(s32[6]{0:T(128)S(1)} %copy-done.10, bf16[64,32,128]{2,1,0:T(8,128)(2,1)S(1)} %copy-done, s32[64,32]{1,0:T(8,128)S(1)} %copy.12.mask_ref, f32[1,128]{1,0:T(1,128)S(1)} %bitcast.23, f32[1,128]{1,0:T(1,128)S(1)} %bitcast.27, ...), custom_call_target="tpu_custom_call" | custom-call | tf_op jit(solution)/shard_map/edges/pallas_call | solution.py:238
  7.4 29.1 %all_to_all.20 = bf16[64,32,128]{2,1,0:T(8,128)(2,1)S(1)} all-to-all(bf16[64,32,128]{2,1,0:T(8,128)(2,1)S(1)} %bitcast.20), channel_id=1, replica_groups=mesh['slab'=2,'x'=4,'core'=2,'y'=4,'z'=4] {'x','y','z'}, dimensions={0} | all-to-all | bytes 1048576 | tf_op jit(solution)/shard_map/all_to_all | solution.py:256
  36.5 0.2 sort.1
  36.7 0.1 collective-permute-start
  36.8 1.5 %collective-permute-done.other_ref = bf16[512,256]{1,0:T(8,128)(2,1)S(1)} collective-permute-done((bf16[512,256]{1,0:T(8,128)(2,1)S(1)}, bf16[512,256]{1,0:T(8,128)(2,1)S(1)}, u32[]{:S(2)}, u32[]{:S(2)}) %collective-permute-start) | collective-permute-done | bytes 262176 | tf_op jit(solution)/shard_map/ppermute | solution.py:260
  38.3 0.8 triangle.1
  39.2 0.0 copy-start.5
  39.2 0.0 copy-start.6
  39.2 23.8 %all_to_all.21 = bf16[128,8,128]{2,1,0:T(8,128)(2,1)S(1)} all-to-all(bf16[128,8,128]{2,1,0:T(8,128)(2,1)S(1)} %bitcast.21), channel_id=1, replica_groups=mesh['slab'=2,'x'=4,'core'=2,'y'=4,'z'=4] {'x','y','z','slab'}, dimensions={0} | all-to-all | bytes 524288 | tf_op jit(solution)/shard_map/all_to_all | solution.py:256
  63.0 0.0 copy-done.2
  63.0 0.0 copy-done.5
  63.0 0.0 copy-done.6
  63.0 0.6 copy-done.8
  63.7 0.0 copy-done.9
  63.7 1.2 %middle.1 = (bf16[1024,128]{1,0:T(8,128)(2,1)S(1)}, bf16[1024,128]{1,0:T(8,128)(2,1)S(1)}) custom-call(bf16[1024,128]{1,0:T(8,128)(2,1)S(1)} %bitcast.18, bf16[64,32,128]{2,1,0:T(8,128)(2,1)S(1)} %copy-done.2, bf16[1024,128]{1,0:T(8,128)(2,1)S(1)} %get-tuple-element.21.x_ref, bf16[128,128]{1,0:T(8,128)(2,1)S(1)} %copy-done.5, ...), custom_call_target="tpu_custom_call" | custom-call | tf_op jit(solution)/shard_map/middle/pallas_call | solution.py:238
  64.9 19.9 %all_to_all.22 = bf16[128,8,128]{2,1,0:T(8,128)(2,1)S(1)} all-to-all(bf16[128,8,128]{2,1,0:T(8,128)(2,1)S(1)} %bitcast.22), channel_id=1, replica_groups=mesh['slab'=2,'x'=4,'core'=2,'y'=4,'z'=4] {'x','y','z','slab'}, dimensions={0} | all-to-all | bytes 524288 | tf_op jit(solution)/shard_map/all_to_all | solution.py:256
  84.8 0.8 grads.1
  85.6 0.1 collective-permute-start.1
  85.7 1.5 %collective-permute-done.1.other_ref = bf16[512,256]{1,0:T(8,128)(2,1)S(1)} collective-permute-done((bf16[512,256]{1,0:T(8,128)(2,1)S(1)}, bf16[512,256]{1,0:T(8,128)(2,1)S(1)}, u32[]{:S(2)}, u32[]{:S(2)}) %collective-permute-start.1) | collective-permute-done | bytes 262176 | tf_op jit(solution)/shard_map/ppermute | solution.py:260
  87.2 0.2 join.1
  87.4 0.0 copy-start.1
  87.4 0.0 copy-start.4
  87.4 26.6 %all_to_all.23 = bf16[128,16,128]{2,1,0:T(8,128)(2,1)S(1)} all-to-all(bf16[128,16,128]{2,1,0:T(8,128)(2,1)S(1)} %bitcast.16), channel_id=1, replica_groups=mesh['slab'=2,'x'=4,'core'=2,'y'=4,'z'=4] {'x','y','z','slab'}, dimensions={0} | all-to-all | bytes 1048576 | tf_op jit(solution)/shard_map/all_to_all | solution.py:256
  114.0 3.4 %final.1 = bf16[64,16,128]{2,1,0:T(8,128)(2,1)} custom-call(bf16[2048,128]{1,0:T(8,128)(2,1)S(1)} %bitcast.15, bf16[64,32,128]{2,1,0:T(8,128)(2,1)S(1)} %copy-done.1, bf16[1024,128]{1,0:T(8,128)(2,1)S(1)} %get-tuple-element.21.x_ref, f32[16,128]{1,0:T(8,128)S(1)} %get-tuple-element.27.keep_ref, bf16[1024,128]{1,0:T(8,128)(2,1)S(1)} %get-tuple-element.28.gate_grad_ref, ...), custom_call_target="tpu_custom_call" | custom-call | tf_op jit(solution)/shard_map/final/pallas_call | solution.py:238
  (8 shorter events, 0.0 us)
Async XLA Ops:
  0.8 0.7 copy-start.7
  0.8 0.7 copy-start.10
  0.8 0.7 copy-start.11
  1.5 1.0 copy-start
  2.5 0.9 copy-start.3
  36.7 1.6 %collective-permute-start = (bf16[512,256]{1,0:T(8,128)(2,1)S(1)}, bf16[512,256]{1,0:T(8,128)(2,1)S(1)}, u32[]{:S(2)}, u32[]{:S(2)}) collective-permute-start(bf16[512,256]{1,0:T(8,128)(2,1)S(1)} %get-tuple-element.19.own_ref), channel_id=1, source_target_pairs={{0,16},{16,0},{1,17},{17,1},{2,18},{18,2},{3,19},{19,3},{4,20},{20... | collective-permute-start | bytes 786440 | tf_op jit(solution)/shard_map/ppermute | solution.py:260
  38.3 24.7 %copy-start.2 = (bf16[64,32,128]{2,1,0:T(8,128)(2,1)S(1)}, bf16[64,32,128]{2,1,0:T(8,128)(2,1)}, u32[]{:S(2)}) copy-start(bf16[64,32,128]{2,1,0:T(8,128)(2,1)} %grad_ref.1) | copy-start | bytes 1572868
  39.2 23.9 %copy-start.5 = (bf16[128,128]{1,0:T(8,128)(2,1)S(1)}, bf16[128,128]{1,0:T(8,128)(2,1)}, u32[]{:S(2)}) copy-start(bf16[128,128]{1,0:T(8,128)(2,1)} %w_gate_ref.3) | copy-start | bytes 98308
  39.2 23.8 %copy-start.6 = (bf16[128,128]{1,0:T(8,128)(2,1)S(1)}, bf16[128,128]{1,0:T(8,128)(2,1)}, u32[]{:S(2)}) copy-start(bf16[128,128]{1,0:T(8,128)(2,1)} %w_out_ref.1) | copy-start | bytes 98308
  63.0 0.7 copy-start.8
  63.0 0.7 copy-start.9
  85.6 1.6 %collective-permute-start.1 = (bf16[512,256]{1,0:T(8,128)(2,1)S(1)}, bf16[512,256]{1,0:T(8,128)(2,1)S(1)}, u32[]{:S(2)}, u32[]{:S(2)}) collective-permute-start(bf16[512,256]{1,0:T(8,128)(2,1)S(1)} %get-tuple-element.26), channel_id=1, source_target_pairs={{0,16},{16,0},{1,17},{17,1},{2,18},{18,2},{3,19},{19,3},{4,20},{20... | collective-permute-start | bytes 786440 | tf_op jit(solution)/shard_map/ppermute | solution.py:260
  87.4 26.6 %copy-start.1 = (bf16[64,32,128]{2,1,0:T(8,128)(2,1)S(1)}, bf16[64,32,128]{2,1,0:T(8,128)(2,1)}, u32[]{:S(2)}) copy-start(bf16[64,32,128]{2,1,0:T(8,128)(2,1)} %act_ref.3) | copy-start | bytes 1572868
  87.4 26.6 %copy-start.4 = (bf16[128,512]{1,0:T(8,128)(2,1)S(1)}, bf16[128,512]{1,0:T(8,128)(2,1)}, u32[]{:S(2)}) copy-start(bf16[128,512]{1,0:T(8,128)(2,1)} %w_proj_ref.1) | copy-start | bytes 393220

commit v3 on v2

v3 whole, which is shorter than its diff:
```python
import jax
import jax.numpy as jnp
from jax import lax
from jax.experimental import pallas as pl
from jax.experimental.pallas import tpu as pltpu
from jax.sharding import Mesh
from jax.sharding import PartitionSpec as P

BF16 = jnp.bfloat16
F32 = jnp.float32
LANES = 128
ROWS = 64
HALF = 16
COLS = 2 * HALF
LOW = 8
CHANNELS = 128
OWN = CHANNELS // 2
POINTS = ROWS * HALF
LINES = 4
NEAR = ("z", "x", "y")
FAR = ("z", "x", "y", "slab")


def dot(a, b, ca, cb):
    return lax.dot_general(a, b, (((ca,), (cb,)), ((), ())), preferred_element_type=F32)


def place(k):
    return ((k % LOW) * (HALF // LOW) + k // LOW) * ROWS


def normalize(values):
    average = jnp.mean(values, axis=-1, keepdims=True)
    centred = values - average
    inv_std = lax.rsqrt(jnp.mean(centred * centred, axis=-1, keepdims=True) + 1e-05)
    return centred * inv_std, inv_std


def mix(a, b):
    low = lax.broadcasted_iota(jnp.int32, a.shape, 1) < ROWS
    first = jnp.where(low, a, pltpu.roll(b, ROWS, 1))
    second = jnp.where(low, pltpu.roll(a, ROWS, 1), b)
    return first, second


def block(m):
    return slice(m * LANES, (m + 1) * LANES)


def load_half(ref, slab_at, scratch):
    start = pl.multiple_of(slab_at * HALF, HALF)
    scratch[...] = ref[:, pl.ds(start, HALF), :].astype(F32).reshape(POINTS, LANES)


def column(scratch, k, width=HALF):
    return scratch[pl.ds(k, ROWS, stride=width), :]


def two_columns(scratch, low):
    return jnp.concatenate([column(scratch, low), column(scratch, low + LOW)], axis=0)


def keep_rows(mask, starts_ref, row_at, col_at):
    wide = jnp.concatenate([mask, mask], axis=1)
    shape = (COLS, LANES)
    lane = lax.broadcasted_iota(jnp.int32, shape, 1)
    row_ids = row_at * ROWS + jnp.where(lane < ROWS, lane, lane - ROWS)
    col_ids = col_at * COLS + lax.broadcasted_iota(jnp.int32, shape, 0)
    row_chain = jnp.zeros(shape, jnp.int32)
    col_chain = jnp.zeros(shape, jnp.int32)
    for at in range(starts_ref.shape[0]):
        start_at = starts_ref[at]
        row_chain = row_chain + (row_ids >= start_at).astype(jnp.int32)
        col_chain = col_chain + (col_ids >= start_at).astype(jnp.int32)
    return jnp.where((row_chain == col_chain) | (wide > 0), 1.0, 0.0)


def halves(a, b):
    return jnp.where(lax.broadcasted_iota(jnp.int32, a.shape, 1) < ROWS, a, b)


def edges_kernel(
    starts_ref, act_ref, mask_ref, gain_ref, bias_ref, w_ref, edges_ref, x_ref, keep_ref,
    tile, kept, x_all, projected, turned,
):
    slab_at = lax.axis_index("slab")
    row_at = lax.axis_index("x") * 2 + lax.axis_index("core")
    col_at = lax.axis_index("y") * 4 + lax.axis_index("z")
    kept[...] = keep_rows(mask_ref[...], starts_ref, row_at, col_at)
    start = pl.multiple_of(slab_at * HALF, HALF)
    keep_ref[...] = halves(kept[pl.ds(start, LOW), :], kept[pl.ds(start + LOW, LOW), :])
    own = []
    for at in range(2):
        first, second = mix(w_ref[:, block(at)].astype(F32), w_ref[:, block(at + 2)].astype(F32))
        own.append(jnp.where(slab_at == 0, first, second).astype(BF16))
    w_own = jnp.concatenate(own, axis=1)
    tile[...] = act_ref[...].astype(F32).reshape(ROWS * COLS, LANES)
    for k in range(COLS):
        normed, _ = normalize(column(tile, k, COLS))
        at = (k % HALF * 2 + k // HALF) * ROWS
        x_all[pl.ds(at, ROWS), :] = (normed * gain_ref[...] + bias_ref[...]).astype(BF16)
    projected[...] = dot(w_own, x_all[...], 0, 1)
    for k in range(HALF):
        both = jax.nn.sigmoid(projected[0:128, block(k)]) * projected[128:256, block(k)]
        both = both * halves(kept[k : k + 1, :], kept[k + HALF : k + HALF + 1, :])
        turned[pl.ds(k, OWN, stride=COLS), :] = both[0:OWN, :]
        turned[pl.ds(k + HALF, OWN, stride=COLS), :] = both[OWN:CHANNELS, :]
    edges_ref[...] = turned[...].astype(BF16)
    for k in range(HALF):
        mine = pl.multiple_of(2 * k * ROWS + slab_at * ROWS, ROWS)
        x_ref[pl.ds(place(k), ROWS), :] = x_all[pl.ds(mine, ROWS), :]


def ahead_kernel(
    act_ref, grad_ref, x_ref, keep_ref, w_proj_ref, w_gate_ref, w_out_ref, gain_ref, in_gain_ref,
    slope_ref, grad_hat_ref, factor_ref, normed_ref, inv_ref, tall_gain_ref, tile, projected,
):
    tall_gain_ref[...] = jnp.broadcast_to(in_gain_ref[...], (LANES, LANES)).T
    slab_at = lax.axis_index("slab")
    load_half(grad_ref, slab_at, tile)
    gain = jnp.broadcast_to(gain_ref[...], (CHANNELS, LANES)).T
    for low in range(LOW):
        here = pl.ds(low * LANES, LANES)
        gate = jax.nn.sigmoid(dot(x_ref[here, :], w_gate_ref[...], 1, 0))
        grad_in = two_columns(tile, low)
        slope_ref[here, :] = grad_in * gate * (1.0 - gate)
        mid_in_grad = (grad_in * gate).astype(BF16)
        grad_hat = dot(w_out_ref[...], mid_in_grad, 1, 1) * gain
        grad_hat_ref[pl.ds(low, CHANNELS, stride=LOW), :] = grad_hat - jnp.mean(grad_hat, axis=0, keepdims=True)
    load_half(act_ref, slab_at, tile)
    for low in range(LOW):
        values = two_columns(tile, low).T
        centred = values - jnp.mean(values, axis=0, keepdims=True)
        inv = lax.rsqrt(jnp.mean(centred * centred, axis=0, keepdims=True) + 1e-05)
        normed_ref[:, block(low)] = centred * inv
        inv_ref[:, block(low)] = inv
    projected[...] = dot(w_proj_ref[...], x_ref[...], 0, 1)
    for low in range(LOW):
        keep = keep_ref[low : low + 1, :]
        for side in range(2):
            at = side * 256
            sig = jax.nn.sigmoid(projected[at : at + 128, block(low)])
            value = projected[at + 128 : at + 256, block(low)]
            factor_ref[at : at + 128, block(low)] = (keep * value * sig * (1.0 - sig)).astype(BF16)
            factor_ref[at + 128 : at + 256, block(low)] = (keep * sig).astype(BF16)


def sort_kernel(edges_ref, left_ref, right_ref):
    for m in range(LINES // 2):
        for side, ref in enumerate((left_ref, right_ref)):
            a, b = (
                jnp.concatenate(
                    [
                        edges_ref[pl.ds((z * 16 + x * 4 + y) * COLS + side * HALF, HALF), :].astype(F32)
                        for z in range(LINES)
                        for y in range(LINES)
                    ],
                    axis=0,
                )
                for x in (2 * m, 2 * m + 1)
            )
            first, second = mix(a, b)
            both = jnp.concatenate(
                [first.reshape(16, HALF, LANES), second.reshape(16, HALF, LANES)], axis=1
            )
            ref[:, block(m)] = both.reshape(512, LANES).astype(BF16)


def triangle_kernel(left_ref, own_ref, other_ref, out_ref, right_ref):
    core_at = lax.axis_index("core")
    for m in range(LINES // 2):
        own, other = own_ref[:, block(m)].astype(F32), other_ref[:, block(m)].astype(F32)
        a = jnp.where(core_at == 0, own, other)
        b = jnp.where(core_at == 0, other, own)
        first, second = mix(a, b)
        right_ref[:, block(2 * m)] = first.astype(BF16)
        right_ref[:, block(2 * m + 1)] = second.astype(BF16)
    for m in range(LINES // 2):
        tri = dot(right_ref[...], left_ref[:, block(m)], 0, 0)
        tri = tri.reshape(32, HALF, LANES)
        a = tri[:, 0:LOW, :].reshape(256, LANES)
        b = tri[:, LOW:HALF, :].reshape(256, LANES)
        for x, part in zip((2 * m, 2 * m + 1), mix(a, b)):
            part = part.reshape(LINES, LINES, HALF, LANES)
            for z in range(LINES):
                out_ref[pl.ds((z * 4 + x) * 64, 64), :] = part[:, z].reshape(64, LANES).astype(BF16)


def middle_kernel(tri_ref, grad_hat_ref, out_ref, hats_ref):
    parts = tri_ref[...].astype(F32).reshape(OWN, 2 * LOW, LANES)
    tri = jnp.concatenate([parts[:, 0:LOW, :], parts[:, LOW : 2 * LOW, :]], axis=0)
    average = jnp.mean(tri, axis=0, keepdims=True)
    centred = tri - average
    inv = lax.rsqrt(jnp.mean(centred * centred, axis=0, keepdims=True) + 1e-05)
    hat = centred * inv
    hats_ref[...] = hat.reshape(CHANNELS * LOW, LANES)
    grad_hat = grad_hat_ref[...].reshape(CHANNELS, LOW, LANES)
    second = jnp.mean(grad_hat * hat, axis=0, keepdims=True)
    done = (grad_hat - hat * second) * inv
    both = jnp.concatenate([done[0:OWN], done[OWN:CHANNELS]], axis=1)
    out_ref[...] = both.astype(BF16).reshape(CHANNELS * LOW, LANES)


def late_kernel(hats_ref, slope_ref, w_gate_ref, w_out_ref, gain_ref, bias_ref, out_ref):
    gain = jnp.broadcast_to(gain_ref[...], (CHANNELS, LANES)).T
    bias = jnp.broadcast_to(bias_ref[...], (CHANNELS, LANES)).T
    for low in range(LOW):
        hat = hats_ref[pl.ds(low, CHANNELS, stride=LOW), :]
        mid_out = (hat * gain + bias).astype(BF16)
        proj_out = dot(mid_out, w_out_ref[...], 0, 0)
        gate_grad = (slope_ref[pl.ds(low * LANES, LANES), :] * proj_out).astype(BF16)
        out_ref[:, block(low)] = dot(w_gate_ref[...], gate_grad, 1, 1)


def grads_kernel(tri_grad_ref, left_ref, right_ref, left_grad_ref, own_ref, other_ref, grid_t):
    core_at = lax.axis_index("core")
    for m in range(LINES // 2):
        a, b = (
            jnp.concatenate(
                [
                    tri_grad_ref[pl.ds((z * 16 + x * 4 + y) * HALF, HALF), :].astype(F32)
                    for y in range(LINES)
                    for z in range(LINES)
                ],
                axis=0,
            )
            for x in (2 * m, 2 * m + 1)
        )
        first, second = mix(a, b)
        both = jnp.concatenate(
            [first.reshape(32, LOW, LANES), second.reshape(32, LOW, LANES)], axis=1
        )
        grid_t[:, block(m)] = both.reshape(32 * HALF, LANES).astype(BF16)
    for m in range(LINES // 2):
        a = dot(left_ref[...], grid_t[pl.ds(2 * m * LANES, LANES), :], 1, 1)
        b = dot(left_ref[...], grid_t[pl.ds((2 * m + 1) * LANES, LANES), :], 1, 1)
        first, second = mix(a, b)
        own_ref[:, block(m)] = jnp.where(core_at == 0, first, second)
        other_ref[:, block(m)] = jnp.where(core_at == 0, second, first).astype(BF16)
    for m in range(LINES // 2):
        left_grad_ref[:, block(m)] = dot(right_ref[...], grid_t[:, block(m)], 1, 0)


def join_kernel(left_grad_ref, own_ref, other_ref, out_ref):
    for m in range(LINES // 2):
        left_grad = left_grad_ref[:, block(m)]
        right_grad = own_ref[:, block(m)] + other_ref[:, block(m)].astype(F32)
        sides = []
        for grad in (left_grad, right_grad):
            grad = grad.reshape(32, HALF, LANES)
            a = grad[:, 0:LOW, :].reshape(256, LANES)
            b = grad[:, LOW:HALF, :].reshape(256, LANES)
            sides.append([part.reshape(32, LOW, LANES) for part in mix(a, b)])
        for at, x in enumerate((2 * m, 2 * m + 1)):
            both = jnp.concatenate([sides[0][at], sides[1][at]], axis=1)
            both = both.astype(BF16).reshape(512, LANES)
            for z in range(LINES):
                out_ref[pl.ds((z * 4 + x) * LANES, LANES), :] = both[z * LANES : (z + 1) * LANES]


def final_kernel(
    grads_ref, factor_ref, part_ref, normed_ref, inv_ref, w_proj_ref, tall_gain_ref, out_ref,
    grads, proj_grad, result,
):
    grads[...] = grads_ref[...].astype(F32)
    for low in range(LOW):
        for side in range(2):
            grad = jnp.concatenate(
                [
                    grads[pl.ds(slab * HALF + side * LOW + low, OWN, stride=2 * HALF), :]
                    for slab in range(2)
                ],
                axis=0,
            )
            for at in (side * 256, side * 256 + 128):
                factor = factor_ref[at : at + 128, block(low)].astype(F32)
                proj_grad[at : at + 128, block(low)] = (grad * factor).astype(BF16)
    gain = tall_gain_ref[...]
    for low in range(LOW):
        x_grad = dot(w_proj_ref[...], proj_grad[:, block(low)], 1, 0) + part_ref[:, block(low)]
        normed = normed_ref[:, block(low)]
        in_hat = x_grad * gain
        first = jnp.mean(in_hat, axis=0, keepdims=True)
        second = jnp.mean(in_hat * normed, axis=0, keepdims=True)
        done = ((in_hat - first - normed * second) * inv_ref[:, block(low)]).T
        result[pl.ds(low, ROWS, stride=HALF), :] = done[0:ROWS, :]
        result[pl.ds(low + LOW, ROWS, stride=HALF), :] = done[ROWS:LANES, :]
    out_ref[...] = result[...].reshape(ROWS, HALF, LANES).astype(BF16)


SMEM = pl.BlockSpec(memory_space=pltpu.SMEM)
VMEM = pl.BlockSpec(memory_space=pltpu.VMEM)


def call(kernel, outs, scratch, args, name, smem=0, cost=None, room=24):
    single = not isinstance(outs, list)
    return pl.pallas_call(
        kernel,
        out_shape=outs,
        in_specs=[SMEM] * smem + [VMEM] * (len(args) - smem),
        out_specs=VMEM if single else [VMEM] * len(outs),
        scratch_shapes=scratch,
        compiler_params=pltpu.CompilerParams(vmem_limit_bytes=room * 1024 * 1024),
        cost_estimate=cost,
        name=name,
    )(*args)


def shape(dims, kind):
    return jax.ShapeDtypeStruct(dims, kind)


def exchange(flat, axes):
    pieces = lax.axis_size(axes)
    cut = flat.reshape(pieces, flat.shape[0] // pieces, LANES)
    return lax.all_to_all(cut, axes, 0, 0, tiled=True).reshape(flat.shape)


def swap(x):
    return lax.ppermute(x, "core", [(0, 1), (1, 0)])


def on_device(
    pair_act, out_grad, pair_mask, chain_starts, in_gain, in_bias, w_proj, w_gate, w_out, mid_gain, mid_bias
):
    in_gain, in_bias, mid_gain, mid_bias = (
        v.reshape(1, LANES) for v in (in_gain, in_bias, mid_gain, mid_bias)
    )
    edge_rows = OWN * COLS
    tri_rows = CHANNELS * LOW
    edges, x_in, keep = call(
        edges_kernel,
        [shape((edge_rows, LANES), BF16), shape((POINTS, LANES), BF16), shape((LOW, LANES), F32)],
        [
            pltpu.VMEM((2 * POINTS, LANES), F32),
            pltpu.VMEM((COLS, LANES), F32),
            pltpu.VMEM((2 * POINTS, LANES), BF16),
            pltpu.VMEM((256, 2 * POINTS), F32),
            pltpu.VMEM((edge_rows, LANES), F32),
        ],
        (chain_starts, pair_act, pair_mask.T, in_gain, in_bias, w_proj),
        "edges",
        smem=1,
        room=63,
    )
    edges = exchange(edges, NEAR)
    slope, grad_hat, factor, normed, inv, tall_gain = call(
        ahead_kernel,
        [
            shape((POINTS, LANES), F32),
            shape((tri_rows, LANES), F32),
            shape((512, POINTS), BF16),
            shape((LANES, POINTS), F32),
            shape((1, POINTS), F32),
            shape((LANES, LANES), F32),
        ],
        [pltpu.VMEM((POINTS, LANES), F32), pltpu.VMEM((512, POINTS), F32)],
        (pair_act, out_grad, x_in, keep, w_proj, w_gate, w_out, mid_gain, in_gain),
        "ahead",
        cost=pl.CostEstimate(flops=300_000_000, bytes_accessed=6_000_000, transcendentals=700_000),
    )
    edges, slope, grad_hat, factor, normed, inv, tall_gain = lax.optimization_barrier(
        (edges, slope, grad_hat, factor, normed, inv, tall_gain)
    )
    left, own = call(
        sort_kernel, [shape((512, 256), BF16), shape((512, 256), BF16)], [], (edges,), "sort"
    )
    tri, right = call(
        triangle_kernel,
        [shape((tri_rows, LANES), BF16), shape((512, 512), BF16)],
        [],
        (left, own, swap(own)),
        "triangle",
    )
    tri = exchange(tri, FAR)
    tri_grad, hats = call(
        middle_kernel,
        [shape((tri_rows, LANES), BF16), shape((tri_rows, LANES), F32)],
        [],
        (tri, grad_hat),
        "middle",
    )
    tri_grad = exchange(tri_grad, FAR)
    left_grad, own, other = call(
        grads_kernel,
        [shape((512, 256), F32), shape((512, 256), F32), shape((512, 256), BF16)],
        [pltpu.VMEM((512, 256), BF16)],
        (tri_grad, left, right),
        "grads",
    )
    other, hats = lax.optimization_barrier((other, hats))
    swapped = swap(other)
    part = call(
        late_kernel,
        shape((LANES, POINTS), F32),
        [],
        (hats, slope, w_gate, w_out, mid_gain, mid_bias),
        "late",
        cost=pl.CostEstimate(flops=70_000_000, bytes_accessed=2_000_000, transcendentals=0),
    )
    swapped, part = lax.optimization_barrier((swapped, part))
    grads = call(
        join_kernel, shape((CHANNELS * HALF, LANES), BF16), [], (left_grad, own, swapped), "join"
    )
    grads = exchange(grads, FAR)
    result = call(
        final_kernel,
        shape((ROWS, HALF, LANES), BF16),
        [
            pltpu.VMEM((CHANNELS * HALF, LANES), F32),
            pltpu.VMEM((512, POINTS), BF16),
            pltpu.VMEM((POINTS, LANES), F32),
        ],
        (grads, factor, part, normed, inv, w_proj, tall_gain),
        "final",
    )
    return result.reshape(ROWS, 1, 1, HALF, LANES)


def solution(mesh):
    fine = Mesh(mesh.devices.reshape(2, LINES, 2, 4, 4), ("slab", "x", "core", "y", "z"))
    row, col = ("x", "core"), ("y", "z")
    in_specs = (P(row, col, None), P(row, col, None), P(row, col)) + (P(),) * 8
    out_specs = P(row, col, "slab", None, None)
    return jax.shard_map(
        on_device, mesh=fine, in_specs=in_specs, out_specs=out_specs, check_vma=False
    )
```

time: 118 us -> 112 us (0.949)
  blocking collectives: 99.4 us -> 70.9 us
  starting transfers between devices: 0.19 us -> 12.6 us
  waiting for transfers between devices: 3.04 us -> 11.3 us
  Pallas kernels: 10.5 us -> 11.8 us
    all_to_all x4 -> x3, blocking collectives: 99.4 us -> 70.9 us  [exchange(): return lax.all_to_all(cut, axes, 0, 0, tiled=True).reshape(flat.shape)]
    all_to_all x0 -> x1, starting transfers between devices: none -> 12.2 us  [exchange(): return lax.all_to_all(cut, axes, 0, 0, tiled=True).reshape(flat.shape)]
    all_to_all x0 -> x1, waiting for transfers between devices: none -> 9.63 us  [exchange(): return lax.all_to_all(cut, axes, 0, 0, tiled=True).reshape(flat.shape)]
    ppermute x2, waiting for transfers between devices: 3.04 us -> 1.62 us  [swap(): return lax.ppermute(x, 'core', [(0, 1), (1, 0)])]
    pallas_call x7 -> x9, Pallas kernels: 10.5 us -> 11.8 us  [call(): pl.pallas_call(kernel, out_shape=outs, in_specs=[SMEM] * smem + [VMEM] *...]
    unnamed x25 -> x36, local copies, waits for them, and re-layouts: 4.09 us -> 4.78 us
  transfers between devices with their start and end apart: 2 -> 3, of which waited for: 2 -> 3; matrix products, arithmetic and copies ran while one was open for 0% -> 0% of each run, Pallas kernels for 0% -> 2%
where the time goes in v3:
time: 112 us; the launch traced here: 111 us
  blocking collectives  70.9 us (63%)
  starting transfers between devices  12.6 us (11%)
  Pallas kernels  11.8 us (11%)
  waiting for transfers between devices  11.3 us (10%)
  local copies, waits for them, and re-layouts  4.78 us (4%)
    all_to_all x3, blocking collectives, exchange(): return lax.all_to_all(cut, axes, 0, 0, tiled=True).reshape(flat.shape)  70.9 us
    all_to_all x1, starting transfers between devices, exchange(): return lax.all_to_all(cut, axes, 0, 0, tiled=True).reshape(flat.shape)  12.2 us
    pallas_call x9, Pallas kernels, call(): pl.pallas_call(kernel, out_shape=outs, in_specs=[SMEM] * smem + [VMEM] *...  11.8 us
    all_to_all x1, waiting for transfers between devices, exchange(): return lax.all_to_all(cut, axes, 0, 0, tiled=True).reshape(flat.shape)  9.63 us
    unnamed x36, local copies, waits for them, and re-layouts  4.78 us
  transfers between devices with their start and end apart: 3, of which 3 were waited for; matrix products, arithmetic and copies ran while one was open for 0% of the time, Pallas kernels for 2%

profile of v3, /device:TPU:2, one launch (start us, length us, event | category | flops | bytes accessed | tf_op | source)
XLA Modules:
  0.0 111.5 jit_solution(6809941085572531714)
XLA Ops:
  0.0 4.2 %edges.1 = (bf16[2048,128]{1,0:T(8,128)(2,1)}, bf16[1024,128]{1,0:T(8,128)(2,1)}, f32[8,128]{1,0:T(8,128)}) custom-call(s32[6]{0:T(128)} %starts_ref.1, bf16[64,32,128]{2,1,0:T(8,128)(2,1)} %act_ref.3, s32[32,64]{1,0:T(8,128)} %bitcast.29, f32[1,128]{1,0:T(1,128)} %bitcast.23, f32[1,128]{1,0:T(1,128)} %bitcast.30, bf16[128,512]{1,0:T(8,128)(2,1)} %w_proj_ref.3), custom_call_target="tpu_custom_call" | custom-call | tf_op jit(solution)/shard_map/edges/pallas_call | solution.py:297
  4.2 12.2 %all-to-all-start = ((bf16[64,32,128]{2,1,0:T(8,128)(2,1)}), bf16[64,32,128]{2,1,0:T(8,128)(2,1)S(1)}, u32[]{:S(2)}, u32[]{:S(2)}) async-start(bf16[64,32,128]{2,1,0:T(8,128)(2,1)} %bitcast.28), calls=%async_computation | async-start | bytes 1048576 | tf_op jit(solution)/shard_map/all_to_all | solution.py:316
  16.4 0.0 copy-start.14
  16.4 0.0 copy-start.15
  16.4 0.0 copy-start.16
  16.5 0.6 copy-done.14
  17.1 0.0 copy-done.16
  17.1 0.8 copy-done.8
  17.9 0.8 copy-done.10
  18.6 1.7 %ahead.1 = (f32[1024,128]{1,0:T(8,128)S(1)}, f32[1024,128]{1,0:T(8,128)S(1)}, bf16[512,1024]{1,0:T(8,128)(2,1)S(1)}, f32[128,1024]{1,0:T(8,128)S(1)}, f32[1,1024]{1,0:T(1,128)S(1)}, /*index=5*/f32[128,128]{1,0:T(8,128)S(1)}) custom-call(bf16[64,32,128]{2,1,0:T(8,128)(2,1)S(1)} %copy-done, bf16[64,32,128]{2,1,0:T(8,128)(2,1)S(1)} %copy-done.2, ...), custom_call_target="tpu_custom_call" | custom-call | flops 300000000 | bytes 6000000 | tf_op jit(solution)/shard_map/ahead/pallas_call | solution.py:297
  20.3 0.8 copy-done.3
  21.1 0.8 copy-done.5
  21.9 0.6 copy-done.12
  22.6 9.6 %all-to-all-done = bf16[64,32,128]{2,1,0:T(8,128)(2,1)S(1)} async-done(((bf16[64,32,128]{2,1,0:T(8,128)(2,1)}), bf16[64,32,128]{2,1,0:T(8,128)(2,1)S(1)}, u32[]{:S(2)}, u32[]{:S(2)}) %all-to-all-start) | async-done | bytes 524320 | tf_op jit(solution)/shard_map/all_to_all | solution.py:316
  32.2 0.2 sort.1
  32.4 0.1 collective-permute-start
  32.5 1.5 %collective-permute-done.other_ref = bf16[512,256]{1,0:T(8,128)(2,1)S(1)} collective-permute-done((bf16[512,256]{1,0:T(8,128)(2,1)S(1)}, bf16[512,256]{1,0:T(8,128)(2,1)S(1)}, u32[]{:S(2)}, u32[]{:S(2)}) %collective-permute-start) | collective-permute-done | bytes 262176 | tf_op jit(solution)/shard_map/ppermute | solution.py:320
  34.0 0.8 triangle.1
  34.9 24.6 %all_to_all.20 = bf16[128,8,128]{2,1,0:T(8,128)(2,1)S(1)} all-to-all(bf16[128,8,128]{2,1,0:T(8,128)(2,1)S(1)} %bitcast.21), channel_id=1, replica_groups=mesh['slab'=2,'x'=4,'core'=2,'y'=4,'z'=4] {'z','x','y','slab'}, dimensions={0} | all-to-all | bytes 524288 | tf_op jit(solution)/shard_map/all_to_all | solution.py:316
  59.5 0.5 middle.1
  60.0 19.8 %all_to_all.21 = bf16[128,8,128]{2,1,0:T(8,128)(2,1)S(1)} all-to-all(bf16[128,8,128]{2,1,0:T(8,128)(2,1)S(1)} %bitcast.22), channel_id=1, replica_groups=mesh['slab'=2,'x'=4,'core'=2,'y'=4,'z'=4] {'z','x','y','slab'}, dimensions={0} | all-to-all | bytes 524288 | tf_op jit(solution)/shard_map/all_to_all | solution.py:316
  79.9 0.8 grads.1
  80.7 0.0 copy-start.17
  80.7 0.3 collective-permute-start.1
  81.0 0.4 copy-done.17
  81.4 1.0 late.1.part_ref
  82.4 0.1 collective-permute-done.1.other_ref
  82.5 0.2 join.1
  82.8 0.0 copy-start.13
  82.8 26.4 %all_to_all.22 = bf16[128,16,128]{2,1,0:T(8,128)(2,1)S(1)} all-to-all(bf16[128,16,128]{2,1,0:T(8,128)(2,1)S(1)} %bitcast.16), channel_id=1, replica_groups=mesh['slab'=2,'x'=4,'core'=2,'y'=4,'z'=4] {'z','x','y','slab'}, dimensions={0} | all-to-all | bytes 1048576 | tf_op jit(solution)/shard_map/all_to_all | solution.py:316
  109.2 0.0 copy-done.13
  109.2 2.3 %final.1 = bf16[64,16,128]{2,1,0:T(8,128)(2,1)} custom-call(bf16[2048,128]{1,0:T(8,128)(2,1)S(1)} %bitcast.18, bf16[512,1024]{1,0:T(8,128)(2,1)S(1)} %get-tuple-element.58.factor_ref, f32[128,1024]{1,0:T(8,128)S(1)} %late.1.part_ref, f32[128,1024]{1,0:T(8,128)S(1)} %copy-done.4, f32[1,1024]{1,0:T(1,128)S(1)} %get-tuple-element.61.inv_ref, ...), custom_call_target="tpu_custom_call" | custom-call | tf_op jit(solution)/shard_map/final/pallas_call | solution.py:297
  (22 shorter events, 0.0 us)
Async XLA Ops:
  0.0 16.5 %copy-start.2 = (bf16[64,32,128]{2,1,0:T(8,128)(2,1)S(1)}, bf16[64,32,128]{2,1,0:T(8,128)(2,1)}, u32[]{:S(2)}) copy-start(bf16[64,32,128]{2,1,0:T(8,128)(2,1)} %grad_ref.1) | copy-start | bytes 1572868
  4.2 12.3 %copy-start = (bf16[64,32,128]{2,1,0:T(8,128)(2,1)S(1)}, bf16[64,32,128]{2,1,0:T(8,128)(2,1)}, u32[]{:S(2)}) copy-start(bf16[64,32,128]{2,1,0:T(8,128)(2,1)} %act_ref.3) | copy-start | bytes 1572868
  4.2 12.3 %copy-start.1 = (bf16[128,512]{1,0:T(8,128)(2,1)S(1)}, bf16[128,512]{1,0:T(8,128)(2,1)}, u32[]{:S(2)}) copy-start(bf16[128,512]{1,0:T(8,128)(2,1)} %w_proj_ref.3) | copy-start | bytes 393220
  4.2 12.3 %copy-start.7 = (bf16[1024,128]{1,0:T(8,128)(2,1)S(1)}, bf16[1024,128]{1,0:T(8,128)(2,1)}, u32[]{:S(2)}) copy-start(bf16[1024,128]{1,0:T(8,128)(2,1)} %get-tuple-element.35.x_ref) | copy-start | bytes 786436
  4.2 28.0 %all-to-all-start = ((bf16[64,32,128]{2,1,0:T(8,128)(2,1)}), bf16[64,32,128]{2,1,0:T(8,128)(2,1)S(1)}, u32[]{:S(2)}, u32[]{:S(2)}) async-start(bf16[64,32,128]{2,1,0:T(8,128)(2,1)} %bitcast.28), calls=%async_computation | async-start | bytes 1048576 | tf_op jit(solution)/shard_map/all_to_all | solution.py:316
  16.4 0.7 copy-start.14
  16.4 0.7 copy-start.15
  16.4 0.7 copy-start.16
  17.1 0.8 copy-start.8
  17.9 0.8 copy-start.10
  20.3 0.8 copy-start.3
  21.1 0.8 copy-start.5
  21.9 0.6 copy-start.12
  32.4 1.6 %collective-permute-start = (bf16[512,256]{1,0:T(8,128)(2,1)S(1)}, bf16[512,256]{1,0:T(8,128)(2,1)S(1)}, u32[]{:S(2)}, u32[]{:S(2)}) collective-permute-start(bf16[512,256]{1,0:T(8,128)(2,1)S(1)} %get-tuple-element.45.own_ref), channel_id=1, source_target_pairs={{0,16},{16,0},{1,17},{17,1},{2,18},{18,2},{3,19},{19,3},{4,20},{20... | collective-permute-start | bytes 786440 | tf_op jit(solution)/shard_map/ppermute | solution.py:320
  79.9 1.1 copy-start.6
  79.9 1.1 %copy-start.9 = (bf16[128,128]{1,0:T(8,128)(2,1)S(1)}, bf16[128,128]{1,0:T(8,128)(2,1)}, u32[]{:S(2)}) copy-start(bf16[128,128]{1,0:T(8,128)(2,1)} %w_gate_ref.3) | copy-start | bytes 98308
  79.9 1.1 %copy-start.11 = (bf16[128,128]{1,0:T(8,128)(2,1)S(1)}, bf16[128,128]{1,0:T(8,128)(2,1)}, u32[]{:S(2)}) copy-start(bf16[128,128]{1,0:T(8,128)(2,1)} %w_out_ref.3) | copy-start | bytes 98308
  80.7 0.7 copy-start.17
  80.7 1.8 %collective-permute-start.1 = (bf16[512,256]{1,0:T(8,128)(2,1)S(1)}, bf16[512,256]{1,0:T(8,128)(2,1)S(1)}, u32[]{:S(2)}, u32[]{:S(2)}) collective-permute-start(bf16[512,256]{1,0:T(8,128)(2,1)S(1)} %get-tuple-element.54), channel_id=1, source_target_pairs={{0,16},{16,0},{1,17},{17,1},{2,18},{18,2},{3,19},{19,3},{4,20},{20... | collective-permute-start | bytes 786440 | tf_op jit(solution)/shard_map/ppermute | solution.py:320
  82.8 26.4 %copy-start.4 = (f32[128,1024]{1,0:T(8,128)S(1)}, f32[128,1024]{1,0:T(8,128)}, u32[]{:S(2)}) copy-start(f32[128,1024]{1,0:T(8,128)} %copy-done.3) | copy-start | bytes 1572868
  82.8 26.4 %copy-start.13 = (f32[128,128]{1,0:T(8,128)S(1)}, f32[128,128]{1,0:T(8,128)}, u32[]{:S(2)}) copy-start(f32[128,128]{1,0:T(8,128)} %copy-done.12) | copy-start | bytes 196612

commit v4 on v3

--- a/solution.py
+++ b/solution.py
@@ -16,6 +16,8 @@
 CHANNELS = 128
 OWN = CHANNELS // 2
 POINTS = ROWS * HALF
+PITCH = COLS + 8
+STEP = HALF + 8
 LINES = 4
 NEAR = ("z", "x", "y")
 FAR = ("z", "x", "y", "slab")
@@ -94,31 +96,35 @@
         first, second = mix(w_ref[:, block(at)].astype(F32), w_ref[:, block(at + 2)].astype(F32))
         own.append(jnp.where(slab_at == 0, first, second).astype(BF16))
     w_own = jnp.concatenate(own, axis=1)
-    tile[...] = act_ref[...].astype(F32).reshape(ROWS * COLS, LANES)
+    values = act_ref[...].astype(F32)
+    spare = jnp.zeros((ROWS, PITCH - COLS, LANES), F32)
+    tile[...] = jnp.concatenate([values, spare], axis=1).reshape(ROWS * PITCH, LANES)
     for k in range(COLS):
-        normed, _ = normalize(column(tile, k, COLS))
+        normed, _ = normalize(column(tile, k, PITCH))
         at = (k % HALF * 2 + k // HALF) * ROWS
         x_all[pl.ds(at, ROWS), :] = (normed * gain_ref[...] + bias_ref[...]).astype(BF16)
     projected[...] = dot(w_own, x_all[...], 0, 1)
     for k in range(HALF):
         both = jax.nn.sigmoid(projected[0:128, block(k)]) * projected[128:256, block(k)]
         both = both * halves(kept[k : k + 1, :], kept[k + HALF : k + HALF + 1, :])
-        turned[pl.ds(k, OWN, stride=COLS), :] = both[0:OWN, :]
-        turned[pl.ds(k + HALF, OWN, stride=COLS), :] = both[OWN:CHANNELS, :]
-    edges_ref[...] = turned[...].astype(BF16)
+        turned[pl.ds(k, OWN, stride=PITCH), :] = both[0:OWN, :]
+        turned[pl.ds(k + HALF, OWN, stride=PITCH), :] = both[OWN:CHANNELS, :]
+    done = turned[...].reshape(OWN, PITCH, LANES)[:, 0:COLS, :]
+    edges_ref[...] = done.reshape(OWN * COLS, LANES).astype(BF16)
     for k in range(HALF):
         mine = pl.multiple_of(2 * k * ROWS + slab_at * ROWS, ROWS)
         x_ref[pl.ds(place(k), ROWS), :] = x_all[pl.ds(mine, ROWS), :]
 
 
 def ahead_kernel(
-    act_ref, grad_ref, x_ref, keep_ref, w_proj_ref, w_gate_ref, w_out_ref, gain_ref, in_gain_ref,
-    slope_ref, grad_hat_ref, factor_ref, normed_ref, inv_ref, tall_gain_ref, tile, projected,
+    act_ref, grad_ref, x_ref, keep_ref, w_proj_ref, w_gate_ref, w_out_ref, gain_ref, bias_ref, in_gain_ref,
+    slope_ref, grad_hat_ref, factor_ref, normed_ref, inv_ref, tall_ref, tile, projected,
 ):
-    tall_gain_ref[...] = jnp.broadcast_to(in_gain_ref[...], (LANES, LANES)).T
+    for at, ref in enumerate((in_gain_ref, gain_ref, bias_ref)):
+        tall_ref[at] = jnp.broadcast_to(ref[...], (LANES, LANES)).T
     slab_at = lax.axis_index("slab")
     load_half(grad_ref, slab_at, tile)
-    gain = jnp.broadcast_to(gain_ref[...], (CHANNELS, LANES)).T
+    gain = tall_ref[1]
     for low in range(LOW):
         here = pl.ds(low * LANES, LANES)
         gate = jax.nn.sigmoid(dot(x_ref[here, :], w_gate_ref[...], 1, 0))
@@ -201,9 +207,11 @@
     out_ref[...] = both.astype(BF16).reshape(CHANNELS * LOW, LANES)
 
 
-def late_kernel(hats_ref, slope_ref, w_gate_ref, w_out_ref, gain_ref, bias_ref, out_ref):
-    gain = jnp.broadcast_to(gain_ref[...], (CHANNELS, LANES)).T
-    bias = jnp.broadcast_to(bias_ref[...], (CHANNELS, LANES)).T
+def late_kernel(
+    hats_ref, slope_ref, w_gate_ref, w_out_ref, tall_ref, right_ref, grid_t_ref, out_ref, left_grad_ref
+):
+    left_grad_ref[...] = dot(right_ref[...], grid_t_ref[...], 1, 0)
+    gain, bias = tall_ref[1], tall_ref[2]
     for low in range(LOW):
         hat = hats_ref[pl.ds(low, CHANNELS, stride=LOW), :]
         mid_out = (hat * gain + bias).astype(BF16)
@@ -212,7 +220,7 @@
         out_ref[:, block(low)] = dot(w_gate_ref[...], gate_grad, 1, 1)
 
 
-def grads_kernel(tri_grad_ref, left_ref, right_ref, left_grad_ref, own_ref, other_ref, grid_t):
+def grads_kernel(tri_grad_ref, left_ref, own_ref, other_ref, grid_t):
     core_at = lax.axis_index("core")
     for m in range(LINES // 2):
         a, b = (
@@ -237,8 +245,6 @@
         first, second = mix(a, b)
         own_ref[:, block(m)] = jnp.where(core_at == 0, first, second)
         other_ref[:, block(m)] = jnp.where(core_at == 0, second, first).astype(BF16)
-    for m in range(LINES // 2):
-        left_grad_ref[:, block(m)] = dot(right_ref[...], grid_t[:, block(m)], 1, 0)
 
 
 def join_kernel(left_grad_ref, own_ref, other_ref, out_ref):
@@ -259,15 +265,19 @@
 
 
 def final_kernel(
-    grads_ref, factor_ref, part_ref, normed_ref, inv_ref, w_proj_ref, tall_gain_ref, out_ref,
+    grads_ref, factor_ref, part_ref, normed_ref, inv_ref, w_proj_ref, tall_ref, out_ref,
     grads, proj_grad, result,
 ):
-    grads[...] = grads_ref[...].astype(F32)
+    got = grads_ref[...].astype(F32).reshape(OWN, 2, HALF, LANES)
+    spare = jnp.zeros((OWN, STEP - HALF, LANES), F32)
+    for slab in range(2):
+        part = jnp.concatenate([got[:, slab], spare], axis=1)
+        grads[pl.ds(slab * OWN * STEP, OWN * STEP), :] = part.reshape(OWN * STEP, LANES)
     for low in range(LOW):
         for side in range(2):
             grad = jnp.concatenate(
                 [
-                    grads[pl.ds(slab * HALF + side * LOW + low, OWN, stride=2 * HALF), :]
+                    grads[pl.ds(slab * OWN * STEP + side * LOW + low, OWN, stride=STEP), :]
                     for slab in range(2)
                 ],
                 axis=0,
@@ -275,7 +285,7 @@
             for at in (side * 256, side * 256 + 128):
                 factor = factor_ref[at : at + 128, block(low)].astype(F32)
                 proj_grad[at : at + 128, block(low)] = (grad * factor).astype(BF16)
-    gain = tall_gain_ref[...]
+    gain = tall_ref[0]
     for low in range(LOW):
         x_grad = dot(w_proj_ref[...], proj_grad[:, block(low)], 1, 0) + part_ref[:, block(low)]
         normed = normed_ref[:, block(low)]
@@ -283,9 +293,9 @@
         first = jnp.mean(in_hat, axis=0, keepdims=True)
         second = jnp.mean(in_hat * normed, axis=0, keepdims=True)
         done = ((in_hat - first - normed * second) * inv_ref[:, block(low)]).T
-        result[pl.ds(low, ROWS, stride=HALF), :] = done[0:ROWS, :]
-        result[pl.ds(low + LOW, ROWS, stride=HALF), :] = done[ROWS:LANES, :]
-    out_ref[...] = result[...].reshape(ROWS, HALF, LANES).astype(BF16)
+        result[pl.ds(low, ROWS, stride=STEP), :] = done[0:ROWS, :]
+        result[pl.ds(low + LOW, ROWS, stride=STEP), :] = done[ROWS:LANES, :]
+    out_ref[...] = result[...].reshape(ROWS, STEP, LANES)[:, 0:HALF, :].astype(BF16)
 
 
 SMEM = pl.BlockSpec(memory_space=pltpu.SMEM)
@@ -332,11 +342,11 @@
         edges_kernel,
         [shape((edge_rows, LANES), BF16), shape((POINTS, LANES), BF16), shape((LOW, LANES), F32)],
         [
-            pltpu.VMEM((2 * POINTS, LANES), F32),
+            pltpu.VMEM((ROWS * PITCH, LANES), F32),
             pltpu.VMEM((COLS, LANES), F32),
             pltpu.VMEM((2 * POINTS, LANES), BF16),
             pltpu.VMEM((256, 2 * POINTS), F32),
-            pltpu.VMEM((edge_rows, LANES), F32),
+            pltpu.VMEM((OWN * PITCH, LANES), F32),
         ],
         (chain_starts, pair_act, pair_mask.T, in_gain, in_bias, w_proj),
         "edges",
@@ -344,7 +354,7 @@
         room=63,
     )
     edges = exchange(edges, NEAR)
-    slope, grad_hat, factor, normed, inv, tall_gain = call(
+    slope, grad_hat, factor, normed, inv, tall = call(
         ahead_kernel,
         [
             shape((POINTS, LANES), F32),
@@ -352,15 +362,15 @@
             shape((512, POINTS), BF16),
             shape((LANES, POINTS), F32),
             shape((1, POINTS), F32),
-            shape((LANES, LANES), F32),
+            shape((3, LANES, LANES), F32),
         ],
         [pltpu.VMEM((POINTS, LANES), F32), pltpu.VMEM((512, POINTS), F32)],
-        (pair_act, out_grad, x_in, keep, w_proj, w_gate, w_out, mid_gain, in_gain),
+        (pair_act, out_grad, x_in, keep, w_proj, w_gate, w_out, mid_gain, mid_bias, in_gain),
         "ahead",
         cost=pl.CostEstimate(flops=300_000_000, bytes_accessed=6_000_000, transcendentals=700_000),
     )
-    edges, slope, grad_hat, factor, normed, inv, tall_gain = lax.optimization_barrier(
-        (edges, slope, grad_hat, factor, normed, inv, tall_gain)
+    edges, slope, grad_hat, factor, normed, inv, tall = lax.optimization_barrier(
+        (edges, slope, grad_hat, factor, normed, inv, tall)
     )
     left, own = call(
         sort_kernel, [shape((512, 256), BF16), shape((512, 256), BF16)], [], (edges,), "sort"
@@ -381,24 +391,24 @@
         "middle",
     )
     tri_grad = exchange(tri_grad, FAR)
-    left_grad, own, other = call(
+    own, other, grid_t = call(
         grads_kernel,
-        [shape((512, 256), F32), shape((512, 256), F32), shape((512, 256), BF16)],
-        [pltpu.VMEM((512, 256), BF16)],
-        (tri_grad, left, right),
+        [shape((512, 256), F32), shape((512, 256), BF16), shape((512, 256), BF16)],
+        [],
+        (tri_grad, left),
         "grads",
     )
-    other, hats = lax.optimization_barrier((other, hats))
+    other, hats, grid_t = lax.optimization_barrier((other, hats, grid_t))
     swapped = swap(other)
-    part = call(
+    part, left_grad = call(
         late_kernel,
-        shape((LANES, POINTS), F32),
+        [shape((LANES, POINTS), F32), shape((512, 256), F32)],
         [],
-        (hats, slope, w_gate, w_out, mid_gain, mid_bias),
+        (hats, slope, w_gate, w_out, tall, right, grid_t),
         "late",
-        cost=pl.CostEstimate(flops=70_000_000, bytes_accessed=2_000_000, transcendentals=0),
-    )
-    swapped, part = lax.optimization_barrier((swapped, part))
+        cost=pl.CostEstimate(flops=210_000_000, bytes_accessed=3_000_000, transcendentals=0),
+    )
+    swapped, part, left_grad = lax.optimization_barrier((swapped, part, left_grad))
     grads = call(
         join_kernel, shape((CHANNELS * HALF, LANES), BF16), [], (left_grad, own, swapped), "join"
     )
@@ -407,11 +417,11 @@
         final_kernel,
         shape((ROWS, HALF, LANES), BF16),
         [
-            pltpu.VMEM((CHANNELS * HALF, LANES), F32),
+            pltpu.VMEM((CHANNELS * STEP, LANES), F32),
             pltpu.VMEM((512, POINTS), BF16),
-            pltpu.VMEM((POINTS, LANES), F32),
+            pltpu.VMEM((ROWS * STEP, LANES), F32),
         ],
-        (grads, factor, part, normed, inv, w_proj, tall_gain),
+        (grads, factor, part, normed, inv, w_proj, tall),
         "final",
     )
     return result.reshape(ROWS, 1, 1, HALF, LANES)

time: 112 us -> 111 us (level)
  local copies, waits for them, and re-layouts: 4.78 us -> 3.05 us
  waiting for transfers between devices: 11.3 us -> 12.6 us
    unnamed x36 -> x32, local copies, waits for them, and re-layouts: 4.78 us -> 3.05 us
    all_to_all x1, waiting for transfers between devices: 9.63 us -> 10.9 us  [exchange(): return lax.all_to_all(cut, axes, 0, 0, tiled=True).reshape(flat.shape)]
  transfers between devices with their start and end apart: 3 -> 3, of which waited for: 3 -> 3; matrix products, arithmetic and copies ran while one was open for 0% -> 0% of each run, Pallas kernels for 2% -> 3%
where the time goes in v4:
time: 111 us
  blocking collectives  71.4 us (64%)
  waiting for transfers between devices  12.6 us (11%)
  starting transfers between devices  12.4 us (11%)
  Pallas kernels  10.8 us (10%)
  local copies, waits for them, and re-layouts  3.05 us (3%)
    all_to_all x3, blocking collectives, exchange(): return lax.all_to_all(cut, axes, 0, 0, tiled=True).reshape(flat.shape)  71.4 us
    all_to_all x1, starting transfers between devices, exchange(): return lax.all_to_all(cut, axes, 0, 0, tiled=True).reshape(flat.shape)  12.2 us
    all_to_all x1, waiting for transfers between devices, exchange(): return lax.all_to_all(cut, axes, 0, 0, tiled=True).reshape(flat.shape)  10.9 us
    pallas_call x9, Pallas kernels, call(): pl.pallas_call(kernel, out_shape=outs, in_specs=[SMEM] * smem + [VMEM] *...  10.8 us
    unnamed x32, local copies, waits for them, and re-layouts  3.05 us
  transfers between devices with their start and end apart: 3, of which 3 were waited for; matrix products, arithmetic and copies ran while one was open for 0% of the time, Pallas kernels for 3%

profile of v4, /device:TPU:2, one launch (start us, length us, event | category | flops | bytes accessed | tf_op | source)
XLA Modules:
  0.0 110.5 jit_solution(6117270569893761928)
XLA Ops:
  0.0 3.5 %edges.1 = (bf16[2048,128]{1,0:T(8,128)(2,1)}, bf16[1024,128]{1,0:T(8,128)(2,1)}, f32[8,128]{1,0:T(8,128)}) custom-call(s32[6]{0:T(128)} %starts_ref.1, bf16[64,32,128]{2,1,0:T(8,128)(2,1)} %act_ref.3, s32[32,64]{1,0:T(8,128)} %bitcast.28, f32[1,128]{1,0:T(1,128)} %bitcast.23, f32[1,128]{1,0:T(1,128)} %bitcast.29, bf16[128,512]{1,0:T(8,128)(2,1)} %w_proj_ref.3), custom_call_target="tpu_custom_call" | custom-call | tf_op jit(solution)/shard_map/edges/pallas_call | solution.py:307
  3.5 0.0 copy-start.10
  3.5 0.0 copy-start.11
  3.6 12.2 %all-to-all-start = ((bf16[64,32,128]{2,1,0:T(8,128)(2,1)}), bf16[64,32,128]{2,1,0:T(8,128)(2,1)S(1)}, u32[]{:S(2)}, u32[]{:S(2)}) async-start(bf16[64,32,128]{2,1,0:T(8,128)(2,1)} %bitcast.27), calls=%async_computation | async-start | bytes 1048576 | tf_op jit(solution)/shard_map/all_to_all | solution.py:326
  15.8 0.0 copy-start.13
  15.8 0.0 copy-start.14
  15.8 0.0 copy-start.15
  15.9 0.6 copy-done.12
  16.5 0.0 copy-done.13
  16.5 0.0 copy-done.14
  16.5 0.0 copy-done.15
  16.5 1.7 %ahead.1 = (f32[1024,128]{1,0:T(8,128)S(1)}, f32[1024,128]{1,0:T(8,128)S(1)}, bf16[512,1024]{1,0:T(8,128)(2,1)S(1)}, f32[128,1024]{1,0:T(8,128)S(1)}, f32[1,1024]{1,0:T(1,128)S(1)}, /*index=5*/f32[3,128,128]{2,1,0:T(8,128)S(1)}) custom-call(bf16[64,32,128]{2,1,0:T(8,128)(2,1)S(1)} %copy-done, bf16[64,32,128]{2,1,0:T(8,128)(2,1)S(1)} %copy-done.2, ...), custom_call_target="tpu_custom_call" | custom-call | flops 300000000 | bytes 6000000 | tf_op jit(solution)/shard_map/ahead/pallas_call | solution.py:307
  18.2 0.8 copy-done.3
  19.0 0.8 copy-done.5
  19.8 0.8 copy-done.7
  20.6 10.9 %all-to-all-done = bf16[64,32,128]{2,1,0:T(8,128)(2,1)S(1)} async-done(((bf16[64,32,128]{2,1,0:T(8,128)(2,1)}), bf16[64,32,128]{2,1,0:T(8,128)(2,1)S(1)}, u32[]{:S(2)}, u32[]{:S(2)}) %all-to-all-start) | async-done | bytes 524320 | tf_op jit(solution)/shard_map/all_to_all | solution.py:326
  31.6 0.2 sort.1
  31.8 0.1 collective-permute-start
  31.9 1.5 %collective-permute-done.other_ref = bf16[512,256]{1,0:T(8,128)(2,1)S(1)} collective-permute-done((bf16[512,256]{1,0:T(8,128)(2,1)S(1)}, bf16[512,256]{1,0:T(8,128)(2,1)S(1)}, u32[]{:S(2)}, u32[]{:S(2)}) %collective-permute-start) | collective-permute-done | bytes 262176 | tf_op jit(solution)/shard_map/ppermute | solution.py:330
  33.4 0.8 triangle.1
  34.2 24.6 %all_to_all.20 = bf16[128,8,128]{2,1,0:T(8,128)(2,1)S(1)} all-to-all(bf16[128,8,128]{2,1,0:T(8,128)(2,1)S(1)} %bitcast.21), channel_id=1, replica_groups=mesh['slab'=2,'x'=4,'core'=2,'y'=4,'z'=4] {'z','x','y','slab'}, dimensions={0} | all-to-all | bytes 524288 | tf_op jit(solution)/shard_map/all_to_all | solution.py:326
  58.8 0.5 middle.1
  59.4 0.0 copy-start.8
  59.4 20.0 %all_to_all.21 = bf16[128,8,128]{2,1,0:T(8,128)(2,1)S(1)} all-to-all(bf16[128,8,128]{2,1,0:T(8,128)(2,1)S(1)} %bitcast.22), channel_id=1, replica_groups=mesh['slab'=2,'x'=4,'core'=2,'y'=4,'z'=4] {'z','x','y','slab'}, dimensions={0} | all-to-all | bytes 524288 | tf_op jit(solution)/shard_map/all_to_all | solution.py:326
  79.4 0.6 grads.1
  80.0 0.1 collective-permute-start.1
  80.1 1.4 %late.1 = (f32[128,1024]{1,0:T(8,128)S(1)}, f32[512,256]{1,0:T(8,128)S(1)}) custom-call(f32[1024,128]{1,0:T(8,128)S(1)} %get-tuple-element.57.hats_ref, f32[1024,128]{1,0:T(8,128)S(1)} %copy-done.8, bf16[128,128]{1,0:T(8,128)(2,1)S(1)} %copy-done.10, bf16[128,128]{1,0:T(8,128)(2,1)S(1)} %copy-done.11, f32[3,128,128]{2,1,0:T(8,128)S(1)} %get-tuple-element.59.tall_ref, ...), custom_call_target="tpu_custom_call" | custom-call | flops 210000000 | bytes 3000000 | tf_op jit(solution)/shard_map/late/pallas_call | solution.py:307
  81.5 0.1 collective-permute-done.1.other_ref
  81.6 0.2 join.1
  81.9 0.0 copy-start.4
  81.9 26.8 %all_to_all.22 = bf16[128,16,128]{2,1,0:T(8,128)(2,1)S(1)} all-to-all(bf16[128,16,128]{2,1,0:T(8,128)(2,1)S(1)} %bitcast.17), channel_id=1, replica_groups=mesh['slab'=2,'x'=4,'core'=2,'y'=4,'z'=4] {'z','x','y','slab'}, dimensions={0} | all-to-all | bytes 1048576 | tf_op jit(solution)/shard_map/all_to_all | solution.py:326
  108.7 1.8 %final.1 = bf16[64,16,128]{2,1,0:T(8,128)(2,1)} custom-call(bf16[2048,128]{1,0:T(8,128)(2,1)S(1)} %bitcast.16, bf16[512,1024]{1,0:T(8,128)(2,1)S(1)} %get-tuple-element.67.factor_ref, f32[128,1024]{1,0:T(8,128)S(1)} %get-tuple-element.68.part_ref, f32[128,1024]{1,0:T(8,128)S(1)} %copy-done.4, f32[1,1024]{1,0:T(1,128)S(1)} %get-tuple-element.70.inv_ref, ...), custom_call_target="tpu_custom_call" | custom-call | tf_op jit(solution)/shard_map/final/pallas_call | solution.py:307
  (18 shorter events, 0.0 us)
Async XLA Ops:
  0.0 15.8 %copy-start.2 = (bf16[64,32,128]{2,1,0:T(8,128)(2,1)S(1)}, bf16[64,32,128]{2,1,0:T(8,128)(2,1)}, u32[]{:S(2)}) copy-start(bf16[64,32,128]{2,1,0:T(8,128)(2,1)} %grad_ref.1) | copy-start | bytes 1572868
  3.5 12.3 %copy-start = (bf16[64,32,128]{2,1,0:T(8,128)(2,1)S(1)}, bf16[64,32,128]{2,1,0:T(8,128)(2,1)}, u32[]{:S(2)}) copy-start(bf16[64,32,128]{2,1,0:T(8,128)(2,1)} %act_ref.3) | copy-start | bytes 1572868
  3.5 12.3 %copy-start.1 = (bf16[128,512]{1,0:T(8,128)(2,1)S(1)}, bf16[128,512]{1,0:T(8,128)(2,1)}, u32[]{:S(2)}) copy-start(bf16[128,512]{1,0:T(8,128)(2,1)} %w_proj_ref.3) | copy-start | bytes 393220
  3.5 12.3 %copy-start.9 = (bf16[1024,128]{1,0:T(8,128)(2,1)S(1)}, bf16[1024,128]{1,0:T(8,128)(2,1)}, u32[]{:S(2)}) copy-start(bf16[1024,128]{1,0:T(8,128)(2,1)} %get-tuple-element.39.x_ref) | copy-start | bytes 786436
  3.5 12.3 %copy-start.10 = (bf16[128,128]{1,0:T(8,128)(2,1)S(1)}, bf16[128,128]{1,0:T(8,128)(2,1)}, u32[]{:S(2)}) copy-start(bf16[128,128]{1,0:T(8,128)(2,1)} %w_gate_ref.3) | copy-start | bytes 98308
  3.5 12.3 %copy-start.11 = (bf16[128,128]{1,0:T(8,128)(2,1)S(1)}, bf16[128,128]{1,0:T(8,128)(2,1)}, u32[]{:S(2)}) copy-start(bf16[128,128]{1,0:T(8,128)(2,1)} %w_out_ref.3) | copy-start | bytes 98308
  3.6 28.0 %all-to-all-start = ((bf16[64,32,128]{2,1,0:T(8,128)(2,1)}), bf16[64,32,128]{2,1,0:T(8,128)(2,1)S(1)}, u32[]{:S(2)}, u32[]{:S(2)}) async-start(bf16[64,32,128]{2,1,0:T(8,128)(2,1)} %bitcast.27), calls=%async_computation | async-start | bytes 1048576 | tf_op jit(solution)/shard_map/all_to_all | solution.py:326
  15.8 0.7 copy-start.12
  15.8 0.7 copy-start.13
  15.8 0.7 copy-start.14
  15.8 0.7 copy-start.15
  18.2 0.8 copy-start.3
  19.0 0.8 copy-start.5
  19.8 0.8 copy-start.7
  31.8 1.6 %collective-permute-start = (bf16[512,256]{1,0:T(8,128)(2,1)S(1)}, bf16[512,256]{1,0:T(8,128)(2,1)S(1)}, u32[]{:S(2)}, u32[]{:S(2)}) collective-permute-start(bf16[512,256]{1,0:T(8,128)(2,1)S(1)} %get-tuple-element.49.own_ref), channel_id=1, source_target_pairs={{0,16},{16,0},{1,17},{17,1},{2,18},{18,2},{3,19},{19,3},{4,20},{20... | collective-permute-start | bytes 786440 | tf_op jit(solution)/shard_map/ppermute | solution.py:330
  33.4 25.4 %copy-start.6 = (f32[1024,128]{1,0:T(8,128)S(1)}, f32[1024,128]{1,0:T(8,128)}, u32[]{:S(2)}) copy-start(f32[1024,128]{1,0:T(8,128)} %copy-done.5) | copy-start | bytes 1572868
  59.4 20.7 %copy-start.8 = (f32[1024,128]{1,0:T(8,128)S(1)}, f32[1024,128]{1,0:T(8,128)}, u32[]{:S(2)}) copy-start(f32[1024,128]{1,0:T(8,128)} %copy-done.7) | copy-start | bytes 1572868
  80.0 1.6 %collective-permute-start.1 = (bf16[512,256]{1,0:T(8,128)(2,1)S(1)}, bf16[512,256]{1,0:T(8,128)(2,1)S(1)}, u32[]{:S(2)}, u32[]{:S(2)}) collective-permute-start(bf16[512,256]{1,0:T(8,128)(2,1)S(1)} %get-tuple-element.56), channel_id=1, source_target_pairs={{0,16},{16,0},{1,17},{17,1},{2,18},{18,2},{3,19},{19,3},{4,20},{20... | collective-permute-start | bytes 786440 | tf_op jit(solution)/shard_map/ppermute | solution.py:330
  81.9 26.8 %copy-start.4 = (f32[128,1024]{1,0:T(8,128)S(1)}, f32[128,1024]{1,0:T(8,128)}, u32[]{:S(2)}) copy-start(f32[128,1024]{1,0:T(8,128)} %copy-done.3) | copy-start | bytes 1572868

commit v5 on v4

--- a/solution.py
+++ b/solution.py
@@ -27,14 +27,10 @@
     return lax.dot_general(a, b, (((ca,), (cb,)), ((), ())), preferred_element_type=F32)
 
 
-def place(k):
-    return ((k % LOW) * (HALF // LOW) + k // LOW) * ROWS
-
-
 def normalize(values):
-    average = jnp.mean(values, axis=-1, keepdims=True)
+    average = jnp.mean(values, axis=0, keepdims=True)
     centred = values - average
-    inv_std = lax.rsqrt(jnp.mean(centred * centred, axis=-1, keepdims=True) + 1e-05)
+    inv_std = lax.rsqrt(jnp.mean(centred * centred, axis=0, keepdims=True) + 1e-05)
     return centred * inv_std, inv_std
 
 
@@ -82,7 +78,7 @@
 
 
 def edges_kernel(
-    starts_ref, act_ref, mask_ref, gain_ref, bias_ref, w_ref, edges_ref, x_ref, keep_ref,
+    starts_ref, act_ref, mask_ref, gain_ref, bias_ref, w_ref, edges_ref, keep_ref,
     tile, kept, x_all, projected, turned,
 ):
     slab_at = lax.axis_index("slab")
@@ -99,11 +95,12 @@
     values = act_ref[...].astype(F32)
     spare = jnp.zeros((ROWS, PITCH - COLS, LANES), F32)
     tile[...] = jnp.concatenate([values, spare], axis=1).reshape(ROWS * PITCH, LANES)
-    for k in range(COLS):
-        normed, _ = normalize(column(tile, k, PITCH))
-        at = (k % HALF * 2 + k // HALF) * ROWS
-        x_all[pl.ds(at, ROWS), :] = (normed * gain_ref[...] + bias_ref[...]).astype(BF16)
-    projected[...] = dot(w_own, x_all[...], 0, 1)
+    gain, bias = (jnp.broadcast_to(ref[...], (LANES, LANES)).T for ref in (gain_ref, bias_ref))
+    for k in range(HALF):
+        values = jnp.concatenate([column(tile, k, PITCH), column(tile, k + HALF, PITCH)], axis=0)
+        normed, _ = normalize(values.T)
+        x_all[:, block(k)] = (normed * gain + bias).astype(BF16)
+    projected[...] = dot(w_own, x_all[...], 0, 0)
     for k in range(HALF):
         both = jax.nn.sigmoid(projected[0:128, block(k)]) * projected[128:256, block(k)]
         both = both * halves(kept[k : k + 1, :], kept[k + HALF : k + HALF + 1, :])
@@ -111,36 +108,33 @@
         turned[pl.ds(k + HALF, OWN, stride=PITCH), :] = both[OWN:CHANNELS, :]
     done = turned[...].reshape(OWN, PITCH, LANES)[:, 0:COLS, :]
     edges_ref[...] = done.reshape(OWN * COLS, LANES).astype(BF16)
-    for k in range(HALF):
-        mine = pl.multiple_of(2 * k * ROWS + slab_at * ROWS, ROWS)
-        x_ref[pl.ds(place(k), ROWS), :] = x_all[pl.ds(mine, ROWS), :]
 
 
 def ahead_kernel(
-    act_ref, grad_ref, x_ref, keep_ref, w_proj_ref, w_gate_ref, w_out_ref, gain_ref, bias_ref, in_gain_ref,
-    slope_ref, grad_hat_ref, factor_ref, normed_ref, inv_ref, tall_ref, tile, projected,
+    act_ref, grad_ref, keep_ref, w_proj_ref, w_gate_ref, w_out_ref, gain_ref, bias_ref, in_gain_ref, in_bias_ref,
+    slope_ref, grad_hat_ref, factor_ref, normed_ref, inv_ref, tall_ref, tile, x_in, projected,
 ):
     for at, ref in enumerate((in_gain_ref, gain_ref, bias_ref)):
         tall_ref[at] = jnp.broadcast_to(ref[...], (LANES, LANES)).T
     slab_at = lax.axis_index("slab")
+    in_bias = jnp.broadcast_to(in_bias_ref[...], (LANES, LANES)).T
+    load_half(act_ref, slab_at, tile)
+    for low in range(LOW):
+        normed, inv = normalize(two_columns(tile, low).T)
+        normed_ref[:, block(low)] = normed
+        inv_ref[:, block(low)] = inv
+        x_in[:, block(low)] = (normed * tall_ref[0] + in_bias).astype(BF16)
     load_half(grad_ref, slab_at, tile)
     gain = tall_ref[1]
     for low in range(LOW):
         here = pl.ds(low * LANES, LANES)
-        gate = jax.nn.sigmoid(dot(x_ref[here, :], w_gate_ref[...], 1, 0))
+        gate = jax.nn.sigmoid(dot(x_in[:, block(low)], w_gate_ref[...], 0, 0))
         grad_in = two_columns(tile, low)
         slope_ref[here, :] = grad_in * gate * (1.0 - gate)
         mid_in_grad = (grad_in * gate).astype(BF16)
         grad_hat = dot(w_out_ref[...], mid_in_grad, 1, 1) * gain
         grad_hat_ref[pl.ds(low, CHANNELS, stride=LOW), :] = grad_hat - jnp.mean(grad_hat, axis=0, keepdims=True)
-    load_half(act_ref, slab_at, tile)
-    for low in range(LOW):
-        values = two_columns(tile, low).T
-        centred = values - jnp.mean(values, axis=0, keepdims=True)
-        inv = lax.rsqrt(jnp.mean(centred * centred, axis=0, keepdims=True) + 1e-05)
-        normed_ref[:, block(low)] = centred * inv
-        inv_ref[:, block(low)] = inv
-    projected[...] = dot(w_proj_ref[...], x_ref[...], 0, 1)
+    projected[...] = dot(w_proj_ref[...], x_in[...], 0, 0)
     for low in range(LOW):
         keep = keep_ref[low : low + 1, :]
         for side in range(2):
@@ -172,24 +166,34 @@
             ref[:, block(m)] = both.reshape(512, LANES).astype(BF16)
 
 
-def triangle_kernel(left_ref, own_ref, other_ref, out_ref, right_ref):
-    core_at = lax.axis_index("core")
-    for m in range(LINES // 2):
-        own, other = own_ref[:, block(m)].astype(F32), other_ref[:, block(m)].astype(F32)
-        a = jnp.where(core_at == 0, own, other)
-        b = jnp.where(core_at == 0, other, own)
-        first, second = mix(a, b)
-        right_ref[:, block(2 * m)] = first.astype(BF16)
-        right_ref[:, block(2 * m + 1)] = second.astype(BF16)
+def pieces_of(left_ref, right_ref, put):
     for m in range(LINES // 2):
         tri = dot(right_ref[...], left_ref[:, block(m)], 0, 0)
-        tri = tri.reshape(32, HALF, LANES)
-        a = tri[:, 0:LOW, :].reshape(256, LANES)
-        b = tri[:, LOW:HALF, :].reshape(256, LANES)
+        tri = tri.reshape(16, HALF, LANES)
+        a = tri[:, 0:LOW, :].reshape(LANES, LANES)
+        b = tri[:, LOW:HALF, :].reshape(LANES, LANES)
         for x, part in zip((2 * m, 2 * m + 1), mix(a, b)):
-            part = part.reshape(LINES, LINES, HALF, LANES)
-            for z in range(LINES):
-                out_ref[pl.ds((z * 4 + x) * 64, 64), :] = part[:, z].reshape(64, LANES).astype(BF16)
+            part = part.reshape(LINES, 2, HALF, LANES)
+            for z in range(2):
+                put((z * 4 + x) * 64, part[:, z].reshape(64, LANES).astype(BF16))
+
+
+def own_kernel(left_ref, own_ref, out_ref):
+    def put(at, rows):
+        out_ref[pl.ds(at, 64), :] = rows
+
+    pieces_of(left_ref, own_ref, put)
+
+
+def other_kernel(left_ref, other_ref, part_ref, out_ref):
+    core_at = lax.axis_index("core")
+    out_ref[pl.ds(pl.multiple_of(core_at * 512, 512), 512), :] = part_ref[...]
+    start = (1 - core_at) * 512
+
+    def put(at, rows):
+        out_ref[pl.ds(pl.multiple_of(start + at, 64), 64), :] = rows
+
+    pieces_of(left_ref, other_ref, put)
 
 
 def middle_kernel(tri_ref, grad_hat_ref, out_ref, hats_ref):
@@ -208,9 +212,9 @@
 
 
 def late_kernel(
-    hats_ref, slope_ref, w_gate_ref, w_out_ref, tall_ref, right_ref, grid_t_ref, out_ref, left_grad_ref
+    hats_ref, slope_ref, w_gate_ref, w_out_ref, tall_ref, own_ref, other_ref, grid_t_ref, out_ref, left_grad_ref
 ):
-    left_grad_ref[...] = dot(right_ref[...], grid_t_ref[...], 1, 0)
+    left_grad_ref[...] = dot(own_ref[...], grid_t_ref[0], 1, 0) + dot(other_ref[...], grid_t_ref[1], 1, 0)
     gain, bias = tall_ref[1], tall_ref[2]
     for low in range(LOW):
         hat = hats_ref[pl.ds(low, CHANNELS, stride=LOW), :]
@@ -222,29 +226,28 @@
 
 def grads_kernel(tri_grad_ref, left_ref, own_ref, other_ref, grid_t):
     core_at = lax.axis_index("core")
-    for m in range(LINES // 2):
-        a, b = (
-            jnp.concatenate(
-                [
-                    tri_grad_ref[pl.ds((z * 16 + x * 4 + y) * HALF, HALF), :].astype(F32)
-                    for y in range(LINES)
-                    for z in range(LINES)
-                ],
-                axis=0,
+    for group, core in enumerate((core_at, 1 - core_at)):
+        for m in range(LINES // 2):
+            a, b = (
+                jnp.concatenate(
+                    [
+                        tri_grad_ref[
+                            pl.ds(pl.multiple_of(core * 512 + (z * 16 + x * 4 + y) * HALF, HALF), HALF), :
+                        ].astype(F32)
+                        for y in range(LINES)
+                        for z in range(2)
+                    ],
+                    axis=0,
+                )
+                for x in (2 * m, 2 * m + 1)
             )
-            for x in (2 * m, 2 * m + 1)
-        )
-        first, second = mix(a, b)
-        both = jnp.concatenate(
-            [first.reshape(32, LOW, LANES), second.reshape(32, LOW, LANES)], axis=1
-        )
-        grid_t[:, block(m)] = both.reshape(32 * HALF, LANES).astype(BF16)
-    for m in range(LINES // 2):
-        a = dot(left_ref[...], grid_t[pl.ds(2 * m * LANES, LANES), :], 1, 1)
-        b = dot(left_ref[...], grid_t[pl.ds((2 * m + 1) * LANES, LANES), :], 1, 1)
-        first, second = mix(a, b)
-        own_ref[:, block(m)] = jnp.where(core_at == 0, first, second)
-        other_ref[:, block(m)] = jnp.where(core_at == 0, second, first).astype(BF16)
+            first, second = mix(a, b)
+            both = jnp.concatenate(
+                [first.reshape(16, LOW, LANES), second.reshape(16, LOW, LANES)], axis=1
+            )
+            grid_t[group, :, block(m)] = both.reshape(256, LANES).astype(BF16)
+    own_ref[...] = dot(left_ref[...], grid_t[0], 1, 1)
+    other_ref[...] = dot(left_ref[...], grid_t[1], 1, 1).astype(BF16)
 
 
 def join_kernel(left_grad_ref, own_ref, other_ref, out_ref):
@@ -338,13 +341,13 @@
     )
     edge_rows = OWN * COLS
     tri_rows = CHANNELS * LOW
-    edges, x_in, keep = call(
+    edges, keep = call(
         edges_kernel,
-        [shape((edge_rows, LANES), BF16), shape((POINTS, LANES), BF16), shape((LOW, LANES), F32)],
+        [shape((edge_rows, LANES), BF16), shape((LOW, LANES), F32)],
         [
             pltpu.VMEM((ROWS * PITCH, LANES), F32),
             pltpu.VMEM((COLS, LANES), F32),
-            pltpu.VMEM((2 * POINTS, LANES), BF16),
+            pltpu.VMEM((LANES, 2 * POINTS), BF16),
             pltpu.VMEM((256, 2 * POINTS), F32),
             pltpu.VMEM((OWN * PITCH, LANES), F32),
         ],
@@ -364,8 +367,12 @@
             shape((1, POINTS), F32),
             shape((3, LANES, LANES), F32),
         ],
-        [pltpu.VMEM((POINTS, LANES), F32), pltpu.VMEM((512, POINTS), F32)],
-        (pair_act, out_grad, x_in, keep, w_proj, w_gate, w_out, mid_gain, mid_bias, in_gain),
+        [
+            pltpu.VMEM((POINTS, LANES), F32),
+            pltpu.VMEM((LANES, POINTS), BF16),
+            pltpu.VMEM((512, POINTS), F32),
+        ],
+        (pair_act, out_grad, keep, w_proj, w_gate, w_out, mid_gain, mid_bias, in_gain, in_bias),
         "ahead",
         cost=pl.CostEstimate(flops=300_000_000, bytes_accessed=6_000_000, transcendentals=700_000),
     )
@@ -375,12 +382,11 @@
     left, own = call(
         sort_kernel, [shape((512, 256), BF16), shape((512, 256), BF16)], [], (edges,), "sort"
     )
-    tri, right = call(
-        triangle_kernel,
-        [shape((tri_rows, LANES), BF16), shape((512, 512), BF16)],
-        [],
-        (left, own, swap(own)),
-        "triangle",
+    other = swap(own)
+    part = call(own_kernel, shape((tri_rows // 2, LANES), BF16), [], (left, own), "triangle_own")
+    other, part = lax.optimization_barrier((other, part))
+    tri = call(
+        other_kernel, shape((tri_rows, LANES), BF16), [], (left, other, part), "triangle_other"
     )
     tri = exchange(tri, FAR)
     tri_grad, hats = call(
@@ -391,26 +397,26 @@
         "middle",
     )
     tri_grad = exchange(tri_grad, FAR)
-    own, other, grid_t = call(
+    own_grad, other_grad, grid_t = call(
         grads_kernel,
-        [shape((512, 256), F32), shape((512, 256), BF16), shape((512, 256), BF16)],
+        [shape((512, 256), F32), shape((512, 256), BF16), shape((2, 256, 256), BF16)],
         [],
         (tri_grad, left),
         "grads",
     )
-    other, hats, grid_t = lax.optimization_barrier((other, hats, grid_t))
-    swapped = swap(other)
+    other_grad, hats, grid_t = lax.optimization_barrier((other_grad, hats, grid_t))
+    swapped = swap(other_grad)
     part, left_grad = call(
         late_kernel,
         [shape((LANES, POINTS), F32), shape((512, 256), F32)],
         [],
-        (hats, slope, w_gate, w_out, tall, right, grid_t),
+        (hats, slope, w_gate, w_out, tall, own, other, grid_t),
         "late",
         cost=pl.CostEstimate(flops=210_000_000, bytes_accessed=3_000_000, transcendentals=0),
     )
     swapped, part, left_grad = lax.optimization_barrier((swapped, part, left_grad))
     grads = call(
-        join_kernel, shape((CHANNELS * HALF, LANES), BF16), [], (left_grad, own, swapped), "join"
+        join_kernel, shape((CHANNELS * HALF, LANES), BF16), [], (left_grad, own_grad, swapped), "join"
     )
     grads = exchange(grads, FAR)
     result = call(

time: 111 us -> 110 us (level)
    unnamed x32 -> x24, local copies, waits for them, and re-layouts: 3.05 us -> 2.47 us
    pallas_call x9 -> x10, Pallas kernels: 10.8 us -> 10.5 us  [call(): pl.pallas_call(kernel, out_shape=outs, in_specs=[SMEM] * smem + [VMEM] *...]
where the time goes in v5:
time: 110 us; the launch traced here: 109 us
  blocking collectives  71.3 us (65%)
  waiting for transfers between devices  12.5 us (11%)
  starting transfers between devices  12.4 us (11%)
  Pallas kernels  10.5 us (10%)
  local copies, waits for them, and re-layouts  2.47 us (2%)
    all_to_all x3, blocking collectives, exchange(): return lax.all_to_all(cut, axes, 0, 0, tiled=True).reshape(flat.shape)  71.3 us
    all_to_all x1, starting transfers between devices, exchange(): return lax.all_to_all(cut, axes, 0, 0, tiled=True).reshape(flat.shape)  12.2 us
    all_to_all x1, waiting for transfers between devices, exchange(): return lax.all_to_all(cut, axes, 0, 0, tiled=True).reshape(flat.shape)  11.3 us
    pallas_call x10, Pallas kernels, call(): pl.pallas_call(kernel, out_shape=outs, in_specs=[SMEM] * smem + [VMEM] *...  10.5 us
    unnamed x24, local copies, waits for them, and re-layouts  2.47 us
  transfers between devices with their start and end apart: 3, of which 3 were waited for; matrix products, arithmetic and copies ran while one was open for 0% of the time, Pallas kernels for 3%

profile of v5, /device:TPU:2, one launch (start us, length us, event | category | flops | bytes accessed | tf_op | source)
XLA Modules:
  0.0 109.4 jit_solution(1319208648247968291)
XLA Ops:
  0.0 3.1 %edges.1 = (bf16[2048,128]{1,0:T(8,128)(2,1)}, f32[8,128]{1,0:T(8,128)}) custom-call(s32[6]{0:T(128)} %starts_ref.1, bf16[64,32,128]{2,1,0:T(8,128)(2,1)} %act_ref.3, s32[32,64]{1,0:T(8,128)} %bitcast.30, f32[1,128]{1,0:T(1,128)} %bitcast.23, f32[1,128]{1,0:T(1,128)} %bitcast.25, bf16[128,512]{1,0:T(8,128)(2,1)} %w_proj_ref.3), custom_call_target="tpu_custom_call" | custom-call | tf_op jit(solution)/shard_map/edges/pallas_call | solution.py:310
  3.1 0.0 copy-start.5
  3.1 0.0 copy-start.11
  3.1 12.2 %all-to-all-start = ((bf16[64,32,128]{2,1,0:T(8,128)(2,1)}), bf16[64,32,128]{2,1,0:T(8,128)(2,1)S(1)}, u32[]{:S(2)}, u32[]{:S(2)}) async-start(bf16[64,32,128]{2,1,0:T(8,128)(2,1)} %bitcast.29), calls=%async_computation | async-start | bytes 1048576 | tf_op jit(solution)/shard_map/all_to_all | solution.py:329
  15.4 0.0 copy-start.9
  15.4 0.0 copy-start.6
  15.4 0.0 copy-start.7
  15.4 0.0 copy-start.10
  15.4 0.0 copy-done
  15.4 0.0 copy-done.1
  15.5 0.6 copy-done.9
  16.1 0.0 copy-done.7
  16.1 0.0 copy-done.10
  16.1 1.0 copy-done.8
  17.1 1.9 %ahead.1 = (f32[1024,128]{1,0:T(8,128)S(1)}, f32[1024,128]{1,0:T(8,128)S(1)}, bf16[512,1024]{1,0:T(8,128)(2,1)S(1)}, f32[128,1024]{1,0:T(8,128)S(1)}, f32[1,1024]{1,0:T(1,128)S(1)}, /*index=5*/f32[3,128,128]{2,1,0:T(8,128)S(1)}) custom-call(bf16[64,32,128]{2,1,0:T(8,128)(2,1)S(1)} %copy-done, bf16[64,32,128]{2,1,0:T(8,128)(2,1)S(1)} %copy-done.8, ...), custom_call_target="tpu_custom_call" | custom-call | flops 300000000 | bytes 6000000 | tf_op jit(solution)/shard_map/ahead/pallas_call | solution.py:310
  19.1 0.8 copy-done.2
  19.9 11.3 %all-to-all-done = bf16[64,32,128]{2,1,0:T(8,128)(2,1)S(1)} async-done(((bf16[64,32,128]{2,1,0:T(8,128)(2,1)}), bf16[64,32,128]{2,1,0:T(8,128)(2,1)S(1)}, u32[]{:S(2)}, u32[]{:S(2)}) %all-to-all-start) | async-done | bytes 524320 | tf_op jit(solution)/shard_map/all_to_all | solution.py:329
  31.1 0.2 sort.1
  31.4 0.1 collective-permute-start
  31.5 0.4 triangle_own.1.part_ref
  31.9 1.1 %collective-permute-done.other_ref = bf16[512,256]{1,0:T(8,128)(2,1)S(1)} collective-permute-done((bf16[512,256]{1,0:T(8,128)(2,1)S(1)}, bf16[512,256]{1,0:T(8,128)(2,1)S(1)}, u32[]{:S(2)}, u32[]{:S(2)}) %collective-permute-start) | collective-permute-done | bytes 262176 | tf_op jit(solution)/shard_map/ppermute | solution.py:333
  33.0 0.4 triangle_other.1
  33.4 24.6 %all_to_all.20 = bf16[128,8,128]{2,1,0:T(8,128)(2,1)S(1)} all-to-all(bf16[128,8,128]{2,1,0:T(8,128)(2,1)S(1)} %bitcast.20), channel_id=1, replica_groups=mesh['slab'=2,'x'=4,'core'=2,'y'=4,'z'=4] {'z','x','y','slab'}, dimensions={0} | all-to-all | bytes 524288 | tf_op jit(solution)/shard_map/all_to_all | solution.py:329
  58.0 0.5 middle.1
  58.6 20.0 %all_to_all.21 = bf16[128,8,128]{2,1,0:T(8,128)(2,1)S(1)} all-to-all(bf16[128,8,128]{2,1,0:T(8,128)(2,1)S(1)} %bitcast.22), channel_id=1, replica_groups=mesh['slab'=2,'x'=4,'core'=2,'y'=4,'z'=4] {'z','x','y','slab'}, dimensions={0} | all-to-all | bytes 524288 | tf_op jit(solution)/shard_map/all_to_all | solution.py:329
  78.6 0.4 grads.1
  79.0 0.1 collective-permute-start.1
  79.1 1.4 %late.1 = (f32[128,1024]{1,0:T(8,128)S(1)}, f32[512,256]{1,0:T(8,128)S(1)}) custom-call(f32[1024,128]{1,0:T(8,128)S(1)} %get-tuple-element.56.hats_ref, f32[1024,128]{1,0:T(8,128)S(1)} %copy-done.3, bf16[128,128]{1,0:T(8,128)(2,1)S(1)} %copy-done.4, bf16[128,128]{1,0:T(8,128)(2,1)S(1)} %copy-done.5, f32[3,128,128]{2,1,0:T(8,128)S(1)} %get-tuple-element.58.tall_ref, ...), custom_call_target="tpu_custom_call" | custom-call | flops 210000000 | bytes 3000000 | tf_op jit(solution)/shard_map/late/pallas_call | solution.py:310
  80.5 0.1 collective-permute-done.1.other_ref
  80.6 0.2 join.1
  80.9 26.7 %all_to_all.22 = bf16[128,16,128]{2,1,0:T(8,128)(2,1)S(1)} all-to-all(bf16[128,16,128]{2,1,0:T(8,128)(2,1)S(1)} %bitcast.17), channel_id=1, replica_groups=mesh['slab'=2,'x'=4,'core'=2,'y'=4,'z'=4] {'z','x','y','slab'}, dimensions={0} | all-to-all | bytes 1048576 | tf_op jit(solution)/shard_map/all_to_all | solution.py:329
  107.6 1.8 %final.1 = bf16[64,16,128]{2,1,0:T(8,128)(2,1)} custom-call(bf16[2048,128]{1,0:T(8,128)(2,1)S(1)} %bitcast.16, bf16[512,1024]{1,0:T(8,128)(2,1)S(1)} %get-tuple-element.65.factor_ref, f32[128,1024]{1,0:T(8,128)S(1)} %get-tuple-element.66.part_ref, f32[128,1024]{1,0:T(8,128)S(1)} %get-tuple-element.67.normed_ref, f32[1,1024]{1,0:T(1,128)S(1)} %get-tuple-element.68.inv_ref, ...), custom_call_target="tpu_custom_call" | custom-call | tf_op jit(solution)/shard_map/final/pallas_call | solution.py:310
  (11 shorter events, 0.0 us)
Async XLA Ops:
  3.1 12.3 %copy-start = (bf16[64,32,128]{2,1,0:T(8,128)(2,1)S(1)}, bf16[64,32,128]{2,1,0:T(8,128)(2,1)}, u32[]{:S(2)}) copy-start(bf16[64,32,128]{2,1,0:T(8,128)(2,1)} %act_ref.3) | copy-start | bytes 1572868
  3.1 12.3 %copy-start.1 = (bf16[128,512]{1,0:T(8,128)(2,1)S(1)}, bf16[128,512]{1,0:T(8,128)(2,1)}, u32[]{:S(2)}) copy-start(bf16[128,512]{1,0:T(8,128)(2,1)} %w_proj_ref.3) | copy-start | bytes 393220
  3.1 12.3 %copy-start.4 = (bf16[128,128]{1,0:T(8,128)(2,1)S(1)}, bf16[128,128]{1,0:T(8,128)(2,1)}, u32[]{:S(2)}) copy-start(bf16[128,128]{1,0:T(8,128)(2,1)} %w_gate_ref.3) | copy-start | bytes 98308
  3.1 12.3 %copy-start.5 = (bf16[128,128]{1,0:T(8,128)(2,1)S(1)}, bf16[128,128]{1,0:T(8,128)(2,1)}, u32[]{:S(2)}) copy-start(bf16[128,128]{1,0:T(8,128)(2,1)} %w_out_ref.3) | copy-start | bytes 98308
  3.1 12.3 %copy-start.11 = (f32[128]{0:T(128)S(1)}, f32[128]{0:T(128)}, u32[]{:S(2)}) copy-start(f32[128]{0:T(128)} %param.21) | copy-start | bytes 1540
  3.1 28.0 %all-to-all-start = ((bf16[64,32,128]{2,1,0:T(8,128)(2,1)}), bf16[64,32,128]{2,1,0:T(8,128)(2,1)S(1)}, u32[]{:S(2)}, u32[]{:S(2)}) async-start(bf16[64,32,128]{2,1,0:T(8,128)(2,1)} %bitcast.29), calls=%async_computation | async-start | bytes 1048576 | tf_op jit(solution)/shard_map/all_to_all | solution.py:329
  15.4 0.7 copy-start.9
  15.4 0.7 copy-start.6
  15.4 0.7 copy-start.7
  15.4 0.7 copy-start.10
  16.1 1.0 copy-start.8
  19.1 0.8 copy-start.2
  31.4 1.6 %collective-permute-start = (bf16[512,256]{1,0:T(8,128)(2,1)S(1)}, bf16[512,256]{1,0:T(8,128)(2,1)S(1)}, u32[]{:S(2)}, u32[]{:S(2)}) collective-permute-start(bf16[512,256]{1,0:T(8,128)(2,1)S(1)} %get-tuple-element.47.own_ref), channel_id=1, source_target_pairs={{0,16},{16,0},{1,17},{17,1},{2,18},{18,2},{3,19},{19,3},{4,20},{20... | collective-permute-start | bytes 786440 | tf_op jit(solution)/shard_map/ppermute | solution.py:333
  58.6 20.5 %copy-start.3 = (f32[1024,128]{1,0:T(8,128)S(1)}, f32[1024,128]{1,0:T(8,128)}, u32[]{:S(2)}) copy-start(f32[1024,128]{1,0:T(8,128)} %copy-done.2) | copy-start | bytes 1572868
  79.0 1.6 %collective-permute-start.1 = (bf16[512,256]{1,0:T(8,128)(2,1)S(1)}, bf16[512,256]{1,0:T(8,128)(2,1)S(1)}, u32[]{:S(2)}, u32[]{:S(2)}) collective-permute-start(bf16[512,256]{1,0:T(8,128)(2,1)S(1)} %get-tuple-element.55), channel_id=1, source_target_pairs={{0,16},{16,0},{1,17},{17,1},{2,18},{18,2},{3,19},{19,3},{4,20},{20... | collective-permute-start | bytes 786440 | tf_op jit(solution)/shard_map/ppermute | solution.py:333

commit v6 on v5

--- a/solution.py
+++ b/solution.py
@@ -145,31 +145,34 @@
             factor_ref[at + 128 : at + 256, block(low)] = (keep * sig).astype(BF16)
 
 
-def sort_kernel(edges_ref, left_ref, right_ref):
+def sort(edges_ref, side, ref):
     for m in range(LINES // 2):
-        for side, ref in enumerate((left_ref, right_ref)):
-            a, b = (
-                jnp.concatenate(
-                    [
-                        edges_ref[pl.ds((z * 16 + x * 4 + y) * COLS + side * HALF, HALF), :].astype(F32)
-                        for z in range(LINES)
-                        for y in range(LINES)
-                    ],
-                    axis=0,
-                )
-                for x in (2 * m, 2 * m + 1)
+        a, b = (
+            jnp.concatenate(
+                [
+                    edges_ref[pl.ds((z * 16 + x * 4 + y) * COLS + side * HALF, HALF), :].astype(F32)
+                    for z in range(LINES)
+                    for y in range(LINES)
+                ],
+                axis=0,
             )
-            first, second = mix(a, b)
-            both = jnp.concatenate(
-                [first.reshape(16, HALF, LANES), second.reshape(16, HALF, LANES)], axis=1
-            )
-            ref[:, block(m)] = both.reshape(512, LANES).astype(BF16)
+            for x in (2 * m, 2 * m + 1)
+        )
+        first, second = mix(a, b)
+        both = jnp.concatenate(
+            [first.reshape(16, HALF, LANES), second.reshape(16, HALF, LANES)], axis=1
+        )
+        ref[:, block(m)] = both.reshape(512, LANES).astype(BF16)
+
+
+def sort_kernel(edges_ref, right_ref):
+    sort(edges_ref, 1, right_ref)
 
 
 def pieces_of(left_ref, right_ref, put):
+    both = dot(right_ref[...], left_ref[...], 0, 0)
     for m in range(LINES // 2):
-        tri = dot(right_ref[...], left_ref[:, block(m)], 0, 0)
-        tri = tri.reshape(16, HALF, LANES)
+        tri = both[:, block(m)].reshape(16, HALF, LANES)
         a = tri[:, 0:LOW, :].reshape(LANES, LANES)
         b = tri[:, LOW:HALF, :].reshape(LANES, LANES)
         for x, part in zip((2 * m, 2 * m + 1), mix(a, b)):
@@ -178,7 +181,9 @@
                 put((z * 4 + x) * 64, part[:, z].reshape(64, LANES).astype(BF16))
 
 
-def own_kernel(left_ref, own_ref, out_ref):
+def own_kernel(edges_ref, own_ref, left_ref, out_ref):
+    sort(edges_ref, 0, left_ref)
+
     def put(at, rows):
         out_ref[pl.ds(at, 64), :] = rows
 
@@ -216,12 +221,12 @@
 ):
     left_grad_ref[...] = dot(own_ref[...], grid_t_ref[0], 1, 0) + dot(other_ref[...], grid_t_ref[1], 1, 0)
     gain, bias = tall_ref[1], tall_ref[2]
-    for low in range(LOW):
-        hat = hats_ref[pl.ds(low, CHANNELS, stride=LOW), :]
-        mid_out = (hat * gain + bias).astype(BF16)
+    for low in range(0, LOW, 2):
+        hats = [hats_ref[pl.ds(low + at, CHANNELS, stride=LOW), :] for at in range(2)]
+        mid_out = jnp.concatenate([(hat * gain + bias).astype(BF16) for hat in hats], axis=1)
         proj_out = dot(mid_out, w_out_ref[...], 0, 0)
-        gate_grad = (slope_ref[pl.ds(low * LANES, LANES), :] * proj_out).astype(BF16)
-        out_ref[:, block(low)] = dot(w_gate_ref[...], gate_grad, 1, 1)
+        gate_grad = (slope_ref[pl.ds(low * LANES, 2 * LANES), :] * proj_out).astype(BF16)
+        out_ref[:, low * LANES : (low + 2) * LANES] = dot(w_gate_ref[...], gate_grad, 1, 1)
 
 
 def grads_kernel(tri_grad_ref, left_ref, own_ref, other_ref, grid_t):
@@ -290,7 +295,9 @@
                 proj_grad[at : at + 128, block(low)] = (grad * factor).astype(BF16)
     gain = tall_ref[0]
     for low in range(LOW):
-        x_grad = dot(w_proj_ref[...], proj_grad[:, block(low)], 1, 0) + part_ref[:, block(low)]
+        if low % 2 == 0:
+            pair = dot(w_proj_ref[...], proj_grad[:, low * LANES : (low + 2) * LANES], 1, 0)
+        x_grad = pair[:, block(low % 2)] + part_ref[:, block(low)]
         normed = normed_ref[:, block(low)]
         in_hat = x_grad * gain
         first = jnp.mean(in_hat, axis=0, keepdims=True)
@@ -379,12 +386,16 @@
     edges, slope, grad_hat, factor, normed, inv, tall = lax.optimization_barrier(
         (edges, slope, grad_hat, factor, normed, inv, tall)
     )
-    left, own = call(
-        sort_kernel, [shape((512, 256), BF16), shape((512, 256), BF16)], [], (edges,), "sort"
-    )
+    own = call(sort_kernel, shape((512, 256), BF16), [], (edges,), "sort")
     other = swap(own)
-    part = call(own_kernel, shape((tri_rows // 2, LANES), BF16), [], (left, own), "triangle_own")
-    other, part = lax.optimization_barrier((other, part))
+    left, part = call(
+        own_kernel,
+        [shape((512, 256), BF16), shape((tri_rows // 2, LANES), BF16)],
+        [],
+        (edges, own),
+        "triangle_own",
+    )
+    other, left, part = lax.optimization_barrier((other, left, part))
     tri = call(
         other_kernel, shape((tri_rows, LANES), BF16), [], (left, other, part), "triangle_other"
     )

time: 110 us -> 109 us (level)
  no operation moved by 1% of the time
where the time goes in v6:
time: 109 us
  blocking collectives  70.9 us (65%)
  waiting for transfers between devices  12.8 us (12%)
  starting transfers between devices  12.4 us (11%)
  Pallas kernels  9.82 us (9%)
  local copies, waits for them, and re-layouts  2.47 us (2%)
    all_to_all x3, blocking collectives, exchange(): return lax.all_to_all(cut, axes, 0, 0, tiled=True).reshape(flat.shape)  70.9 us
    all_to_all x1, starting transfers between devices, exchange(): return lax.all_to_all(cut, axes, 0, 0, tiled=True).reshape(flat.shape)  12.2 us
    all_to_all x1, waiting for transfers between devices, exchange(): return lax.all_to_all(cut, axes, 0, 0, tiled=True).reshape(flat.shape)  11.3 us
    pallas_call x10, Pallas kernels, call(): pl.pallas_call(kernel, out_shape=outs, in_specs=[SMEM] * smem + [VMEM] *...  9.82 us
    unnamed x24, local copies, waits for them, and re-layouts  2.47 us
  transfers between devices with their start and end apart: 3, of which 3 were waited for; matrix products, arithmetic and copies ran while one was open for 0% of the time, Pallas kernels for 3%

profile of v6, /device:TPU:2, one launch (start us, length us, event | category | flops | bytes accessed | tf_op | source)
XLA Modules:
  0.0 108.6 jit_solution(8104962758704428481)
XLA Ops:
  0.0 3.1 %edges.1 = (bf16[2048,128]{1,0:T(8,128)(2,1)}, f32[8,128]{1,0:T(8,128)}) custom-call(s32[6]{0:T(128)} %starts_ref.1, bf16[64,32,128]{2,1,0:T(8,128)(2,1)} %act_ref.3, s32[32,64]{1,0:T(8,128)} %bitcast.31, f32[1,128]{1,0:T(1,128)} %bitcast.24, f32[1,128]{1,0:T(1,128)} %bitcast.26, bf16[128,512]{1,0:T(8,128)(2,1)} %w_proj_ref.3), custom_call_target="tpu_custom_call" | custom-call | tf_op jit(solution)/shard_map/edges/pallas_call | solution.py:317
  3.1 0.0 copy-start.5
  3.1 0.0 copy-start.11
  3.1 12.2 %all-to-all-start = ((bf16[64,32,128]{2,1,0:T(8,128)(2,1)}), bf16[64,32,128]{2,1,0:T(8,128)(2,1)S(1)}, u32[]{:S(2)}, u32[]{:S(2)}) async-start(bf16[64,32,128]{2,1,0:T(8,128)(2,1)} %bitcast.30), calls=%async_computation | async-start | bytes 1048576 | tf_op jit(solution)/shard_map/all_to_all | solution.py:336
  15.4 0.0 copy-start.9
  15.4 0.0 copy-start.6
  15.4 0.0 copy-start.7
  15.4 0.0 copy-start.10
  15.5 0.6 copy-done.9
  16.1 0.0 copy-done.6
  16.1 0.0 copy-done.10
  16.1 1.0 copy-done.8
  17.1 1.9 %ahead.1 = (f32[1024,128]{1,0:T(8,128)S(1)}, f32[1024,128]{1,0:T(8,128)S(1)}, bf16[512,1024]{1,0:T(8,128)(2,1)S(1)}, f32[128,1024]{1,0:T(8,128)S(1)}, f32[1,1024]{1,0:T(1,128)S(1)}, /*index=5*/f32[3,128,128]{2,1,0:T(8,128)S(1)}) custom-call(bf16[64,32,128]{2,1,0:T(8,128)(2,1)S(1)} %copy-done, bf16[64,32,128]{2,1,0:T(8,128)(2,1)S(1)} %copy-done.8, ...), custom_call_target="tpu_custom_call" | custom-call | flops 300000000 | bytes 6000000 | tf_op jit(solution)/shard_map/ahead/pallas_call | solution.py:317
  19.1 0.0 copy-start.2
  19.1 0.8 copy-done.2
  19.9 11.3 %all-to-all-done = bf16[64,32,128]{2,1,0:T(8,128)(2,1)S(1)} async-done(((bf16[64,32,128]{2,1,0:T(8,128)(2,1)}), bf16[64,32,128]{2,1,0:T(8,128)(2,1)S(1)}, u32[]{:S(2)}, u32[]{:S(2)}) %all-to-all-start) | async-done | bytes 524320 | tf_op jit(solution)/shard_map/all_to_all | solution.py:336
  31.1 0.1 sort.1.own_ref
  31.3 0.1 collective-permute-start
  31.4 0.5 triangle_own.1
  31.9 1.1 collective-permute-done.other_ref
  32.9 0.3 triangle_other.1
  33.3 24.6 %all_to_all.20 = bf16[128,8,128]{2,1,0:T(8,128)(2,1)S(1)} all-to-all(bf16[128,8,128]{2,1,0:T(8,128)(2,1)S(1)} %bitcast.21), channel_id=1, replica_groups=mesh['slab'=2,'x'=4,'core'=2,'y'=4,'z'=4] {'z','x','y','slab'}, dimensions={0} | all-to-all | bytes 524288 | tf_op jit(solution)/shard_map/all_to_all | solution.py:336
  57.9 0.5 middle.1
  58.4 0.0 copy-start.3
  58.4 20.0 %all_to_all.21 = bf16[128,8,128]{2,1,0:T(8,128)(2,1)S(1)} all-to-all(bf16[128,8,128]{2,1,0:T(8,128)(2,1)S(1)} %bitcast.23), channel_id=1, replica_groups=mesh['slab'=2,'x'=4,'core'=2,'y'=4,'z'=4] {'z','x','y','slab'}, dimensions={0} | all-to-all | bytes 524288 | tf_op jit(solution)/shard_map/all_to_all | solution.py:336
  78.4 0.4 grads.1
  78.8 0.1 collective-permute-start.1
  79.0 1.0 late.1
  80.0 0.5 collective-permute-done.1.other_ref
  80.5 0.2 join.1
  80.7 26.3 %all_to_all.22 = bf16[128,16,128]{2,1,0:T(8,128)(2,1)S(1)} all-to-all(bf16[128,16,128]{2,1,0:T(8,128)(2,1)S(1)} %bitcast.19), channel_id=1, replica_groups=mesh['slab'=2,'x'=4,'core'=2,'y'=4,'z'=4] {'z','x','y','slab'}, dimensions={0} | all-to-all | bytes 1048576 | tf_op jit(solution)/shard_map/all_to_all | solution.py:336
  107.0 1.6 %final.1 = bf16[64,16,128]{2,1,0:T(8,128)(2,1)} custom-call(bf16[2048,128]{1,0:T(8,128)(2,1)S(1)} %bitcast.18, bf16[512,1024]{1,0:T(8,128)(2,1)S(1)} %get-tuple-element.67.factor_ref, f32[128,1024]{1,0:T(8,128)S(1)} %get-tuple-element.68.part_ref, f32[128,1024]{1,0:T(8,128)S(1)} %get-tuple-element.69.normed_ref, f32[1,1024]{1,0:T(1,128)S(1)} %get-tuple-element.70.inv_ref, ...), custom_call_target="tpu_custom_call" | custom-call | tf_op jit(solution)/shard_map/final/pallas_call | solution.py:317
  (11 shorter events, 0.0 us)
Async XLA Ops:
  3.1 12.3 %copy-start = (bf16[64,32,128]{2,1,0:T(8,128)(2,1)S(1)}, bf16[64,32,128]{2,1,0:T(8,128)(2,1)}, u32[]{:S(2)}) copy-start(bf16[64,32,128]{2,1,0:T(8,128)(2,1)} %act_ref.3) | copy-start | bytes 1572868
  3.1 12.3 %copy-start.1 = (bf16[128,512]{1,0:T(8,128)(2,1)S(1)}, bf16[128,512]{1,0:T(8,128)(2,1)}, u32[]{:S(2)}) copy-start(bf16[128,512]{1,0:T(8,128)(2,1)} %w_proj_ref.3) | copy-start | bytes 393220
  3.1 12.3 %copy-start.4 = (bf16[128,128]{1,0:T(8,128)(2,1)S(1)}, bf16[128,128]{1,0:T(8,128)(2,1)}, u32[]{:S(2)}) copy-start(bf16[128,128]{1,0:T(8,128)(2,1)} %w_gate_ref.3) | copy-start | bytes 98308
  3.1 12.3 %copy-start.5 = (bf16[128,128]{1,0:T(8,128)(2,1)S(1)}, bf16[128,128]{1,0:T(8,128)(2,1)}, u32[]{:S(2)}) copy-start(bf16[128,128]{1,0:T(8,128)(2,1)} %w_out_ref.3) | copy-start | bytes 98308
  3.1 12.3 %copy-start.11 = (f32[128]{0:T(128)S(1)}, f32[128]{0:T(128)}, u32[]{:S(2)}) copy-start(f32[128]{0:T(128)} %param.21) | copy-start | bytes 1540
  3.1 28.0 %all-to-all-start = ((bf16[64,32,128]{2,1,0:T(8,128)(2,1)}), bf16[64,32,128]{2,1,0:T(8,128)(2,1)S(1)}, u32[]{:S(2)}, u32[]{:S(2)}) async-start(bf16[64,32,128]{2,1,0:T(8,128)(2,1)} %bitcast.30), calls=%async_computation | async-start | bytes 1048576 | tf_op jit(solution)/shard_map/all_to_all | solution.py:336
  15.4 0.7 copy-start.9
  15.4 0.7 copy-start.6
  15.4 0.7 copy-start.7
  15.4 0.7 copy-start.10
  16.1 1.0 copy-start.8
  19.1 0.8 copy-start.2
  31.3 1.6 %collective-permute-start = (bf16[512,256]{1,0:T(8,128)(2,1)S(1)}, bf16[512,256]{1,0:T(8,128)(2,1)S(1)}, u32[]{:S(2)}, u32[]{:S(2)}) collective-permute-start(bf16[512,256]{1,0:T(8,128)(2,1)S(1)} %sort.1.own_ref), channel_id=1, source_target_pairs={{0,16},{16,0},{1,17},{17,1},{2,18},{18,2},{3,19},{19,3},{4,20},{20... | collective-permute-start | bytes 786440 | tf_op jit(solution)/shard_map/ppermute | solution.py:340
  58.4 20.5 %copy-start.3 = (f32[1024,128]{1,0:T(8,128)S(1)}, f32[1024,128]{1,0:T(8,128)}, u32[]{:S(2)}) copy-start(f32[1024,128]{1,0:T(8,128)} %copy-done.2) | copy-start | bytes 1572868
  78.8 1.6 %collective-permute-start.1 = (bf16[512,256]{1,0:T(8,128)(2,1)S(1)}, bf16[512,256]{1,0:T(8,128)(2,1)S(1)}, u32[]{:S(2)}, u32[]{:S(2)}) collective-permute-start(bf16[512,256]{1,0:T(8,128)(2,1)S(1)} %get-tuple-element.57), channel_id=1, source_target_pairs={{0,16},{16,0},{1,17},{17,1},{2,18},{18,2},{3,19},{19,3},{4,20},{20... | collective-permute-start | bytes 786440 | tf_op jit(solution)/shard_map/ppermute | solution.py:340

commit v7 on v6

--- a/solution.py
+++ b/solution.py
@@ -216,10 +216,19 @@
     out_ref[...] = both.astype(BF16).reshape(CHANNELS * LOW, LANES)
 
 
+def two_rows(grad):
+    grad = grad.reshape(32, HALF, LANES)
+    return mix(grad[:, 0:LOW, :].reshape(256, LANES), grad[:, LOW:HALF, :].reshape(256, LANES))
+
+
 def late_kernel(
-    hats_ref, slope_ref, w_gate_ref, w_out_ref, tall_ref, own_ref, other_ref, grid_t_ref, out_ref, left_grad_ref
+    hats_ref, slope_ref, w_gate_ref, w_out_ref, tall_ref, left_ref, own_ref, other_ref, grid_t_ref,
+    out_ref, left_grad_ref, right_grad_ref,
 ):
-    left_grad_ref[...] = dot(own_ref[...], grid_t_ref[0], 1, 0) + dot(other_ref[...], grid_t_ref[1], 1, 0)
+    right_grad_ref[...] = dot(left_ref[...], grid_t_ref[0], 1, 1)
+    left_grad = dot(own_ref[...], grid_t_ref[0], 1, 0) + dot(other_ref[...], grid_t_ref[1], 1, 0)
+    for m in range(LINES // 2):
+        left_grad_ref[2 * m], left_grad_ref[2 * m + 1] = two_rows(left_grad[:, block(m)])
     gain, bias = tall_ref[1], tall_ref[2]
     for low in range(0, LOW, 2):
         hats = [hats_ref[pl.ds(low + at, CHANNELS, stride=LOW), :] for at in range(2)]
@@ -229,7 +238,7 @@
         out_ref[:, low * LANES : (low + 2) * LANES] = dot(w_gate_ref[...], gate_grad, 1, 1)
 
 
-def grads_kernel(tri_grad_ref, left_ref, own_ref, other_ref, grid_t):
+def grads_kernel(tri_grad_ref, left_ref, other_ref, grid_t):
     core_at = lax.axis_index("core")
     for group, core in enumerate((core_at, 1 - core_at)):
         for m in range(LINES // 2):
@@ -251,22 +260,15 @@
                 [first.reshape(16, LOW, LANES), second.reshape(16, LOW, LANES)], axis=1
             )
             grid_t[group, :, block(m)] = both.reshape(256, LANES).astype(BF16)
-    own_ref[...] = dot(left_ref[...], grid_t[0], 1, 1)
     other_ref[...] = dot(left_ref[...], grid_t[1], 1, 1).astype(BF16)
 
 
 def join_kernel(left_grad_ref, own_ref, other_ref, out_ref):
     for m in range(LINES // 2):
-        left_grad = left_grad_ref[:, block(m)]
         right_grad = own_ref[:, block(m)] + other_ref[:, block(m)].astype(F32)
-        sides = []
-        for grad in (left_grad, right_grad):
-            grad = grad.reshape(32, HALF, LANES)
-            a = grad[:, 0:LOW, :].reshape(256, LANES)
-            b = grad[:, LOW:HALF, :].reshape(256, LANES)
-            sides.append([part.reshape(32, LOW, LANES) for part in mix(a, b)])
-        for at, x in enumerate((2 * m, 2 * m + 1)):
-            both = jnp.concatenate([sides[0][at], sides[1][at]], axis=1)
+        for x, part in zip((2 * m, 2 * m + 1), two_rows(right_grad)):
+            left_grad = left_grad_ref[x].reshape(32, LOW, LANES)
+            both = jnp.concatenate([left_grad, part.reshape(32, LOW, LANES)], axis=1)
             both = both.astype(BF16).reshape(512, LANES)
             for z in range(LINES):
                 out_ref[pl.ds((z * 4 + x) * LANES, LANES), :] = both[z * LANES : (z + 1) * LANES]
@@ -408,24 +410,24 @@
         "middle",
     )
     tri_grad = exchange(tri_grad, FAR)
-    own_grad, other_grad, grid_t = call(
+    other_grad, grid_t = call(
         grads_kernel,
-        [shape((512, 256), F32), shape((512, 256), BF16), shape((2, 256, 256), BF16)],
+        [shape((512, 256), BF16), shape((2, 256, 256), BF16)],
         [],
         (tri_grad, left),
         "grads",
     )
     other_grad, hats, grid_t = lax.optimization_barrier((other_grad, hats, grid_t))
     swapped = swap(other_grad)
-    part, left_grad = call(
+    part, left_grad, own_grad = call(
         late_kernel,
-        [shape((LANES, POINTS), F32), shape((512, 256), F32)],
+        [shape((LANES, POINTS), F32), shape((LINES, 256, LANES), F32), shape((512, 256), F32)],
         [],
-        (hats, slope, w_gate, w_out, tall, own, other, grid_t),
+        (hats, slope, w_gate, w_out, tall, left, own, other, grid_t),
         "late",
         cost=pl.CostEstimate(flops=210_000_000, bytes_accessed=3_000_000, transcendentals=0),
     )
-    swapped, part, left_grad = lax.optimization_barrier((swapped, part, left_grad))
+    swapped, part, left_grad, own_grad = lax.optimization_barrier((swapped, part, left_grad, own_grad))
     grads = call(
         join_kernel, shape((CHANNELS * HALF, LANES), BF16), [], (left_grad, own_grad, swapped), "join"
     )

time: 109 us -> 109 us (level)
  no operation moved by 1% of the time
where the time goes in v7:
time: 109 us; the launch traced here: 108 us
  blocking collectives  70.8 us (65%)
  waiting for transfers between devices  13 us (12%)
  starting transfers between devices  12.4 us (11%)
  Pallas kernels  9.45 us (9%)
  local copies, waits for them, and re-layouts  2.47 us (2%)
    all_to_all x3, blocking collectives, exchange(): return lax.all_to_all(cut, axes, 0, 0, tiled=True).reshape(flat.shape)  70.8 us
    all_to_all x1, starting transfers between devices, exchange(): return lax.all_to_all(cut, axes, 0, 0, tiled=True).reshape(flat.shape)  12.2 us
    all_to_all x1, waiting for transfers between devices, exchange(): return lax.all_to_all(cut, axes, 0, 0, tiled=True).reshape(flat.shape)  11.3 us
    pallas_call x10, Pallas kernels, call(): pl.pallas_call(kernel, out_shape=outs, in_specs=[SMEM] * smem + [VMEM] *...  9.45 us
    unnamed x24, local copies, waits for them, and re-layouts  2.47 us
  transfers between devices with their start and end apart: 3, of which 3 were waited for; matrix products, arithmetic and copies ran while one was open for 0% of the time, Pallas kernels for 3%

profile of v7, /device:TPU:2, one launch (start us, length us, event | category | flops | bytes accessed | tf_op | source)
XLA Modules:
  0.0 108.4 jit_solution(514412135385491684)
XLA Ops:
  0.0 3.1 %edges.1 = (bf16[2048,128]{1,0:T(8,128)(2,1)}, f32[8,128]{1,0:T(8,128)}) custom-call(s32[6]{0:T(128)} %starts_ref.1, bf16[64,32,128]{2,1,0:T(8,128)(2,1)} %act_ref.3, s32[32,64]{1,0:T(8,128)} %bitcast.31, f32[1,128]{1,0:T(1,128)} %bitcast.24, f32[1,128]{1,0:T(1,128)} %bitcast.26, bf16[128,512]{1,0:T(8,128)(2,1)} %w_proj_ref.3), custom_call_target="tpu_custom_call" | custom-call | tf_op jit(solution)/shard_map/edges/pallas_call | solution.py:319
  3.1 0.0 copy-start.5
  3.1 0.0 copy-start.11
  3.1 12.2 %all-to-all-start = ((bf16[64,32,128]{2,1,0:T(8,128)(2,1)}), bf16[64,32,128]{2,1,0:T(8,128)(2,1)S(1)}, u32[]{:S(2)}, u32[]{:S(2)}) async-start(bf16[64,32,128]{2,1,0:T(8,128)(2,1)} %bitcast.30), calls=%async_computation | async-start | bytes 1048576 | tf_op jit(solution)/shard_map/all_to_all | solution.py:338
  15.4 0.0 copy-start.9
  15.4 0.0 copy-start.6
  15.4 0.0 copy-start.7
  15.4 0.0 copy-start.10
  15.4 0.0 copy-done
  15.4 0.0 copy-done.1
  15.5 0.6 copy-done.9
  16.1 0.0 copy-done.7
  16.1 0.0 copy-done.10
  16.1 1.0 copy-done.8
  17.1 1.9 %ahead.1 = (f32[1024,128]{1,0:T(8,128)S(1)}, f32[1024,128]{1,0:T(8,128)S(1)}, bf16[512,1024]{1,0:T(8,128)(2,1)S(1)}, f32[128,1024]{1,0:T(8,128)S(1)}, f32[1,1024]{1,0:T(1,128)S(1)}, /*index=5*/f32[3,128,128]{2,1,0:T(8,128)S(1)}) custom-call(bf16[64,32,128]{2,1,0:T(8,128)(2,1)S(1)} %copy-done, bf16[64,32,128]{2,1,0:T(8,128)(2,1)S(1)} %copy-done.8, ...), custom_call_target="tpu_custom_call" | custom-call | flops 300000000 | bytes 6000000 | tf_op jit(solution)/shard_map/ahead/pallas_call | solution.py:319
  19.1 0.8 copy-done.2
  19.9 11.3 %all-to-all-done = bf16[64,32,128]{2,1,0:T(8,128)(2,1)S(1)} async-done(((bf16[64,32,128]{2,1,0:T(8,128)(2,1)}), bf16[64,32,128]{2,1,0:T(8,128)(2,1)S(1)}, u32[]{:S(2)}, u32[]{:S(2)}) %all-to-all-start) | async-done | bytes 524320 | tf_op jit(solution)/shard_map/all_to_all | solution.py:338
  31.1 0.1 sort.1.own_ref
  31.3 0.1 collective-permute-start
  31.4 0.5 triangle_own.1
  31.9 1.1 collective-permute-done.other_ref
  32.9 0.3 triangle_other.1
  33.3 24.6 %all_to_all.20 = bf16[128,8,128]{2,1,0:T(8,128)(2,1)S(1)} all-to-all(bf16[128,8,128]{2,1,0:T(8,128)(2,1)S(1)} %bitcast.21), channel_id=1, replica_groups=mesh['slab'=2,'x'=4,'core'=2,'y'=4,'z'=4] {'z','x','y','slab'}, dimensions={0} | all-to-all | bytes 524288 | tf_op jit(solution)/shard_map/all_to_all | solution.py:338
  57.9 0.5 middle.1
  58.4 20.0 %all_to_all.21 = bf16[128,8,128]{2,1,0:T(8,128)(2,1)S(1)} all-to-all(bf16[128,8,128]{2,1,0:T(8,128)(2,1)S(1)} %bitcast.23), channel_id=1, replica_groups=mesh['slab'=2,'x'=4,'core'=2,'y'=4,'z'=4] {'z','x','y','slab'}, dimensions={0} | all-to-all | bytes 524288 | tf_op jit(solution)/shard_map/all_to_all | solution.py:338
  78.4 0.4 grads.1
  78.8 0.1 collective-permute-start.1
  78.9 0.8 late.1
  79.7 0.7 collective-permute-done.1.other_ref
  80.4 0.1 join.1
  80.5 26.3 %all_to_all.22 = bf16[128,16,128]{2,1,0:T(8,128)(2,1)S(1)} all-to-all(bf16[128,16,128]{2,1,0:T(8,128)(2,1)S(1)} %bitcast.19), channel_id=1, replica_groups=mesh['slab'=2,'x'=4,'core'=2,'y'=4,'z'=4] {'z','x','y','slab'}, dimensions={0} | all-to-all | bytes 1048576 | tf_op jit(solution)/shard_map/all_to_all | solution.py:338
  106.8 1.6 %final.1 = bf16[64,16,128]{2,1,0:T(8,128)(2,1)} custom-call(bf16[2048,128]{1,0:T(8,128)(2,1)S(1)} %bitcast.18, bf16[512,1024]{1,0:T(8,128)(2,1)S(1)} %get-tuple-element.69.factor_ref, f32[128,1024]{1,0:T(8,128)S(1)} %get-tuple-element.70.part_ref, f32[128,1024]{1,0:T(8,128)S(1)} %get-tuple-element.71.normed_ref, f32[1,1024]{1,0:T(1,128)S(1)} %get-tuple-element.72.inv_ref, ...), custom_call_target="tpu_custom_call" | custom-call | tf_op jit(solution)/shard_map/final/pallas_call | solution.py:319
  (11 shorter events, 0.0 us)
Async XLA Ops:
  3.1 12.3 %copy-start = (bf16[64,32,128]{2,1,0:T(8,128)(2,1)S(1)}, bf16[64,32,128]{2,1,0:T(8,128)(2,1)}, u32[]{:S(2)}) copy-start(bf16[64,32,128]{2,1,0:T(8,128)(2,1)} %act_ref.3) | copy-start | bytes 1572868
  3.1 12.3 %copy-start.1 = (bf16[128,512]{1,0:T(8,128)(2,1)S(1)}, bf16[128,512]{1,0:T(8,128)(2,1)}, u32[]{:S(2)}) copy-start(bf16[128,512]{1,0:T(8,128)(2,1)} %w_proj_ref.3) | copy-start | bytes 393220
  3.1 12.3 %copy-start.4 = (bf16[128,128]{1,0:T(8,128)(2,1)S(1)}, bf16[128,128]{1,0:T(8,128)(2,1)}, u32[]{:S(2)}) copy-start(bf16[128,128]{1,0:T(8,128)(2,1)} %w_gate_ref.3) | copy-start | bytes 98308
  3.1 12.3 %copy-start.5 = (bf16[128,128]{1,0:T(8,128)(2,1)S(1)}, bf16[128,128]{1,0:T(8,128)(2,1)}, u32[]{:S(2)}) copy-start(bf16[128,128]{1,0:T(8,128)(2,1)} %w_out_ref.3) | copy-start | bytes 98308
  3.1 12.3 %copy-start.11 = (f32[128]{0:T(128)S(1)}, f32[128]{0:T(128)}, u32[]{:S(2)}) copy-start(f32[128]{0:T(128)} %param.21) | copy-start | bytes 1540
  3.1 28.0 %all-to-all-start = ((bf16[64,32,128]{2,1,0:T(8,128)(2,1)}), bf16[64,32,128]{2,1,0:T(8,128)(2,1)S(1)}, u32[]{:S(2)}, u32[]{:S(2)}) async-start(bf16[64,32,128]{2,1,0:T(8,128)(2,1)} %bitcast.30), calls=%async_computation | async-start | bytes 1048576 | tf_op jit(solution)/shard_map/all_to_all | solution.py:338
  15.4 0.7 copy-start.9
  15.4 0.7 copy-start.6
  15.4 0.7 copy-start.7
  15.4 0.7 copy-start.10
  16.1 1.0 copy-start.8
  19.1 0.8 copy-start.2
  31.3 1.6 %collective-permute-start = (bf16[512,256]{1,0:T(8,128)(2,1)S(1)}, bf16[512,256]{1,0:T(8,128)(2,1)S(1)}, u32[]{:S(2)}, u32[]{:S(2)}) collective-permute-start(bf16[512,256]{1,0:T(8,128)(2,1)S(1)} %sort.1.own_ref), channel_id=1, source_target_pairs={{0,16},{16,0},{1,17},{17,1},{2,18},{18,2},{3,19},{19,3},{4,20},{20... | collective-permute-start | bytes 786440 | tf_op jit(solution)/shard_map/ppermute | solution.py:342
  58.4 20.4 %copy-start.3 = (f32[1024,128]{1,0:T(8,128)S(1)}, f32[1024,128]{1,0:T(8,128)}, u32[]{:S(2)}) copy-start(f32[1024,128]{1,0:T(8,128)} %copy-done.2) | copy-start | bytes 1572868
  78.8 1.6 %collective-permute-start.1 = (bf16[512,256]{1,0:T(8,128)(2,1)S(1)}, bf16[512,256]{1,0:T(8,128)(2,1)S(1)}, u32[]{:S(2)}, u32[]{:S(2)}) collective-permute-start(bf16[512,256]{1,0:T(8,128)(2,1)S(1)} %get-tuple-element.58), channel_id=1, source_target_pairs={{0,16},{16,0},{1,17},{17,1},{2,18},{18,2},{3,19},{19,3},{4,20},{20... | collective-permute-start | bytes 786440 | tf_op jit(solution)/shard_map/ppermute | solution.py:342

commit v8 on v7

--- a/solution.py
+++ b/solution.py
@@ -100,7 +100,9 @@
         values = jnp.concatenate([column(tile, k, PITCH), column(tile, k + HALF, PITCH)], axis=0)
         normed, _ = normalize(values.T)
         x_all[:, block(k)] = (normed * gain + bias).astype(BF16)
-    projected[...] = dot(w_own, x_all[...], 0, 0)
+        if k % 4 == 3:
+            here = slice((k - 3) * LANES, (k + 1) * LANES)
+            projected[:, here] = dot(w_own, x_all[:, here], 0, 0)
     for k in range(HALF):
         both = jax.nn.sigmoid(projected[0:128, block(k)]) * projected[128:256, block(k)]
         both = both * halves(kept[k : k + 1, :], kept[k + HALF : k + HALF + 1, :])
@@ -283,7 +285,8 @@
     for slab in range(2):
         part = jnp.concatenate([got[:, slab], spare], axis=1)
         grads[pl.ds(slab * OWN * STEP, OWN * STEP), :] = part.reshape(OWN * STEP, LANES)
-    for low in range(LOW):
+
+    def fill(low):
         for side in range(2):
             grad = jnp.concatenate(
                 [
@@ -295,18 +298,21 @@
             for at in (side * 256, side * 256 + 128):
                 factor = factor_ref[at : at + 128, block(low)].astype(F32)
                 proj_grad[at : at + 128, block(low)] = (grad * factor).astype(BF16)
+
     gain = tall_ref[0]
-    for low in range(LOW):
-        if low % 2 == 0:
-            pair = dot(w_proj_ref[...], proj_grad[:, low * LANES : (low + 2) * LANES], 1, 0)
-        x_grad = pair[:, block(low % 2)] + part_ref[:, block(low)]
-        normed = normed_ref[:, block(low)]
-        in_hat = x_grad * gain
-        first = jnp.mean(in_hat, axis=0, keepdims=True)
-        second = jnp.mean(in_hat * normed, axis=0, keepdims=True)
-        done = ((in_hat - first - normed * second) * inv_ref[:, block(low)]).T
-        result[pl.ds(low, ROWS, stride=STEP), :] = done[0:ROWS, :]
-        result[pl.ds(low + LOW, ROWS, stride=STEP), :] = done[ROWS:LANES, :]
+    for low in range(0, LOW, 2):
+        fill(low)
+        fill(low + 1)
+        pair = dot(w_proj_ref[...], proj_grad[:, low * LANES : (low + 2) * LANES], 1, 0)
+        for at in range(2):
+            x_grad = pair[:, block(at)] + part_ref[:, block(low + at)]
+            normed = normed_ref[:, block(low + at)]
+            in_hat = x_grad * gain
+            first = jnp.mean(in_hat, axis=0, keepdims=True)
+            second = jnp.mean(in_hat * normed, axis=0, keepdims=True)
+            done = ((in_hat - first - normed * second) * inv_ref[:, block(low + at)]).T
+            result[pl.ds(low + at, ROWS, stride=STEP), :] = done[0:ROWS, :]
+            result[pl.ds(low + at + LOW, ROWS, stride=STEP), :] = done[ROWS:LANES, :]
     out_ref[...] = result[...].reshape(ROWS, STEP, LANES)[:, 0:HALF, :].astype(BF16)
 
 

time: 109 us -> 109 us (level)
  no operation moved by 1% of the time
where the time goes in v8:
time: 109 us; the launch traced here: 108 us
  blocking collectives  70.8 us (65%)
  waiting for transfers between devices  13 us (12%)
  starting transfers between devices  12.4 us (11%)
  Pallas kernels  9.45 us (9%)
  local copies, waits for them, and re-layouts  2.47 us (2%)
    all_to_all x3, blocking collectives, exchange(): return lax.all_to_all(cut, axes, 0, 0, tiled=True).reshape(flat.shape)  70.8 us
    all_to_all x1, starting transfers between devices, exchange(): return lax.all_to_all(cut, axes, 0, 0, tiled=True).reshape(flat.shape)  12.2 us
    all_to_all x1, waiting for transfers between devices, exchange(): return lax.all_to_all(cut, axes, 0, 0, tiled=True).reshape(flat.shape)  11.3 us
    pallas_call x10, Pallas kernels, call(): pl.pallas_call(kernel, out_shape=outs, in_specs=[SMEM] * smem + [VMEM] *...  9.45 us
    unnamed x24, local copies, waits for them, and re-layouts  2.47 us
  transfers between devices with their start and end apart: 3, of which 3 were waited for; matrix products, arithmetic and copies ran while one was open for 0% of the time, Pallas kernels for 3%

profile of v8, /device:TPU:2, one launch (start us, length us, event | category | flops | bytes accessed | tf_op | source)
XLA Modules:
  0.0 108.4 jit_solution(514412135385491684)
XLA Ops:
  0.0 3.1 %edges.1 = (bf16[2048,128]{1,0:T(8,128)(2,1)}, f32[8,128]{1,0:T(8,128)}) custom-call(s32[6]{0:T(128)} %starts_ref.1, bf16[64,32,128]{2,1,0:T(8,128)(2,1)} %act_ref.3, s32[32,64]{1,0:T(8,128)} %bitcast.31, f32[1,128]{1,0:T(1,128)} %bitcast.24, f32[1,128]{1,0:T(1,128)} %bitcast.26, bf16[128,512]{1,0:T(8,128)(2,1)} %w_proj_ref.3), custom_call_target="tpu_custom_call" | custom-call | tf_op jit(solution)/shard_map/edges/pallas_call | solution.py:325
  3.1 0.0 copy-start.5
  3.1 0.0 copy-start.11
  3.1 12.2 %all-to-all-start = ((bf16[64,32,128]{2,1,0:T(8,128)(2,1)}), bf16[64,32,128]{2,1,0:T(8,128)(2,1)S(1)}, u32[]{:S(2)}, u32[]{:S(2)}) async-start(bf16[64,32,128]{2,1,0:T(8,128)(2,1)} %bitcast.30), calls=%async_computation | async-start | bytes 1048576 | tf_op jit(solution)/shard_map/all_to_all | solution.py:344
  15.4 0.0 copy-start.9
  15.4 0.0 copy-start.6
  15.4 0.0 copy-start.7
  15.4 0.0 copy-start.10
  15.4 0.0 copy-done
  15.4 0.0 copy-done.1
  15.5 0.6 copy-done.9
  16.1 0.0 copy-done.7
  16.1 0.0 copy-done.10
  16.1 1.0 copy-done.8
  17.1 1.9 %ahead.1 = (f32[1024,128]{1,0:T(8,128)S(1)}, f32[1024,128]{1,0:T(8,128)S(1)}, bf16[512,1024]{1,0:T(8,128)(2,1)S(1)}, f32[128,1024]{1,0:T(8,128)S(1)}, f32[1,1024]{1,0:T(1,128)S(1)}, /*index=5*/f32[3,128,128]{2,1,0:T(8,128)S(1)}) custom-call(bf16[64,32,128]{2,1,0:T(8,128)(2,1)S(1)} %copy-done, bf16[64,32,128]{2,1,0:T(8,128)(2,1)S(1)} %copy-done.8, ...), custom_call_target="tpu_custom_call" | custom-call | flops 300000000 | bytes 6000000 | tf_op jit(solution)/shard_map/ahead/pallas_call | solution.py:325
  19.1 0.8 copy-done.2
  19.9 11.3 %all-to-all-done = bf16[64,32,128]{2,1,0:T(8,128)(2,1)S(1)} async-done(((bf16[64,32,128]{2,1,0:T(8,128)(2,1)}), bf16[64,32,128]{2,1,0:T(8,128)(2,1)S(1)}, u32[]{:S(2)}, u32[]{:S(2)}) %all-to-all-start) | async-done | bytes 524320 | tf_op jit(solution)/shard_map/all_to_all | solution.py:344
  31.1 0.1 sort.1.own_ref
  31.3 0.1 collective-permute-start
  31.4 0.5 triangle_own.1
  31.9 1.1 collective-permute-done.other_ref
  32.9 0.3 triangle_other.1
  33.3 24.6 %all_to_all.20 = bf16[128,8,128]{2,1,0:T(8,128)(2,1)S(1)} all-to-all(bf16[128,8,128]{2,1,0:T(8,128)(2,1)S(1)} %bitcast.21), channel_id=1, replica_groups=mesh['slab'=2,'x'=4,'core'=2,'y'=4,'z'=4] {'z','x','y','slab'}, dimensions={0} | all-to-all | bytes 524288 | tf_op jit(solution)/shard_map/all_to_all | solution.py:344
  57.9 0.5 middle.1
  58.4 20.0 %all_to_all.21 = bf16[128,8,128]{2,1,0:T(8,128)(2,1)S(1)} all-to-all(bf16[128,8,128]{2,1,0:T(8,128)(2,1)S(1)} %bitcast.23), channel_id=1, replica_groups=mesh['slab'=2,'x'=4,'core'=2,'y'=4,'z'=4] {'z','x','y','slab'}, dimensions={0} | all-to-all | bytes 524288 | tf_op jit(solution)/shard_map/all_to_all | solution.py:344
  78.4 0.4 grads.1
  78.8 0.1 collective-permute-start.1
  78.9 0.8 late.1
  79.7 0.7 collective-permute-done.1.other_ref
  80.4 0.1 join.1
  80.5 26.3 %all_to_all.22 = bf16[128,16,128]{2,1,0:T(8,128)(2,1)S(1)} all-to-all(bf16[128,16,128]{2,1,0:T(8,128)(2,1)S(1)} %bitcast.19), channel_id=1, replica_groups=mesh['slab'=2,'x'=4,'core'=2,'y'=4,'z'=4] {'z','x','y','slab'}, dimensions={0} | all-to-all | bytes 1048576 | tf_op jit(solution)/shard_map/all_to_all | solution.py:344
  106.8 1.6 %final.1 = bf16[64,16,128]{2,1,0:T(8,128)(2,1)} custom-call(bf16[2048,128]{1,0:T(8,128)(2,1)S(1)} %bitcast.18, bf16[512,1024]{1,0:T(8,128)(2,1)S(1)} %get-tuple-element.69.factor_ref, f32[128,1024]{1,0:T(8,128)S(1)} %get-tuple-element.70.part_ref, f32[128,1024]{1,0:T(8,128)S(1)} %get-tuple-element.71.normed_ref, f32[1,1024]{1,0:T(1,128)S(1)} %get-tuple-element.72.inv_ref, ...), custom_call_target="tpu_custom_call" | custom-call | tf_op jit(solution)/shard_map/final/pallas_call | solution.py:325
  (11 shorter events, 0.0 us)
Async XLA Ops:
  3.1 12.3 %copy-start = (bf16[64,32,128]{2,1,0:T(8,128)(2,1)S(1)}, bf16[64,32,128]{2,1,0:T(8,128)(2,1)}, u32[]{:S(2)}) copy-start(bf16[64,32,128]{2,1,0:T(8,128)(2,1)} %act_ref.3) | copy-start | bytes 1572868
  3.1 12.3 %copy-start.1 = (bf16[128,512]{1,0:T(8,128)(2,1)S(1)}, bf16[128,512]{1,0:T(8,128)(2,1)}, u32[]{:S(2)}) copy-start(bf16[128,512]{1,0:T(8,128)(2,1)} %w_proj_ref.3) | copy-start | bytes 393220
  3.1 12.3 %copy-start.4 = (bf16[128,128]{1,0:T(8,128)(2,1)S(1)}, bf16[128,128]{1,0:T(8,128)(2,1)}, u32[]{:S(2)}) copy-start(bf16[128,128]{1,0:T(8,128)(2,1)} %w_gate_ref.3) | copy-start | bytes 98308
  3.1 12.3 %copy-start.5 = (bf16[128,128]{1,0:T(8,128)(2,1)S(1)}, bf16[128,128]{1,0:T(8,128)(2,1)}, u32[]{:S(2)}) copy-start(bf16[128,128]{1,0:T(8,128)(2,1)} %w_out_ref.3) | copy-start | bytes 98308
  3.1 12.3 %copy-start.11 = (f32[128]{0:T(128)S(1)}, f32[128]{0:T(128)}, u32[]{:S(2)}) copy-start(f32[128]{0:T(128)} %param.21) | copy-start | bytes 1540
  3.1 28.0 %all-to-all-start = ((bf16[64,32,128]{2,1,0:T(8,128)(2,1)}), bf16[64,32,128]{2,1,0:T(8,128)(2,1)S(1)}, u32[]{:S(2)}, u32[]{:S(2)}) async-start(bf16[64,32,128]{2,1,0:T(8,128)(2,1)} %bitcast.30), calls=%async_computation | async-start | bytes 1048576 | tf_op jit(solution)/shard_map/all_to_all | solution.py:344
  15.4 0.7 copy-start.9
  15.4 0.7 copy-start.6
  15.4 0.7 copy-start.7
  15.4 0.7 copy-start.10
  16.1 1.0 copy-start.8
  19.1 0.8 copy-start.2
  31.3 1.6 %collective-permute-start = (bf16[512,256]{1,0:T(8,128)(2,1)S(1)}, bf16[512,256]{1,0:T(8,128)(2,1)S(1)}, u32[]{:S(2)}, u32[]{:S(2)}) collective-permute-start(bf16[512,256]{1,0:T(8,128)(2,1)S(1)} %sort.1.own_ref), channel_id=1, source_target_pairs={{0,16},{16,0},{1,17},{17,1},{2,18},{18,2},{3,19},{19,3},{4,20},{20... | collective-permute-start | bytes 786440 | tf_op jit(solution)/shard_map/ppermute | solution.py:348
  58.4 20.4 %copy-start.3 = (f32[1024,128]{1,0:T(8,128)S(1)}, f32[1024,128]{1,0:T(8,128)}, u32[]{:S(2)}) copy-start(f32[1024,128]{1,0:T(8,128)} %copy-done.2) | copy-start | bytes 1572868
  78.8 1.6 %collective-permute-start.1 = (bf16[512,256]{1,0:T(8,128)(2,1)S(1)}, bf16[512,256]{1,0:T(8,128)(2,1)S(1)}, u32[]{:S(2)}, u32[]{:S(2)}) collective-permute-start(bf16[512,256]{1,0:T(8,128)(2,1)S(1)} %get-tuple-element.58), channel_id=1, source_target_pairs={{0,16},{16,0},{1,17},{17,1},{2,18},{18,2},{3,19},{19,3},{4,20},{20... | collective-permute-start | bytes 786440 | tf_op jit(solution)/shard_map/ppermute | solution.py:348

commit v9 on v8

--- a/solution.py
+++ b/solution.py
@@ -203,14 +203,13 @@
     pieces_of(left_ref, other_ref, put)
 
 
-def middle_kernel(tri_ref, grad_hat_ref, out_ref, hats_ref):
+def tri_norm(tri_ref):
     parts = tri_ref[...].astype(F32).reshape(OWN, 2 * LOW, LANES)
-    tri = jnp.concatenate([parts[:, 0:LOW, :], parts[:, LOW : 2 * LOW, :]], axis=0)
-    average = jnp.mean(tri, axis=0, keepdims=True)
-    centred = tri - average
-    inv = lax.rsqrt(jnp.mean(centred * centred, axis=0, keepdims=True) + 1e-05)
-    hat = centred * inv
-    hats_ref[...] = hat.reshape(CHANNELS * LOW, LANES)
+    return normalize(jnp.concatenate([parts[:, 0:LOW, :], parts[:, LOW : 2 * LOW, :]], axis=0))
+
+
+def middle_kernel(tri_ref, grad_hat_ref, out_ref):
+    hat, inv = tri_norm(tri_ref)
     grad_hat = grad_hat_ref[...].reshape(CHANNELS, LOW, LANES)
     second = jnp.mean(grad_hat * hat, axis=0, keepdims=True)
     done = (grad_hat - hat * second) * inv
@@ -224,9 +223,10 @@
 
 
 def late_kernel(
-    hats_ref, slope_ref, w_gate_ref, w_out_ref, tall_ref, left_ref, own_ref, other_ref, grid_t_ref,
-    out_ref, left_grad_ref, right_grad_ref,
+    tri_ref, slope_ref, w_gate_ref, w_out_ref, tall_ref, left_ref, own_ref, other_ref, grid_t_ref,
+    out_ref, left_grad_ref, right_grad_ref, hats_ref,
 ):
+    hats_ref[...] = tri_norm(tri_ref)[0].reshape(CHANNELS * LOW, LANES)
     right_grad_ref[...] = dot(left_ref[...], grid_t_ref[0], 1, 1)
     left_grad = dot(own_ref[...], grid_t_ref[0], 1, 0) + dot(other_ref[...], grid_t_ref[1], 1, 0)
     for m in range(LINES // 2):
@@ -408,9 +408,9 @@
         other_kernel, shape((tri_rows, LANES), BF16), [], (left, other, part), "triangle_other"
     )
     tri = exchange(tri, FAR)
-    tri_grad, hats = call(
+    tri_grad = call(
         middle_kernel,
-        [shape((tri_rows, LANES), BF16), shape((tri_rows, LANES), F32)],
+        shape((tri_rows, LANES), BF16),
         [],
         (tri, grad_hat),
         "middle",
@@ -423,13 +423,13 @@
         (tri_grad, left),
         "grads",
     )
-    other_grad, hats, grid_t = lax.optimization_barrier((other_grad, hats, grid_t))
+    other_grad, tri, grid_t = lax.optimization_barrier((other_grad, tri, grid_t))
     swapped = swap(other_grad)
     part, left_grad, own_grad = call(
         late_kernel,
         [shape((LANES, POINTS), F32), shape((LINES, 256, LANES), F32), shape((512, 256), F32)],
-        [],
-        (hats, slope, w_gate, w_out, tall, left, own, other, grid_t),
+        [pltpu.VMEM((tri_rows, LANES), F32)],
+        (tri, slope, w_gate, w_out, tall, left, own, other, grid_t),
         "late",
         cost=pl.CostEstimate(flops=210_000_000, bytes_accessed=3_000_000, transcendentals=0),
     )

time: 109 us -> 109 us (level)
  no operation moved by 1% of the time
where the time goes in v9:
time: 109 us; the launch traced here: 108 us
  blocking collectives  70.9 us (65%)
  waiting for transfers between devices  12.8 us (12%)
  starting transfers between devices  12.4 us (11%)
  Pallas kernels  9.64 us (9%)
  local copies, waits for them, and re-layouts  2.48 us (2%)
    all_to_all x3, blocking collectives, exchange(): return lax.all_to_all(cut, axes, 0, 0, tiled=True).reshape(flat.shape)  70.9 us
    all_to_all x1, starting transfers between devices, exchange(): return lax.all_to_all(cut, axes, 0, 0, tiled=True).reshape(flat.shape)  12.2 us
    all_to_all x1, waiting for transfers between devices, exchange(): return lax.all_to_all(cut, axes, 0, 0, tiled=True).reshape(flat.shape)  11.3 us
    pallas_call x10, Pallas kernels, call(): pl.pallas_call(kernel, out_shape=outs, in_specs=[SMEM] * smem + [VMEM] *...  9.64 us
    unnamed x24, local copies, waits for them, and re-layouts  2.48 us
  transfers between devices with their start and end apart: 3, of which 3 were waited for; matrix products, arithmetic and copies ran while one was open for 0% of the time, Pallas kernels for 3%

profile of v9, /device:TPU:2, one launch (start us, length us, event | category | flops | bytes accessed | tf_op | source)
XLA Modules:
  0.0 108.4 jit_solution(5968777865315135585)
XLA Ops:
  0.0 3.1 %edges.1 = (bf16[2048,128]{1,0:T(8,128)(2,1)}, f32[8,128]{1,0:T(8,128)}) custom-call(s32[6]{0:T(128)} %starts_ref.1, bf16[64,32,128]{2,1,0:T(8,128)(2,1)} %act_ref.3, s32[32,64]{1,0:T(8,128)} %bitcast.32, f32[1,128]{1,0:T(1,128)} %bitcast.25, f32[1,128]{1,0:T(1,128)} %bitcast.27, bf16[128,512]{1,0:T(8,128)(2,1)} %w_proj_ref.3), custom_call_target="tpu_custom_call" | custom-call | tf_op jit(solution)/shard_map/edges/pallas_call | solution.py:325
  3.1 0.0 copy-start.5
  3.1 0.0 copy-start.11
  3.1 12.2 %all-to-all-start = ((bf16[64,32,128]{2,1,0:T(8,128)(2,1)}), bf16[64,32,128]{2,1,0:T(8,128)(2,1)S(1)}, u32[]{:S(2)}, u32[]{:S(2)}) async-start(bf16[64,32,128]{2,1,0:T(8,128)(2,1)} %bitcast.31), calls=%async_computation | async-start | bytes 1048576 | tf_op jit(solution)/shard_map/all_to_all | solution.py:344
  15.4 0.0 copy-start.9
  15.4 0.0 copy-start.6
  15.4 0.0 copy-start.7
  15.4 0.0 copy-start.10
  15.4 0.0 copy-done
  15.4 0.0 copy-done.1
  15.4 0.0 copy-done.4
  15.5 0.6 copy-done.9
  16.1 0.0 copy-done.10
  16.1 1.0 copy-done.8
  17.1 1.9 %ahead.1 = (f32[1024,128]{1,0:T(8,128)S(1)}, f32[1024,128]{1,0:T(8,128)S(1)}, bf16[512,1024]{1,0:T(8,128)(2,1)S(1)}, f32[128,1024]{1,0:T(8,128)S(1)}, f32[1,1024]{1,0:T(1,128)S(1)}, /*index=5*/f32[3,128,128]{2,1,0:T(8,128)S(1)}) custom-call(bf16[64,32,128]{2,1,0:T(8,128)(2,1)S(1)} %copy-done, bf16[64,32,128]{2,1,0:T(8,128)(2,1)S(1)} %copy-done.8, ...), custom_call_target="tpu_custom_call" | custom-call | flops 300000000 | bytes 6000000 | tf_op jit(solution)/shard_map/ahead/pallas_call | solution.py:325
  19.1 0.8 copy-done.2
  19.9 11.3 %all-to-all-done = bf16[64,32,128]{2,1,0:T(8,128)(2,1)S(1)} async-done(((bf16[64,32,128]{2,1,0:T(8,128)(2,1)}), bf16[64,32,128]{2,1,0:T(8,128)(2,1)S(1)}, u32[]{:S(2)}, u32[]{:S(2)}) %all-to-all-start) | async-done | bytes 524320 | tf_op jit(solution)/shard_map/all_to_all | solution.py:344
  31.1 0.1 sort.1.own_ref
  31.3 0.1 collective-permute-start
  31.4 0.5 triangle_own.1
  31.8 1.1 collective-permute-done.other_ref
  32.9 0.3 triangle_other.1
  33.3 24.6 %all_to_all.20 = bf16[128,8,128]{2,1,0:T(8,128)(2,1)S(1)} all-to-all(bf16[128,8,128]{2,1,0:T(8,128)(2,1)S(1)} %bitcast.22), channel_id=1, replica_groups=mesh['slab'=2,'x'=4,'core'=2,'y'=4,'z'=4] {'z','x','y','slab'}, dimensions={0} | all-to-all | bytes 524288 | tf_op jit(solution)/shard_map/all_to_all | solution.py:344
  57.9 0.5 middle.1
  58.4 20.0 %all_to_all.21 = bf16[128,8,128]{2,1,0:T(8,128)(2,1)S(1)} all-to-all(bf16[128,8,128]{2,1,0:T(8,128)(2,1)S(1)} %bitcast.24), channel_id=1, replica_groups=mesh['slab'=2,'x'=4,'core'=2,'y'=4,'z'=4] {'z','x','y','slab'}, dimensions={0} | all-to-all | bytes 524288 | tf_op jit(solution)/shard_map/all_to_all | solution.py:344
  78.3 0.4 grads.1
  78.7 0.1 collective-permute-start.1
  78.8 1.1 late.1
  79.9 0.4 collective-permute-done.1.other_ref
  80.3 0.1 join.1
  80.5 26.3 %all_to_all.22 = bf16[128,16,128]{2,1,0:T(8,128)(2,1)S(1)} all-to-all(bf16[128,16,128]{2,1,0:T(8,128)(2,1)S(1)} %bitcast.21), channel_id=1, replica_groups=mesh['slab'=2,'x'=4,'core'=2,'y'=4,'z'=4] {'z','x','y','slab'}, dimensions={0} | all-to-all | bytes 1048576 | tf_op jit(solution)/shard_map/all_to_all | solution.py:344
  106.7 1.6 %final.1 = bf16[64,16,128]{2,1,0:T(8,128)(2,1)} custom-call(bf16[2048,128]{1,0:T(8,128)(2,1)S(1)} %bitcast.20, bf16[512,1024]{1,0:T(8,128)(2,1)S(1)} %get-tuple-element.65.factor_ref, f32[128,1024]{1,0:T(8,128)S(1)} %get-tuple-element.66.part_ref, f32[128,1024]{1,0:T(8,128)S(1)} %get-tuple-element.67.normed_ref, f32[1,1024]{1,0:T(1,128)S(1)} %get-tuple-element.68.inv_ref, ...), custom_call_target="tpu_custom_call" | custom-call | tf_op jit(solution)/shard_map/final/pallas_call | solution.py:325
  (11 shorter events, 0.0 us)
Async XLA Ops:
  3.1 12.3 %copy-start = (bf16[64,32,128]{2,1,0:T(8,128)(2,1)S(1)}, bf16[64,32,128]{2,1,0:T(8,128)(2,1)}, u32[]{:S(2)}) copy-start(bf16[64,32,128]{2,1,0:T(8,128)(2,1)} %act_ref.3) | copy-start | bytes 1572868
  3.1 12.3 %copy-start.1 = (bf16[128,512]{1,0:T(8,128)(2,1)S(1)}, bf16[128,512]{1,0:T(8,128)(2,1)}, u32[]{:S(2)}) copy-start(bf16[128,512]{1,0:T(8,128)(2,1)} %w_proj_ref.3) | copy-start | bytes 393220
  3.1 12.3 %copy-start.4 = (bf16[128,128]{1,0:T(8,128)(2,1)S(1)}, bf16[128,128]{1,0:T(8,128)(2,1)}, u32[]{:S(2)}) copy-start(bf16[128,128]{1,0:T(8,128)(2,1)} %w_gate_ref.3) | copy-start | bytes 98308
  3.1 12.3 %copy-start.5 = (bf16[128,128]{1,0:T(8,128)(2,1)S(1)}, bf16[128,128]{1,0:T(8,128)(2,1)}, u32[]{:S(2)}) copy-start(bf16[128,128]{1,0:T(8,128)(2,1)} %w_out_ref.3) | copy-start | bytes 98308
  3.1 12.3 %copy-start.11 = (f32[128]{0:T(128)S(1)}, f32[128]{0:T(128)}, u32[]{:S(2)}) copy-start(f32[128]{0:T(128)} %param.21) | copy-start | bytes 1540
  3.1 28.0 %all-to-all-start = ((bf16[64,32,128]{2,1,0:T(8,128)(2,1)}), bf16[64,32,128]{2,1,0:T(8,128)(2,1)S(1)}, u32[]{:S(2)}, u32[]{:S(2)}) async-start(bf16[64,32,128]{2,1,0:T(8,128)(2,1)} %bitcast.31), calls=%async_computation | async-start | bytes 1048576 | tf_op jit(solution)/shard_map/all_to_all | solution.py:344
  15.4 0.7 copy-start.9
  15.4 0.7 copy-start.6
  15.4 0.7 copy-start.7
  15.4 0.7 copy-start.10
  16.1 1.0 copy-start.8
  19.1 0.8 copy-start.2
  31.3 1.6 %collective-permute-start = (bf16[512,256]{1,0:T(8,128)(2,1)S(1)}, bf16[512,256]{1,0:T(8,128)(2,1)S(1)}, u32[]{:S(2)}, u32[]{:S(2)}) collective-permute-start(bf16[512,256]{1,0:T(8,128)(2,1)S(1)} %sort.1.own_ref), channel_id=1, source_target_pairs={{0,16},{16,0},{1,17},{17,1},{2,18},{18,2},{3,19},{19,3},{4,20},{20... | collective-permute-start | bytes 786440 | tf_op jit(solution)/shard_map/ppermute | solution.py:348
  58.4 20.4 %copy-start.3 = (f32[1024,128]{1,0:T(8,128)S(1)}, f32[1024,128]{1,0:T(8,128)}, u32[]{:S(2)}) copy-start(f32[1024,128]{1,0:T(8,128)} %copy-done.2) | copy-start | bytes 1572868
  78.7 1.6 %collective-permute-start.1 = (bf16[512,256]{1,0:T(8,128)(2,1)S(1)}, bf16[512,256]{1,0:T(8,128)(2,1)S(1)}, u32[]{:S(2)}, u32[]{:S(2)}) collective-permute-start(bf16[512,256]{1,0:T(8,128)(2,1)S(1)} %get-tuple-element.54), channel_id=1, source_target_pairs={{0,16},{16,0},{1,17},{17,1},{2,18},{18,2},{3,19},{19,3},{4,20},{20... | collective-permute-start | bytes 786440 | tf_op jit(solution)/shard_map/ppermute | solution.py:348
